TPU v7x, 256 devices: a whole 4x4x8 slice. The times are simulated.
256 devices in a mesh: lat: 16 (over x_hi, y, core), lon: 16 (over z, x_lo).
Axes of the slice: x: 4 (x_hi: 2, x_lo: 2; x = x_hi * 2 + x_lo), y: 4, z: 8, core: 2. Of those that a mesh axis runs over, the one named last changes fastest.
Arguments:
- tokens: bfloat16 [8, 96, 192, 192], P(None, 'lat', 'lon'), may hold values from -6 to 6
- grad_out: bfloat16 [8, 96, 192, 192], P(None, 'lat', 'lon'), may hold values from -6 to 6
- gain_one: float32 [192], replicated, may hold values from 0.5 to 1.5
- qkv_one: bfloat16 [192, 576], replicated, may hold values from -0.4375 to 0.4375
- proj_one: bfloat16 [192, 192], replicated, may hold values from -0.4375 to 0.4375
- bias_one: float32 [16, 79488], P('lat'), may hold values from -4 to 300
- gain_two: float32 [192], replicated, may hold values from 0.5 to 1.5
- qkv_two: bfloat16 [192, 576], replicated, may hold values from -0.4375 to 0.4375
- proj_two: bfloat16 [192, 192], replicated, may hold values from -0.4375 to 0.4375
- bias_two: float32 [16, 79488], P('lat'), may hold values from -4 to 300
Outputs:
- grad_tokens: bfloat16 [8, 96, 192, 192], P(None, 'lat', 'lon')
- grad_bias_one: float32 [16, 79488], P('lat', 'lon')
- grad_bias_two: float32 [16, 79488], P('lat', 'lon')
All inputs are finite; a program needn't handle non-finite values.
Results may differ from a plain program's by a relative error of at most 0.029.
Values may be sent and summed in bfloat16 or wider, within the bound.
No kernel may reach another device: no remote copies, remote signals or barrier semaphores. Data moves between devices by JAX's collectives and lax.ppermute only.
A program may use at most 192 MiB of HBM per device.

v0:
```python
import jax
import jax.numpy as jnp
from jax import lax
from jax.sharding import PartitionSpec as P

D = 192
HEADS = 6
HEAD_DIM = 32
WIN_LEV = 2
WIN_LAT = 6
WIN_LON = 12
WIN_TOK = 144
LEV = 8


def from_behind(value, axis, by):
    count = lax.axis_size(axis)
    return lax.ppermute(value, axis, [(i, (i + by) % count) for i in range(count)])


def to_windows(grid, lat_win, lon_win):
    width = grid.shape[-1]
    parts = grid.reshape(LEV // WIN_LEV, WIN_LEV, lat_win, WIN_LAT, lon_win, WIN_LON, width)
    parts = parts.transpose(0, 2, 4, 1, 3, 5, 6)
    return parts.reshape(-1, WIN_TOK, width)


def from_windows(windows, lat_win, lon_win):
    width = windows.shape[-1]
    parts = windows.reshape(LEV // WIN_LEV, lat_win, lon_win, WIN_LEV, WIN_LAT, WIN_LON, width)
    parts = parts.transpose(0, 3, 1, 4, 2, 5, 6)
    return parts.reshape(LEV, lat_win * WIN_LAT, lon_win * WIN_LON, width)


def group_mask():
    lat_index = jnp.arange(WIN_TOK, dtype=jnp.int32) // WIN_LON % WIN_LAT
    upper = lat_index >= WIN_LAT // 2
    return jnp.where(upper[:, None] != upper[None, :], jnp.float32(-10000.0), jnp.float32(0.0))


def offset_table():
    offsets = 2 * WIN_LON - 1
    slot = lax.broadcasted_iota(jnp.int32, (offsets, WIN_LON, WIN_LON), 0)
    query_lon = lax.broadcasted_iota(jnp.int32, (offsets, WIN_LON, WIN_LON), 1)
    key_lon = lax.broadcasted_iota(jnp.int32, (offsets, WIN_LON, WIN_LON), 2)
    return jnp.where(
        query_lon - key_lon + (WIN_LON - 1) == slot, jnp.float32(1.0), jnp.float32(0.0)
    )


def expand_rows(bias_rows):
    lat_win = bias_rows.shape[0]
    lev_win = LEV // WIN_LEV
    table = bias_rows.reshape(
        lat_win, lev_win, HEADS, WIN_LEV, WIN_LAT, WIN_LEV, WIN_LAT, 2 * WIN_LON - 1
    )
    full = jnp.einsum(
        "rvhpaqbj,jxy->rvhpaxqby", table, offset_table(), precision=lax.Precision.HIGHEST
    )
    return full.reshape(lat_win, lev_win, HEADS, WIN_TOK, WIN_TOK)


def spread_bias(bias_rows, lon_win):
    expanded = expand_rows(bias_rows)
    lat_win = expanded.shape[0]
    lev_win = LEV // WIN_LEV
    bias_local = expanded.transpose(1, 0, 2, 3, 4)
    full_shape = (lev_win, lat_win, lon_win, HEADS, WIN_TOK, WIN_TOK)
    return bias_local[:, :, None].reshape(-1, HEADS, WIN_TOK, WIN_TOK)


def window_forward(windows, bias_win, mask_add, gain_vec, w_qkv, w_proj):
    num_win = windows.shape[0]
    scaling = HEAD_DIM ** (-0.5)
    inputs_f = windows.astype(jnp.float32)
    centred = inputs_f - jnp.mean(inputs_f, -1, keepdims=True)
    inv_std = lax.rsqrt(jnp.mean(centred * centred, -1, keepdims=True) + 1e-05)
    normed = centred * inv_std
    hidden = (normed * gain_vec).astype(jnp.bfloat16)
    packed = jnp.dot(hidden, w_qkv, preferred_element_type=jnp.float32).astype(jnp.bfloat16)
    packed = packed.reshape(num_win, WIN_TOK, 3, HEADS, HEAD_DIM)
    q_rows, k_rows, v_rows = (packed[:, :, 0], packed[:, :, 1], packed[:, :, 2])
    scores = (
        jnp.einsum("nqhc,nkhc->nhqk", q_rows, k_rows, preferred_element_type=jnp.float32) * scaling
        + bias_win
    )
    if mask_add is not None:
        scores = scores + mask_add[:, None]
    row_max = jnp.max(scores, -1, keepdims=True)
    exp_scores = jnp.exp(scores - row_max)
    attn_probs = exp_scores / jnp.sum(exp_scores, -1, keepdims=True)
    probs_low = attn_probs.astype(jnp.bfloat16)
    attended = jnp.einsum(
        "nhqk,nkhc->nqhc", probs_low, v_rows, preferred_element_type=jnp.float32
    ).astype(jnp.bfloat16)
    attended = attended.reshape(num_win, WIN_TOK, D)
    block_out = (inputs_f + jnp.dot(attended, w_proj, preferred_element_type=jnp.float32)).astype(
        jnp.bfloat16
    )
    return (block_out, (normed, inv_std, q_rows, k_rows, v_rows, attn_probs, probs_low))


def window_backward(saved, grad_win, gain_vec, w_qkv, w_proj):
    normed, inv_std, q_rows, k_rows, v_rows, attn_probs, probs_low = saved
    num_win = grad_win.shape[0]
    scaling = HEAD_DIM ** (-0.5)
    grad_mixed = jnp.dot(grad_win, w_proj.T, preferred_element_type=jnp.float32).astype(
        jnp.bfloat16
    )
    grad_mixed = grad_mixed.reshape(num_win, WIN_TOK, HEADS, HEAD_DIM)
    grad_probs = jnp.einsum(
        "nqhc,nkhc->nhqk", grad_mixed, v_rows, preferred_element_type=jnp.float32
    )
    grad_v = jnp.einsum(
        "nhqk,nqhc->nkhc", probs_low, grad_mixed, preferred_element_type=jnp.float32
    ).astype(jnp.bfloat16)
    grad_scores = attn_probs * (grad_probs - jnp.sum(grad_probs * attn_probs, -1, keepdims=True))
    scaled_low = (grad_scores * scaling).astype(jnp.bfloat16)
    grad_q = jnp.einsum(
        "nhqk,nkhc->nqhc", scaled_low, k_rows, preferred_element_type=jnp.float32
    ).astype(jnp.bfloat16)
    grad_k = jnp.einsum(
        "nhqk,nqhc->nkhc", scaled_low, q_rows, preferred_element_type=jnp.float32
    ).astype(jnp.bfloat16)
    grad_packed = jnp.stack([grad_q, grad_k, grad_v], 2).reshape(num_win, WIN_TOK, 3 * D)
    grad_hidden = jnp.dot(grad_packed, w_qkv.T, preferred_element_type=jnp.float32)
    grad_normed = grad_hidden * gain_vec
    grad_local = inv_std * (
        grad_normed
        - jnp.mean(grad_normed, -1, keepdims=True)
        - normed * jnp.mean(grad_normed * normed, -1, keepdims=True)
    )
    input_grad = (grad_win.astype(jnp.float32) + grad_local).astype(jnp.bfloat16)
    return (input_grad, grad_scores)


def fold_terms(grad_scores, lat_win, lon_win):
    lev_win = LEV // WIN_LEV
    summed = grad_scores.reshape(lev_win, lat_win, lon_win, HEADS, WIN_TOK, WIN_TOK).sum(2)
    summed = summed.transpose(1, 0, 2, 3, 4)
    pairs = summed.reshape(
        lat_win, lev_win, HEADS, WIN_LEV, WIN_LAT, WIN_LON, WIN_LEV, WIN_LAT, WIN_LON
    )
    folded = jnp.einsum(
        "rvhpaxqby,jxy->rvhpaqbj", pairs, offset_table(), precision=lax.Precision.HIGHEST
    )
    return folded.reshape(lat_win, -1)


def relay_forward(paired):
    half_lat = WIN_LAT // 2
    half_lon = WIN_LON // 2
    fetched = from_behind(paired[:, :, :, :half_lon], "lon", -1)
    paired = jnp.concatenate([paired[:, :, :, half_lon:], fetched], 3)
    fetched = from_behind(paired[:, :, :half_lat], "lat", -1)
    paired = jnp.concatenate([paired[:, :, half_lat:], fetched], 2)
    return paired


def relay_back(gradient):
    half_lat = WIN_LAT // 2
    half_lon = WIN_LON // 2
    returned = from_behind(gradient[:, -half_lat:], "lat", 1)
    gradient = jnp.concatenate([returned, gradient[:, :-half_lat]], 1)
    returned = from_behind(gradient[:, :, -half_lon:], "lon", 1)
    gradient = jnp.concatenate([returned, gradient[:, :, :-half_lon]], 2)
    return gradient


def body(
    tokens, grad_out, gain_one, qkv_one, proj_one, bias_one, gain_two, qkv_two, proj_two, bias_two
):
    lat_win = tokens.shape[1] // WIN_LAT
    lon_win = tokens.shape[2] // WIN_LON
    first_windows = to_windows(tokens, lat_win, lon_win)
    first_out, first_saved = window_forward(
        first_windows, spread_bias(bias_one, lon_win), None, gain_one, qkv_one, proj_one
    )
    paired = jnp.stack([from_windows(first_out, lat_win, lon_win), grad_out])
    paired = relay_forward(paired)
    last_band = lax.axis_index("lat") == lax.axis_size("lat") - 1
    band_index = jnp.arange(first_windows.shape[0], dtype=jnp.int32) // lon_win % lat_win
    active = jnp.where(last_band & (band_index == lat_win - 1), jnp.float32(1.0), jnp.float32(0.0))
    mask_add = active[:, None, None] * group_mask()[None]
    second_out, second_saved = window_forward(
        to_windows(paired[0], lat_win, lon_win),
        spread_bias(bias_two, lon_win),
        mask_add,
        gain_two,
        qkv_two,
        proj_two,
    )
    grad_second, scores_two = window_backward(
        second_saved, to_windows(paired[1], lat_win, lon_win), gain_two, qkv_two, proj_two
    )
    term_two = fold_terms(scores_two, lat_win, lon_win)
    grad_first = relay_back(from_windows(grad_second, lat_win, lon_win))
    grad_windows, scores_one = window_backward(
        first_saved, to_windows(grad_first, lat_win, lon_win), gain_one, qkv_one, proj_one
    )
    term_one = fold_terms(scores_one, lat_win, lon_win)
    summed_one, summed_two = (
        lax.psum_scatter(
            term_one.astype(jnp.bfloat16), "lon", scatter_dimension=1, tiled=True
        ).astype(jnp.float32),
        lax.psum_scatter(
            term_two.astype(jnp.bfloat16), "lon", scatter_dimension=1, tiled=True
        ).astype(jnp.float32),
    )
    return (from_windows(grad_windows, lat_win, lon_win), summed_one, summed_two)


def solution(mesh):
    in_specs = (
        P(None, "lat", "lon", None),
        P(None, "lat", "lon", None),
        P(),
        P(),
        P(),
        P("lat", None),
        P(),
        P(),
        P(),
        P("lat", None),
    )
    out_specs = (P(None, "lat", "lon", None), P("lat", "lon"), P("lat", "lon"))
    return jax.shard_map(body, mesh=mesh, in_specs=in_specs, out_specs=out_specs, check_vma=False)
```

profile of v0, /device:TPU:2, one launch (start us, length us, event | category | flops | bytes accessed | tf_op | source)
XLA Modules:
  0.0 669.8 jit_solution(1435162745641189887)
XLA Ops:
  7.3 1.2 convert_reduce_fusion
  8.5 1.1 copy.156
  9.8 1.2 multiply_reduce_fusion.5
  11.5 0.8 copy.238
  12.3 0.5 convolution_convert_fusion.1
  12.8 1.4 copy.162
  14.3 0.8 reduce.4
  15.0 1.2 reshape.257
  16.2 25.6 %convolution_bitcast_fusion.1 = f32[1,4,6,2,6,12,2,6,12]{8,7,6,4,3,2,1,5,0:T(8,128)} fusion(f32[4,6,2,6,2,6,23,1]{6,5,4,3,2,1,0,7:T(8,128)S(1)} %reshape.257), kind=kOutput, calls=%fused_computation.5 | convolution fusion | flops 137368512 | bytes 2308608 | tf_op jit(solution)/shard_map/rvhpaqbj,jxy->rvhpaxqby/dot_general | solution.py:57
  41.8 39.2 %copy.213 = f32[1,4,6,2,6,12,2,6,12]{5,4,3,8,7,6,2,1,0:T(8,128)} copy(f32[1,4,6,2,6,12,2,6,12]{8,7,6,4,3,2,1,5,0:T(8,128)} %convolution_bitcast_fusion.1) | data formatting | bytes 3981312 | tf_op jit(solution)/shard_map/reshape;broadcast_in_dim;transpose;reshape | solution.py:69
  81.0 19.9 %reshape.265 = f32[4,6,144,144]{2,3,1,0:T(8,128)} reshape(f32[1,4,6,2,6,12,2,6,12]{5,4,3,8,7,6,2,1,0:T(8,128)} %copy.213) | data formatting | bytes 3981312 | tf_op jit(solution)/shard_map/reshape;broadcast_in_dim;transpose;reshape | solution.py:69
  100.9 2.7 multiply_add_fusion
  103.6 2.8 fusion.99
  106.4 4.1 convolution_convert_fusion.7
  110.5 0.3 fusion.15
  110.9 1.1 pad_maximum_fusion.5
  112.0 2.3 collective-permute-start
  114.3 0.7 reduce.5
  115.0 1.2 reshape.260
  116.2 25.6 %convolution_bitcast_fusion = f32[1,4,6,2,6,12,2,6,12]{8,7,6,4,3,2,1,5,0:T(8,128)} fusion(f32[4,6,2,6,2,6,23,1]{6,5,4,3,2,1,0,7:T(8,128)S(1)} %reshape.260), kind=kOutput, calls=%fused_computation.4 | convolution fusion | flops 137368512 | bytes 2308608 | tf_op jit(solution)/shard_map/rvhpaqbj,jxy->rvhpaxqby/dot_general | solution.py:57
  141.8 39.2 %copy.214 = f32[1,4,6,2,6,12,2,6,12]{5,4,3,8,7,6,2,1,0:T(8,128)} copy(f32[1,4,6,2,6,12,2,6,12]{8,7,6,4,3,2,1,5,0:T(8,128)} %convolution_bitcast_fusion) | data formatting | bytes 3981312 | tf_op jit(solution)/shard_map/reshape;broadcast_in_dim;transpose;reshape | solution.py:69
  181.0 19.6 %reshape.267 = f32[4,6,144,144]{2,3,1,0:T(8,128)} reshape(f32[1,4,6,2,6,12,2,6,12]{5,4,3,8,7,6,2,1,0:T(8,128)} %copy.214) | data formatting | bytes 3981312 | tf_op jit(solution)/shard_map/reshape;broadcast_in_dim;transpose;reshape | solution.py:69
  200.6 0.6 dynamic-slice
  201.9 1.4 pad_maximum_fusion.4
  203.3 11.7 %collective-permute-start.1 = (bf16[2,8,3,12,192]{4,3,2,1,0:T(8,128)(2,1)S(1)}, bf16[2,8,3,12,192]{4,3,2,1,0:T(8,128)(2,1)S(1)}, u32[]{:S(2)}, u32[]{:S(2)}) collective-permute-start(bf16[2,8,3,12,192]{4,3,2,1,0:T(8,128)(2,1)S(1)} %get-tuple-element.26), channel_id=1, source_target_pairs={{0,240},{16,0},{32,16},{48,32},{64,48},{80,64},{96,80},{112,96},{1... | collective-permute-start | bytes 663560 | tf_op jit(solution)/shard_map/ppermute | solution.py:18
  215.0 5.2 collective-permute-done.1
  220.6 0.3 multiply_reduce_fusion.2
  221.5 0.3 convolution_convert_fusion.9
  221.7 0.9 copy.181
  222.7 0.5 convolution_convert_fusion
  223.2 0.6 copy.176
  223.8 2.7 add_add_fusion
  226.5 2.8 fusion.100
  229.3 2.5 fusion.30
  231.8 4.0 fusion.16
  235.8 6.2 fusion.20
  241.9 7.0 %fusion.19 = bf16[4,144,1,6,32]{1,4,3,0,2:T(8,128)(2,1)} fusion(bf16[4,144,3,6,32]{1,4,3,2,0:T(8,128)(2,1)S(1)} %bitcast.163, f32[4,6,144,144]{2,3,1,0:T(8,128)} %fusion.30, f32[4,6,144,144]{2,3,1,0:T(8,128)} %get-tuple-element.35, f32[4,6,144]{2,1,0:T(8,128)S(1)} %get-tuple-element.34), kind=kOutput, calls=%fused_computation.40 | convolution fusion | flops 35448336 | bytes 14835712 | tf_op jit(solution)/shard_map/nhqk,nkhc->nqhc/dot_general | solution.py:119
  249.0 1.3 pad_maximum_fusion
  250.4 1.0 fusion.97
  251.5 0.4 add_convert_fusion.1
  252.1 7.8 %subtract_multiply_fusion.1 = f32[4,6,144,144]{2,3,1,0:T(8,128)} fusion(f32[4,6,144,144]{2,3,1,0:T(8,128)} %fusion.30, f32[4,6,144,144]{2,3,1,0:T(8,128)} %get-tuple-element.35, f32[4,6,144]{2,1,0:T(8,128)S(1)} %get-tuple-element.34), kind=kOutput, calls=%fused_computation.11 | output fusion | flops 2491919 | bytes 5985792 | tf_op jit(solution)/shard_map/sub | solution.py:117
  259.9 18.4 %reshape.269 = f32[4,6,2,6,12,2,6,12]{4,3,2,7,6,5,1,0:T(8,128)} reshape(f32[4,6,144,144]{2,3,1,0:T(8,128)} %subtract_multiply_fusion.1) | data formatting | bytes 3981312 | tf_op jit(solution)/shard_map/reshape.11
  278.3 38.2 %copy.197 = f32[4,6,2,6,12,2,6,12]{7,6,4,5,3,2,1,0:T(8,128)} copy(f32[4,6,2,6,12,2,6,12]{4,3,2,7,6,5,1,0:T(8,128)} %reshape.269) | data formatting | bytes 3981312 | tf_op jit(solution)/shard_map/reshape.11
  316.6 2.8 collective-permute-start.3
  319.4 54.3 %bitcast_convert_fusion = bf16[4,6,2,6,2,6,23]{6,5,4,3,2,1,0:T(8,128)(2,1)S(1)} fusion(f32[4,6,2,6,12,2,6,12]{7,6,4,5,3,2,1,0:T(8,128)} %copy.197), kind=kOutput, calls=%fused_computation.18 | convolution fusion | flops 137448000 | bytes 2149632 | tf_op jit(solution)/shard_map/rvhpaxqby,jxy->rvhpaqbj/dot_general | solution.py:144
  373.7 2.2 convert_element_type.180
  376.2 0.3 convolution_convert_fusion.8
  376.7 4.0 fusion.23
  380.8 2.4 fusion.32
  383.2 6.2 fusion.22
  389.4 6.3 fusion.21
  395.7 7.8 %subtract_multiply_fusion = f32[4,6,144,144]{2,3,1,0:T(8,128)} fusion(f32[4,6,144,144]{2,3,1,0:T(8,128)} %fusion.32, f32[4,6,144,144]{2,3,1,0:T(8,128)} %get-tuple-element.33, f32[4,6,144]{2,1,0:T(8,128)S(1)} %get-tuple-element.32), kind=kOutput, calls=%fused_computation.7 | output fusion | flops 2491919 | bytes 5985792 | tf_op jit(solution)/shard_map/sub | solution.py:117
  403.5 0.3 pad_maximum_fusion.1
  403.9 0.6 copy-done.12
  404.4 1.0 fusion.96
  405.5 18.4 %reshape.268 = f32[4,6,2,6,12,2,6,12]{4,3,2,7,6,5,1,0:T(8,128)} reshape(f32[4,6,144,144]{2,3,1,0:T(8,128)} %subtract_multiply_fusion) | data formatting | bytes 3981312 | tf_op jit(solution)/shard_map/reshape.6
  423.9 38.2 %copy.195 = f32[4,6,2,6,12,2,6,12]{7,6,4,5,3,2,1,0:T(8,128)} copy(f32[4,6,2,6,12,2,6,12]{4,3,2,7,6,5,1,0:T(8,128)} %reshape.268) | data formatting | bytes 3981312 | tf_op jit(solution)/shard_map/reshape.6
  462.1 53.9 %bitcast_convert_fusion.1 = bf16[4,6,2,6,2,6,23]{6,5,4,3,2,1,0:T(8,128)(2,1)S(1)} fusion(f32[4,6,2,6,12,2,6,12]{7,6,4,5,3,2,1,0:T(8,128)} %copy.195), kind=kOutput, calls=%fused_computation.19 | convolution fusion | flops 137448000 | bytes 2149632 | tf_op jit(solution)/shard_map/rvhpaxqby,jxy->rvhpaqbj/dot_general | solution.py:144
  516.1 2.2 convert_element_type.177
  518.3 0.4 add_convert_fusion
  518.8 0.9 copy.198
  519.6 140.1 %all-reduce.5.cloned.1.call-done = (bf16[1,79488]{1,0:T(2,128)(2,1)}, bf16[1,79488]{1,0:T(2,128)(2,1)}) async-done(((bf16[1,79488]{1,0:T(2,128)(2,1)}, bf16[1,79488]{1,0:T(2,128)(2,1)}), (bf16[1,79488]{1,0:T(2,128)(2,1)}, bf16[1,79488]{1,0:T(2,128)(2,1)})) %all-reduce.5.cloned.1.call-update) | async-done | bytes 317968
  659.7 1.4 dynamic-slice_convert_fusion.1
  661.2 1.4 dynamic-slice_convert_fusion
  (94 shorter events, 2.8 us)
Async XLA Ops:
  7.2 215.5 %copy-start = (bf16[192,576]{1,0:T(8,128)(2,1)S(1)}, bf16[192,576]{1,0:T(8,128)(2,1)}, u32[]{:S(2)}) copy-start(bf16[192,576]{1,0:T(8,128)(2,1)} %param.17) | copy-start | bytes 663556
  7.2 4.3 copy-start.17
  7.2 5.1 copy-start.24
  7.2 5.1 copy-start.11
  7.2 652.5 %all-reduce.5.cloned.1.call-start = ((), (), s32[]{:S(2)}) async-start(), calls=%async_computation | async-start | bytes 1271808
  8.5 5.8 copy-start.15
  11.3 2.9 copy-start.19
  11.5 2.8 copy-start.21
  81.0 19.9 %copy-start.4 = (bf16[4,144,576]{1,2,0:T(8,128)(2,1)S(1)}, bf16[4,144,576]{1,2,0:T(8,128)(2,1)}, u32[]{:S(2)}) copy-start(bf16[4,144,576]{1,2,0:T(8,128)(2,1)} %copy.162) | copy-start | bytes 1990660
  103.6 2.8 copy-start.2
  106.4 4.1 copy-start.13
  106.4 4.5 copy-start.10
  110.5 3.8 copy-start.16
  112.0 89.9 %collective-permute-start = (bf16[2,8,6,6,192]{4,3,2,1,0:T(8,128)(2,1)}, bf16[2,8,6,6,192]{4,3,2,1,0:T(8,128)(2,1)}, u32[]{:S(2)}, u32[]{:S(2)}) collective-permute-start(bf16[2,8,6,6,192]{4,3,2,1,0:T(8,128)(2,1)} %get-tuple-element.28), channel_id=1, source_target_pairs={{0,15},{1,0},{2,1},{3,2},{4,3},{5,4},{6,5},{7,6},{8,7},{9,8},{10,9... | collective-permute-start | bytes 663560 | tf_op jit(solution)/shard_map/ppermute | solution.py:18
  181.0 19.6 %copy-start.26 = (u32[256]{0:T(256)S(1)}, u32[256]{0:T(256)}, u32[]{:S(2)}) copy-start(u32[256]{0:T(256)} %constant.87) | copy-start | bytes 3076
  181.0 20.9 %copy-start.9 = (bf16[2,8,6,6,192]{4,3,2,1,0:T(8,128)(2,1)S(1)}, bf16[2,8,6,6,192]{4,3,2,1,0:T(8,128)(2,1)}, u32[]{:S(2)}) copy-start(bf16[2,8,6,6,192]{4,3,2,1,0:T(8,128)(2,1)} %get-tuple-element.29) | copy-start | bytes 663556
  201.9 19.5 %copy-start.18 = (bf16[192,192]{1,0:T(8,128)(2,1)S(1)}, bf16[192,192]{1,0:T(8,128)(2,1)}, u32[]{:S(2)}) copy-start(bf16[192,192]{1,0:T(8,128)(2,1)} %param.18) | copy-start | bytes 221188
  203.3 17.0 %collective-permute-start.1 = (bf16[2,8,3,12,192]{4,3,2,1,0:T(8,128)(2,1)S(1)}, bf16[2,8,3,12,192]{4,3,2,1,0:T(8,128)(2,1)S(1)}, u32[]{:S(2)}, u32[]{:S(2)}) collective-permute-start(bf16[2,8,3,12,192]{4,3,2,1,0:T(8,128)(2,1)S(1)} %get-tuple-element.26), channel_id=1, source_target_pairs={{0,240},{16,0},{32,16},{48,32},{64,48},{80,64},{96,80},{112,96},{1... | collective-permute-start | bytes 663560 | tf_op jit(solution)/shard_map/ppermute | solution.py:18
  220.2 2.4 copy-start.23
  221.4 1.2 copy-start.6
  226.5 2.8 copy-start.3
  226.5 2.8 copy-start.8
  249.0 2.5 copy-start.7
  252.0 64.5 %collective-permute-start.2 = (bf16[8,3,12,192]{3,2,1,0:T(8,128)(2,1)S(1)}, bf16[8,3,12,192]{3,2,1,0:T(8,128)(2,1)S(1)}, u32[]{:S(2)}, u32[]{:S(2)}) collective-permute-start(bf16[8,3,12,192]{3,2,1,0:T(8,128)(2,1)S(1)} %get-tuple-element.30), channel_id=1, source_target_pairs={{0,16},{16,32},{32,48},{48,64},{64,80},{80,96},{96,112},{112,128},... | collective-permute-start | bytes 331784 | tf_op jit(solution)/shard_map/ppermute | solution.py:18
  316.6 59.6 %copy-start.14 = (bf16[192,192]{1,0:T(8,128)(2,1)S(1)}, bf16[192,192]{1,0:T(8,128)(2,1)}, u32[]{:S(2)}) copy-start(bf16[192,192]{1,0:T(8,128)(2,1)} %param.14) | copy-start | bytes 221188
  316.6 59.3 %collective-permute-start.3 = (bf16[8,6,6,192]{3,2,1,0:T(8,128)(2,1)S(1)}, bf16[8,6,6,192]{3,2,1,0:T(8,128)(2,1)S(1)}, u32[]{:S(2)}, u32[]{:S(2)}) collective-permute-start(bf16[8,6,6,192]{3,2,1,0:T(8,128)(2,1)S(1)} %fusion.59), channel_id=1, source_target_pairs={{0,1},{1,2},{2,3},{3,4},{4,5},{5,6},{6,7},{7,8},{8,9},{9,10},{10,1... | collective-permute-start | bytes 331784 | tf_op jit(solution)/shard_map/ppermute | solution.py:18
  376.7 4.1 copy-start.5
  403.5 0.9 copy-start.12
  403.5 0.9 copy-start.20
  403.5 0.9 copy-start.22
  403.5 0.9 copy-start.25
  462.1 200.5 %copy-start.1 = (bf16[192,576]{1,0:T(8,128)(2,1)S(1)}, bf16[192,576]{1,0:T(8,128)(2,1)}, u32[]{:S(2)}) copy-start(bf16[192,576]{1,0:T(8,128)(2,1)} %param.17) | copy-start | bytes 663556
Sparse Core Ops, SparseCore 0:
  518.4 141.2 all-reduce.4
where the time goes:
time: 683 us; the launch traced here: 670 us
  local copies, waits for them, and re-layouts  247 us (36%)
  matrix products  211 us (31%)
  waiting for transfers between devices  145 us (21%)
  other arithmetic  34 us (5%)
  starting transfers between devices  16.8 us (2%)
  between operations  15.7 us (2%)
    unnamed x2, waiting for transfers between devices  140 us
    another operation x4, local copies, waits for them, and re-layouts, spread_bias(): return bias_local[:, :, None].reshape(-1, HEADS, WIN_TOK, WIN_TOK)  118 us
    another operation x5, local copies, waits for them, and re-layouts  114 us
    dot_general x2, matrix products, fold_terms(): jnp.einsum('rvhpaxqby,jxy->rvhpaqbj', pairs, offset_table(), precision=la...  108 us
    dot_general x2, matrix products, expand_rows(): jnp.einsum('rvhpaqbj,jxy->rvhpaxqby', table, offset_table(), precision=la...  51.2 us
    ppermute x4, starting transfers between devices, from_behind(): lax.ppermute(value, axis, [(i, (i + by) % count) for i in range(count)])  16.8 us
    sub x2, other arithmetic, window_backward(): grad_probs - jnp.sum(grad_probs * attn_probs, -1, keepdims=True)  15.6 us
  transfers between devices with their start and end apart: 5, of which 2 were waited for; matrix products, arithmetic and copies ran while one was open for 31% of the time, Pallas kernels for 0%

commit v1 on v0

v1 whole, which is shorter than its diff:
```python
import functools
import math

import jax
import jax.numpy as jnp
import numpy as np
from jax import lax
from jax.experimental import pallas as pl
from jax.experimental.pallas import tpu as pltpu
from jax.sharding import PartitionSpec as P

D = 192
HEADS = 6
HEAD_DIM = 32
WIN_LEV = 2
WIN_LAT = 6
WIN_LON = 12
WIN_TOK = 144
LEV = 8
LEV_WIN = LEV // WIN_LEV
BAND = WIN_LEV * WIN_LAT
OFFSETS = 2 * WIN_LON - 1
ROWS = OFFSETS * BAND
SLAB = HEADS * BAND
LANES = WIN_LON * SLAB
PIECE = 48
PIECES = 4 * PIECE
LOG2E = math.log2(math.e)
SCALE = HEAD_DIM ** (-0.5)
BF16 = jnp.bfloat16
F32 = jnp.float32


def constants():
    lanes = np.arange(LANES)
    lane_lon, lane_head, lane_pair = lanes // SLAB, lanes // BAND % HEADS, lanes % BAND
    rep = (lane_lon * BAND + lane_pair)[:, None] == np.arange(WIN_TOK)[None, :]
    mask = lane_head[:, None] == (np.arange(D) // HEAD_DIM)[None, :]
    rows = np.arange(ROWS)
    source = (rows % BAND) * OFFSETS + (OFFSETS - 1 - rows // BAND)
    perm = source[:, None] == np.arange(ROWS)[None, :]
    tok = np.arange(WIN_TOK)
    lon, lev, lat = tok // BAND, tok // WIN_LAT % WIN_LEV, tok % WIN_LAT
    within = (lon % 6) * 6 + lev * 3 + lat % 3
    cut = 2 * (lat < 3) + (lon < 6)
    joined = 2 * (lat >= 3) + (lon >= 6)
    places = np.arange(PIECES)
    split = (cut * PIECE + within)[:, None] == places[None, :]
    turn = ((lev * WIN_LAT + lat) * WIN_LON + lon)[:, None] == tok[None, :]
    join = (joined * PIECE + within)[:, None] == places[None, :]
    return dict(
        rep=rep, mask=mask, mask_t=mask.T, perm=perm, split=split, split_t=split.T, join=join, join_t=join.T, turn=turn, turn_t=turn.T
    )


CONST = {name: value.astype(jnp.bfloat16) for name, value in constants().items()}


def dot(a, b, contract=((1,), (0,))):
    return lax.dot_general(a, b, (contract, ((), ())), preferred_element_type=F32)


NT = ((1,), (1,))
TN = ((0,), (0,))


def expand_table(table, perm_ref, spread_ref):
    high = table.astype(BF16)
    rest = table - high.astype(F32)
    middle = rest.astype(BF16)
    low = (rest - middle.astype(F32)).astype(BF16)
    perm = perm_ref[...]
    spread_ref[...] = (dot(perm, high, NT) + dot(perm, middle, NT) + dot(perm, low, NT)) * LOG2E


def write_bias(spread_ref, store):
    for query_lon in range(WIN_LON):
        first = (WIN_LON - 1 - query_lon) * BAND
        store(query_lon * SLAB, spread_ref[first : first + WIN_TOK, :])


def fold_scores(low, perm_ref, folded_ref):
    folded_ref[...] = jnp.zeros_like(folded_ref)
    wide = low.astype(F32)
    for query_lon in range(WIN_LON):
        first = (WIN_LON - 1 - query_lon) * BAND
        folded_ref[first : first + WIN_TOK, :] += wide[:, query_lon * SLAB : (query_lon + 1) * SLAB]
    folded = (folded_ref[...] * (1.0 / SCALE)).astype(BF16)
    return dot(folded, perm_ref[...], TN).astype(BF16)


def gather_tokens(grid_ref, rows_ref):
    for lev in range(WIN_LEV):
        for lat in range(WIN_LAT):
            first = (lev * WIN_LAT + lat) * WIN_LON
            rows_ref[first : first + WIN_LON, :] = grid_ref[lev, lat].astype(F32)
    return rows_ref[...].astype(BF16)


def forward(inputs_f, bias, gain, w_qkv_ref, w_proj, rep, mask, mask_t):
    centred = inputs_f - jnp.mean(inputs_f, -1, keepdims=True)
    inv_std = lax.rsqrt(jnp.mean(centred * centred, -1, keepdims=True) + 1e-05)
    normed = centred * inv_std
    hidden = (normed * gain).astype(BF16)
    packed = dot(hidden, w_qkv_ref[...]).astype(BF16)
    q_rows, k_rows, v_rows = packed[:, :D], packed[:, D : 2 * D], packed[:, 2 * D :]
    q_spread = dot(rep, q_rows).astype(BF16) * mask
    scores = dot(k_rows, q_spread, NT) * (SCALE * LOG2E) + bias
    exp_scores = jnp.exp2(scores - jnp.max(scores, 0, keepdims=True))
    attn_probs = exp_scores * (1.0 / jnp.sum(exp_scores, 0, keepdims=True))
    probs_low = attn_probs.astype(BF16)
    return normed, inv_std, q_spread, k_rows, v_rows, attn_probs, probs_low


def gathered(values, weights, rep, mask_t):
    spread = dot(values, weights, TN).astype(BF16) * mask_t
    return dot(spread, rep)


def backward(normed, inv_std, q_spread, k_rows, v_rows, attn_probs, probs_low, grad, gain, w_qkv_ref, w_proj, rep, mask, mask_t):
    grad_mixed = dot(grad, w_proj, NT).astype(BF16)
    mixed_spread = dot(rep, grad_mixed).astype(BF16) * mask
    grad_probs = dot(v_rows, mixed_spread, NT)
    grad_v = dot(probs_low, mixed_spread).astype(BF16)
    grad_scores = attn_probs * (grad_probs - jnp.sum(grad_probs * attn_probs, 0, keepdims=True))
    scaled_low = (grad_scores * SCALE).astype(BF16)
    grad_k = dot(scaled_low, q_spread).astype(BF16)
    grad_q = gathered(k_rows, scaled_low, rep, mask_t).T.astype(BF16)
    grad_hidden = (
        dot(grad_q, w_qkv_ref[:, :D], NT)
        + dot(grad_k, w_qkv_ref[:, D : 2 * D], NT)
        + dot(grad_v, w_qkv_ref[:, 2 * D :], NT)
    )
    grad_normed = grad_hidden * gain
    grad_local = inv_std * (
        grad_normed
        - jnp.mean(grad_normed, -1, keepdims=True)
        - normed * jnp.mean(grad_normed * normed, -1, keepdims=True)
    )
    return (grad.astype(F32) + grad_local).astype(BF16), scaled_low


def first_kernel(
    tokens_ref, grad_ref, table_ref, gain_ref, w_qkv_ref, w_proj_ref, rep_ref, mask_ref, mask_t_ref, perm_ref, split_t_ref, turn_ref,
    stay_ref, lon_ref, lat_ref, both_ref, normed_ref, inv_ref, q_ref, k_ref, v_ref, probs_ref,
    rows_ref, spread_ref, bias_ref,
):
    expand_table(table_ref[0], perm_ref, spread_ref)

    def store(lane, block):
        bias_ref[:, lane : lane + SLAB] = block

    write_bias(spread_ref, store)
    rep, mask, mask_t = rep_ref[...], mask_ref[...], mask_t_ref[...]
    inputs_f = dot(turn_ref[...], gather_tokens(tokens_ref, rows_ref))
    normed, inv_std, q_spread, k_rows, v_rows, attn_probs, probs_low = forward(
        inputs_f, bias_ref[...], gain_ref[...], w_qkv_ref, w_proj_ref[...], rep, mask, mask_t
    )
    attended = gathered(v_rows, probs_low, rep, mask_t).T.astype(BF16)
    block_out = (inputs_f + dot(attended, w_proj_ref[...])).astype(BF16)
    normed_ref[0] = normed
    inv_ref[0] = jnp.broadcast_to(inv_std, (WIN_TOK, 128))
    q_ref[0] = q_spread
    k_ref[0] = k_rows
    v_ref[0] = v_rows
    probs_ref[0] = probs_low
    out_pieces = dot(split_t_ref[...], block_out).astype(BF16)
    grad_rows = dot(turn_ref[...], gather_tokens(grad_ref, rows_ref)).astype(BF16)
    grad_pieces = dot(split_t_ref[...], grad_rows).astype(BF16)
    for place, ref in enumerate((stay_ref, lon_ref, lat_ref, both_ref)):
        ref[0, 0] = out_pieces[place * PIECE : (place + 1) * PIECE]
        ref[1, 0] = grad_pieces[place * PIECE : (place + 1) * PIECE]


def bias_kernel(active_ref, table_ref, perm_ref, bias_ref, spread_ref):
    expand_table(table_ref[0], perm_ref, spread_ref)
    blocked = active_ref[0, 0] * (-10000.0 * LOG2E)
    key_lat = lax.broadcasted_iota(jnp.int32, (WIN_TOK, SLAB), 0) % WIN_LAT
    query_lat = lax.broadcasted_iota(jnp.int32, (WIN_TOK, SLAB), 1) % WIN_LAT
    apart = jnp.where((key_lat < 3) != (query_lat < 3), blocked, 0.0)

    def store(lane, block):
        bias_ref[0, :, lane : lane + SLAB] = block + apart

    write_bias(spread_ref, store)


def second_kernel(
    stay_ref, lon_ref, lat_ref, both_ref, bias_ref, gain_ref, w_qkv_ref, w_proj_ref, rep_ref, mask_ref, mask_t_ref, join_ref, join_t_ref,
    stay_out, lon_out, lat_out, both_out, low_ref,
):
    rep, mask, mask_t = rep_ref[...], mask_ref[...], mask_t_ref[...]
    join = join_ref[...]
    arrived = (stay_ref, lon_ref, lat_ref, both_ref)
    inputs = dot(join, jnp.concatenate([ref[0, 0] for ref in arrived], 0))
    grad = dot(join, jnp.concatenate([ref[1, 0] for ref in arrived], 0)).astype(BF16)
    gain, w_proj = gain_ref[...], w_proj_ref[...]
    saved = forward(inputs, bias_ref[0], gain, w_qkv_ref, w_proj, rep, mask, mask_t)
    input_grad, scaled_low = backward(*saved, grad, gain, w_qkv_ref, w_proj, rep, mask, mask_t)
    low_ref[0] = scaled_low
    pieces = dot(join_t_ref[...], input_grad).astype(BF16)
    for place, ref in enumerate((stay_out, lon_out, lat_out, both_out)):
        ref[0] = pieces[place * PIECE : (place + 1) * PIECE]


def fold_kernel(low_ref, perm_ref, out_ref, folded_ref):
    out_ref[0] = fold_scores(low_ref[0], perm_ref, folded_ref)


def third_kernel(
    stay_ref, lon_ref, lat_ref, both_ref, normed_ref, inv_ref, q_ref, k_ref, v_ref, probs_ref,
    gain_ref, w_qkv_ref, w_proj_ref, rep_ref, mask_ref, mask_t_ref, perm_ref, split_ref, turn_ref,
    grid_ref, term_ref,
    rows_ref, folded_ref,
):
    rep, mask, mask_t = rep_ref[...], mask_ref[...], mask_t_ref[...]
    arrived = (stay_ref, lon_ref, lat_ref, both_ref)
    grad = dot(split_ref[...], jnp.concatenate([ref[0] for ref in arrived], 0)).astype(BF16)
    probs_low = probs_ref[0]
    saved = (normed_ref[0], inv_ref[0][:, :1], q_ref[0], k_ref[0], v_ref[0], probs_low.astype(F32), probs_low)
    input_grad, scaled_low = backward(*saved, grad, gain_ref[...], w_qkv_ref, w_proj_ref[...], rep, mask, mask_t)
    rows_ref[...] = dot(turn_ref[...], input_grad)
    for lev in range(WIN_LEV):
        for lat in range(WIN_LAT):
            first = (lev * WIN_LAT + lat) * WIN_LON
            grid_ref[lev, lat] = rows_ref[first : first + WIN_LON, :].astype(BF16)
    term_ref[0] = fold_scores(scaled_low, perm_ref, folded_ref)


def fixed(*shape):
    return pl.BlockSpec(shape, lambda v: (0,) * len(shape))


def level(*shape):
    return pl.BlockSpec((1,) + shape, lambda v: (v,) + (0,) * len(shape))


def pair_of(*shape):
    return pl.BlockSpec((2, 1) + shape, lambda v: (0, v) + (0,) * len(shape))


GRID = pl.BlockSpec((WIN_LEV, WIN_LAT, WIN_LON, D), lambda v: (v, 0, 0, 0))
WEIGHTS = [fixed(1, D), fixed(D, 3 * D), fixed(D, D), fixed(LANES, WIN_TOK), fixed(LANES, D), fixed(D, LANES)]


def call(kernel, in_specs, out_specs, out_shapes, scratch, flops):
    return pl.pallas_call(
        kernel,
        grid=(LEV_WIN,),
        in_specs=in_specs,
        out_specs=out_specs,
        out_shape=[jax.ShapeDtypeStruct(shape, dtype) for shape, dtype in out_shapes],
        scratch_shapes=[pltpu.VMEM(shape, F32) for shape in scratch],
        compiler_params=pltpu.CompilerParams(vmem_limit_bytes=48 * 1024 * 1024),
        cost_estimate=pl.CostEstimate(flops=flops, bytes_accessed=4_000_000, transcendentals=500_000),
    )


def shifted(axes, by):
    sizes = [lax.axis_size(axis) for axis in axes]
    if len(sizes) == 1:
        return [(i, (i + by) % sizes[0]) for i in range(sizes[0])]
    rows, columns = sizes
    return [
        (a * columns + o, (a + by) % rows * columns + (o + by) % columns)
        for a in range(rows)
        for o in range(columns)
    ]


def exchange(pieces, by):
    stay, lon, lat, both = pieces
    return (
        stay,
        lax.ppermute(lon, ("lon",), shifted(("lon",), by)),
        lax.ppermute(lat, ("lat",), shifted(("lat",), by)),
        lax.ppermute(both, ("lat", "lon"), shifted(("lat", "lon"), by)),
    )


def body(
    tokens, grad_out, gain_one, qkv_one, proj_one, bias_one, gain_two, qkv_two, proj_two, bias_two
):
    const = {name: jnp.asarray(value) for name, value in CONST.items()}
    spread = (const["rep"], const["mask"], const["mask_t"])
    tables = (LEV_WIN, SLAB, ROWS)
    block_one = (gain_one.reshape(1, D), qkv_one, proj_one) + spread
    block_two = (gain_two.reshape(1, D), qkv_two, proj_two) + spread
    pair = ((2, LEV_WIN, PIECE, D), BF16)
    piece = ((LEV_WIN, PIECE, D), BF16)

    first = call(
        first_kernel,
        [GRID, GRID, level(SLAB, ROWS)] + WEIGHTS + [fixed(ROWS, ROWS), fixed(PIECES, WIN_TOK), fixed(WIN_TOK, WIN_TOK)],
        [pair_of(PIECE, D)] * 4
        + [level(WIN_TOK, D), level(WIN_TOK, 128), level(LANES, D)]
        + [level(WIN_TOK, D)] * 2
        + [level(WIN_TOK, LANES)],
        [pair] * 4
        + [((LEV_WIN, WIN_TOK, D), F32), ((LEV_WIN, WIN_TOK, 128), F32), ((LEV_WIN, LANES, D), BF16)]
        + [((LEV_WIN, WIN_TOK, D), BF16)] * 2
        + [((LEV_WIN, WIN_TOK, LANES), BF16)],
        [(WIN_TOK, D), (ROWS, SLAB), (WIN_TOK, LANES)],
        2_000_000_000,
    )(tokens, grad_out, bias_one.reshape(tables), *block_one, const["perm"], const["split_t"], const["turn"])
    pieces, saved = first[:4], first[4:]
    pieces, table_two = lax.optimization_barrier((tuple(pieces), bias_two.reshape(tables)))
    pieces = exchange(pieces, -1)

    active = jnp.where(lax.axis_index("lat") == lax.axis_size("lat") - 1, 1.0, 0.0).astype(F32).reshape(1, 1)
    (bias_full,) = call(
        bias_kernel,
        [pl.BlockSpec(memory_space=pltpu.SMEM), level(SLAB, ROWS), fixed(ROWS, ROWS)],
        [level(WIN_TOK, LANES)],
        [((LEV_WIN, WIN_TOK, LANES), F32)],
        [(ROWS, SLAB)],
        500_000_000,
    )(active, table_two, const["perm"])

    second = call(
        second_kernel,
        [pair_of(PIECE, D)] * 4 + [level(WIN_TOK, LANES)] + WEIGHTS + [fixed(WIN_TOK, PIECES), fixed(PIECES, WIN_TOK)],
        [level(PIECE, D)] * 4 + [level(WIN_TOK, LANES)],
        [piece] * 4 + [((LEV_WIN, WIN_TOK, LANES), BF16)],
        [],
        4_000_000_000,
    )(*pieces, bias_full, *block_two, const["join"], const["join_t"])
    grad_pieces, low_two = second[:4], second[4]
    grad_pieces = exchange(grad_pieces, 1)

    term = ((LEV_WIN, SLAB, ROWS), BF16)
    (term_two,) = call(
        fold_kernel,
        [level(WIN_TOK, LANES), fixed(ROWS, ROWS)],
        [level(SLAB, ROWS)],
        [term],
        [(ROWS, SLAB)],
        500_000_000,
    )(low_two, const["perm"])

    grad_tokens, term_one = call(
        third_kernel,
        [level(PIECE, D)] * 4
        + [level(WIN_TOK, D), level(WIN_TOK, 128), level(LANES, D)]
        + [level(WIN_TOK, D)] * 2
        + [level(WIN_TOK, LANES)]
        + WEIGHTS
        + [fixed(ROWS, ROWS), fixed(WIN_TOK, PIECES), fixed(WIN_TOK, WIN_TOK)],
        [GRID, level(SLAB, ROWS)],
        [((LEV, WIN_LAT, WIN_LON, D), BF16), term],
        [(WIN_TOK, D), (ROWS, SLAB)],
        4_000_000_000,
    )(*grad_pieces, *saved, *block_one, const["perm"], const["split"], const["turn_t"])

    tiles = lax.axis_size("lon")
    share = LEV_WIN * SLAB // tiles
    both_terms = jnp.stack([term_one.reshape(tiles, share, ROWS), term_two.reshape(tiles, share, ROWS)], 1)
    received = lax.all_to_all(both_terms, "lon", 0, 0, tiled=True)
    summed = received.reshape(tiles, 2, share, ROWS).astype(F32).sum(0)
    return grad_tokens, summed[0].reshape(1, -1), summed[1].reshape(1, -1)


def solution(mesh):
    in_specs = (
        P(None, "lat", "lon", None),
        P(None, "lat", "lon", None),
        P(),
        P(),
        P(),
        P("lat", None),
        P(),
        P(),
        P(),
        P("lat", None),
    )
    out_specs = (P(None, "lat", "lon", None), P("lat", "lon"), P("lat", "lon"))
    return jax.shard_map(body, mesh=mesh, in_specs=in_specs, out_specs=out_specs, check_vma=False)
```

time: 683 us -> 97 us (0.14)
  the two profiles are of different devices: /device:TPU:2 before, /device:TPU:24 now
where the time goes in v1:
time: 97 us; the launch traced here: 96.5 us
  Pallas kernels  33.4 us (34%)
  waiting for transfers between devices  26.1 us (27%)
  local copies, waits for them, and re-layouts  16.1 us (17%)
  starting transfers between devices  14.8 us (15%)
  other arithmetic  5.1 us (5%)
  between operations  0.97 us (1%)
    all_to_all x1, waiting for transfers between devices, body(): received = lax.all_to_all(both_terms, 'lon', 0, 0, tiled=True)  16.3 us
    unnamed x65, local copies, waits for them, and re-layouts  11.5 us
    pallas_call x1, Pallas kernels, body(): call(second_kernel, [pair_of(PIECE, D)] * 4 + [level(WIN_TOK, LANES)] + W...  10.3 us
    pallas_call x1, Pallas kernels, body(): call(first_kernel, [GRID, GRID, level(SLAB, ROWS)] + WEIGHTS + [fixed(ROW...  9.95 us
    pallas_call x1, Pallas kernels, body(): call(third_kernel, [level(PIECE, D)] * 4 + [level(WIN_TOK, D), level(WIN_...  8.74 us
    ppermute x2, starting transfers between devices, exchange(): lax.ppermute(lon, ('lon',), shifted(('lon',), by))  6.95 us
    ppermute x2, waiting for transfers between devices, exchange(): lax.ppermute(both, ('lat', 'lon'), shifted(('lat', 'lon'), by))  6.39 us
    all_to_all x1, starting transfers between devices, body(): received = lax.all_to_all(both_terms, 'lon', 0, 0, tiled=True)  4.44 us
  transfers between devices with their start and end apart: 7, of which 5 were waited for; matrix products, arithmetic and copies ran while one was open for 2% of the time, Pallas kernels for 5%

profile of v1, /device:TPU:24, one launch (start us, length us, event | category | flops | bytes accessed | tf_op | source)
XLA Modules:
  0.0 96.5 jit_solution(5282391548798534953)
XLA Ops:
  0.6 0.0 copy-start
  0.6 0.0 copy-start.7
  0.7 0.0 copy-start.8
  0.7 0.0 copy-start.9
  0.7 0.0 copy-start.13
  0.7 0.0 copy-start.14
  0.7 1.9 %reduce = f32[79488]{0:T(1024)S(1)} reduce(f32[1,79488]{1,0:T(1,128)} %param.25, f32[]{:T(128)} %constant.42), dimensions={0}, to_apply=%param.25.reduce_sub_computation | reduce | bytes 635908 | tf_op args[5]
  2.6 0.4 reshape.21.table_ref
  3.0 1.7 %reduce.1 = f32[79488]{0:T(1024)S(1)} reduce(f32[1,79488]{1,0:T(1,128)} %param.29, f32[]{:T(128)} %constant.42), dimensions={0}, to_apply=%param.29.reduce_sub_computation | reduce | bytes 635908 | tf_op args[9]
  4.8 0.4 reshape.23.table_ref
  5.2 1.0 %copy.33.tokens_ref = bf16[8,6,12,192]{3,2,1,0:T(8,128)(2,1)S(1)} copy(bf16[8,6,12,192]{3,0,2,1:T(8,128)(2,1)} %param.20) | data formatting | bytes 442368 | tf_op args[0]
  6.2 1.0 %copy.34.grad_ref = bf16[8,6,12,192]{3,2,1,0:T(8,128)(2,1)S(1)} copy(bf16[8,6,12,192]{3,0,2,1:T(8,128)(2,1)} %param.21) | data formatting | bytes 442368 | tf_op args[1]
  7.3 0.0 copy-done
  7.3 0.0 copy-done.7
  7.3 0.0 copy-done.8
  7.3 0.0 copy-done.9
  7.3 0.0 copy-done.13
  7.3 0.0 copy-done.14
  7.3 0.0 copy-done.4
  7.3 0.0 copy-done.2
  7.4 0.0 copy-done.6
  7.4 10.0 %shard_map.211 = (bf16[2,4,48,192]{3,2,1,0:T(8,128)(2,1)S(1)}, bf16[2,4,48,192]{3,2,1,0:T(8,128)(2,1)S(1)}, bf16[2,4,48,192]{3,2,1,0:T(8,128)(2,1)S(1)}, bf16[2,...) custom-call(bf16[8,6,12,192]{3,2,1,0:T(8,128)(2,1)S(1)} %copy.33.tok, ...), custom_call_target="tpu_custom_call" | custom-call | flops 2000000000 | bytes 4000000 | tf_op jit(solution)/shard_map/pallas_call | solution.py:292
  17.3 0.8 copy-done.19
  18.2 0.7 copy-done.21
  18.9 0.7 copy-done.23
  19.6 0.7 copy-done.25
  20.3 0.7 copy-done.27
  21.0 6.9 %collective-permute-start = (bf16[2,4,48,192]{3,2,1,0:T(8,128)(2,1)S(1)}, bf16[2,4,48,192]{3,2,1,0:T(8,128)(2,1)S(1)}, u32[]{:S(2)}, u32[]{:S(2)}) collective-permute-start(bf16[2,4,48,192]{3,2,1,0:T(8,128)(2,1)S(1)} %get-tuple-element.30), channel_id=1, source_target_pairs={{0,15},{1,0},{2,1},{3,2},{4,3},{5,4},{6,5},{7,6},{8,7},{9,8},{10,9... | collective-permute-start | bytes 442376 | tf_op jit(solution)/shard_map/ppermute | solution.py:275
  27.8 0.0 collective-permute-start.1
  27.9 0.8 collective-permute-start.2
  28.7 2.4 %shard_map.212.bias_ref = f32[4,144,864]{2,1,0:T(8,128)S(1)} custom-call(f32[1,1]{1,0:T(1,128)} %bitcast.1.active_ref, f32[4,72,276]{2,1,0:T(8,128)S(1)} %reshape.23.table_ref, bf16[276,276]{1,0:T(8,128)(2,1)S(1)} %copy-done), custom_call_target="tpu_custom_call" | custom-call | flops 500000000 | bytes 4000000 | tf_op jit(solution)/shard_map/pallas_call | solution.py:311
  31.1 2.1 %collective-permute-done.lon_ref = bf16[2,4,48,192]{3,2,1,0:T(8,128)(2,1)S(1)} collective-permute-done((bf16[2,4,48,192]{3,2,1,0:T(8,128)(2,1)S(1)}, bf16[2,4,48,192]{3,2,1,0:T(8,128)(2,1)S(1)}, u32[]{:S(2)}, u32[]{:S(2)}) %collective-permute-start) | collective-permute-done | bytes 147488 | tf_op jit(solution)/shard_map/ppermute | solution.py:275
  33.2 0.0 collective-permute-done.1.lat_ref
  33.2 3.1 %collective-permute-done.2.both_ref = bf16[2,4,48,192]{3,2,1,0:T(8,128)(2,1)S(1)} collective-permute-done((bf16[2,4,48,192]{3,2,1,0:T(8,128)(2,1)S(1)}, bf16[2,4,48,192]{3,2,1,0:T(8,128)(2,1)S(1)}, u32[]{:S(2)}, u32[]{:S(2)}) %collective-permute-start.2) | collective-permute-done | bytes 147488 | tf_op jit(solution)/shard_map/ppermute | solution.py:277
  36.2 0.0 copy-done.1
  36.2 0.0 copy-done.10
  36.2 0.0 copy-done.17
  36.2 0.0 copy-done.28
  36.3 10.3 %shard_map.213 = (bf16[4,48,192]{2,1,0:T(8,128)(2,1)S(1)}, bf16[4,48,192]{2,1,0:T(8,128)(2,1)S(1)}, bf16[4,48,192]{2,1,0:T(8,128)(2,1)S(1)}, bf16[4,48,192]{2,1,0:T(8,128)(2,1)S(1)}, bf16[4,144,864]{2,1,0:T(8,128)(2,1)S(1)}) custom-call(bf16[2,4,48,192]{3,2,1,0:T(8,128)(2,1)S(1)} %copy-done.28, bf16[2,4,48,192]{3,2,1,0:T(8,128)(2,1)S(1)} %collective-permute-done.lon_ref, ...), custom_call_target="tpu_custom_call" | custom-call | flops 4000000000 | bytes 4000000 | tf_op jit(solution)/shard_map/pallas_call | solution.py:320
  46.6 0.6 copy-done.29
  47.2 0.1 collective-permute-start.3
  47.3 2.3 %collective-permute-start.4 = (bf16[4,48,192]{2,1,0:T(8,128)(2,1)S(1)}, bf16[4,48,192]{2,1,0:T(8,128)(2,1)S(1)}, u32[]{:S(2)}, u32[]{:S(2)}) collective-permute-start(bf16[4,48,192]{2,1,0:T(8,128)(2,1)S(1)} %get-tuple-element.36), channel_id=1, source_target_pairs={{0,16},{16,32},{32,48},{48,64},{64,80},{80,96},{96,112},{112,128},... | collective-permute-start | bytes 221192 | tf_op jit(solution)/shard_map/ppermute | solution.py:276
  49.6 0.3 collective-permute-start.5
  49.9 2.0 %shard_map.215 = bf16[4,72,276]{2,1,0:T(8,128)(2,1)S(1)} custom-call(bf16[4,144,864]{2,1,0:T(8,128)(2,1)S(1)} %get-tuple-element.46.low_ref, bf16[276,276]{1,0:T(8,128)(2,1)S(1)} %copy-done), custom_call_target="tpu_custom_call" | custom-call | flops 500000000 | bytes 4000000 | tf_op jit(solution)/shard_map/pallas_call | solution.py:332
  51.9 0.8 stack_reshape.7
  52.7 1.3 %collective-permute-done.3.lon_ref = bf16[4,48,192]{2,1,0:T(8,128)(2,1)S(1)} collective-permute-done((bf16[4,48,192]{2,1,0:T(8,128)(2,1)S(1)}, bf16[4,48,192]{2,1,0:T(8,128)(2,1)S(1)}, u32[]{:S(2)}, u32[]{:S(2)}) %collective-permute-start.3) | collective-permute-done | bytes 73760 | tf_op jit(solution)/shard_map/ppermute | solution.py:275
  54.0 0.0 collective-permute-done.4.lat_ref
  54.0 3.3 %collective-permute-done.5.both_ref = bf16[4,48,192]{2,1,0:T(8,128)(2,1)S(1)} collective-permute-done((bf16[4,48,192]{2,1,0:T(8,128)(2,1)S(1)}, bf16[4,48,192]{2,1,0:T(8,128)(2,1)S(1)}, u32[]{:S(2)}, u32[]{:S(2)}) %collective-permute-start.5) | collective-permute-done | bytes 73760 | tf_op jit(solution)/shard_map/ppermute | solution.py:277
  57.4 0.0 copy-done.11
  57.4 1.2 %copy-done.18 = bf16[4,144,864]{2,1,0:T(8,128)(2,1)S(1)} copy-done((bf16[4,144,864]{2,1,0:T(8,128)(2,1)S(1)}, bf16[4,144,864]{2,1,0:T(8,128)(2,1)}, u32[]{:S(2)}) %copy-start.18) | copy-done | bytes 995352
  58.6 1.1 %copy-done.20 = f32[4,144,192]{2,1,0:T(8,128)S(1)} copy-done((f32[4,144,192]{2,1,0:T(8,128)S(1)}, f32[4,144,192]{2,1,0:T(8,128)}, u32[]{:S(2)}) %copy-start.20) | copy-done | bytes 442392
  59.7 1.0 copy-done.24
  60.7 1.0 copy-done.26
  61.6 8.7 %shard_map.214 = (bf16[8,6,12,192]{3,2,1,0:T(8,128)(2,1)S(1)}, bf16[4,72,276]{2,1,0:T(8,128)(2,1)S(1)}) custom-call(bf16[4,48,192]{2,1,0:T(8,128)(2,1)S(1)} %copy-done.30, bf16[4,48,192]{2,1,0:T(8,128)(2,1)S(1)} %collective-permute-done.3.lon_ref, bf16[4,48,192]{2,1,0:T(8,128)(2,1)S(1)} %collective-permute-done.4.lat_ref, ...), custom_call_target="tpu_custom_call" | custom-call | flops 4000000000 | bytes 4000000 | tf_op jit(solution)/shard_map/pallas_call | solution.py:341
  70.4 0.1 stack_reshape.6
  70.5 1.1 %pad_maximum_fusion = bf16[16,2,18,276]{3,2,0,1:T(8,128)(2,1)S(1)} fusion(bf16[16,1,18,276]{3,2,0,1:T(8,128)(2,1)} %stack_reshape.7, bf16[16,1,18,276]{3,2,0,1:T(8,128)(2,1)S(1)} %stack_reshape.6), kind=kLoop, calls=%fused_computation.1 | loop fusion | flops 158976 | bytes 635904 | tf_op jit(solution)/shard_map/stack | solution.py:357
  71.6 1.2 %copy.35 = bf16[16,2,18,276]{3,1,2,0:T(2,128)(2,1)} copy(bf16[16,2,18,276]{3,2,0,1:T(8,128)(2,1)S(1)} %pad_maximum_fusion) | data formatting | bytes 635904 | tf_op jit(solution)/shard_map/stack | solution.py:357
  72.8 4.4 %all-to-all-start = ((bf16[16,2,18,276]{3,1,2,0:T(2,128)(2,1)}), bf16[16,2,18,276]{3,1,2,0:T(2,128)(2,1)S(1)}, u32[]{:S(2)}, u32[]{:S(2)}) async-start(bf16[16,2,18,276]{3,1,2,0:T(2,128)(2,1)} %copy.35), calls=%async_computation | async-start | bytes 884736 | tf_op jit(solution)/shard_map/all_to_all | solution.py:358
  77.2 0.9 copy.36
  78.1 16.3 %all-to-all-done = bf16[16,2,18,276]{3,1,2,0:T(2,128)(2,1)S(1)} async-done(((bf16[16,2,18,276]{3,1,2,0:T(2,128)(2,1)}), bf16[16,2,18,276]{3,1,2,0:T(2,128)(2,1)S(1)}, u32[]{:S(2)}, u32[]{:S(2)}) %all-to-all-start) | async-done | bytes 317984 | tf_op jit(solution)/shard_map/all_to_all | solution.py:358
  94.4 0.4 convert_reduce_fusion
  94.8 0.1 slice_reduce_fusion
  95.0 0.7 reshape_squeeze.7
  95.7 0.7 reshape_squeeze.6
  (32 shorter events, 0.1 us)
Async XLA Ops:
  0.6 6.6 %copy-start = (bf16[276,276]{1,0:T(8,128)(2,1)S(1)}, bf16[276,276]{1,0:T(8,128)(2,1)}, u32[]{:S(2)}) copy-start(bf16[276,276]{1,0:T(8,128)(2,1)} %constant.32.clone.perm_ref) | copy-start | bytes 457060
  0.6 6.6 %copy-start.7 = (bf16[864,192]{1,0:T(8,128)(2,1)S(1)}, bf16[864,192]{1,0:T(8,128)(2,1)}, u32[]{:S(2)}) copy-start(bf16[864,192]{1,0:T(8,128)(2,1)} %constant.30.clone.mask_ref) | copy-start | bytes 995332
  0.7 6.6 %copy-start.8 = (bf16[864,144]{1,0:T(8,128)(2,1)S(1)}, bf16[864,144]{1,0:T(8,128)(2,1)}, u32[]{:S(2)}) copy-start(bf16[864,144]{1,0:T(8,128)(2,1)} %constant.29.clone.rep_ref) | copy-start | bytes 746500
  0.7 6.6 %copy-start.9 = (bf16[192,864]{1,0:T(8,128)(2,1)S(1)}, bf16[192,864]{1,0:T(8,128)(2,1)}, u32[]{:S(2)}) copy-start(bf16[192,864]{1,0:T(8,128)(2,1)} %constant.31.clone.mask_t_ref) | copy-start | bytes 995332
  0.7 6.6 %copy-start.13 = (bf16[192,144]{1,0:T(8,128)(2,1)S(1)}, bf16[192,144]{1,0:T(8,128)(2,1)}, u32[]{:S(2)}) copy-start(bf16[192,144]{1,0:T(8,128)(2,1)} %constant.34.clone.split_t_ref) | copy-start | bytes 165892
  0.7 6.6 %copy-start.14 = (bf16[144,144]{1,0:T(8,128)(2,1)S(1)}, bf16[144,144]{1,0:T(8,128)(2,1)}, u32[]{:S(2)}) copy-start(bf16[144,144]{1,0:T(8,128)(2,1)} %constant.37.clone.turn_ref) | copy-start | bytes 124420
  0.7 6.6 %copy-start.4 = (bf16[192,192]{1,0:T(8,128)(2,1)S(1)}, bf16[192,192]{1,0:T(8,128)(2,1)}, u32[]{:S(2)}) copy-start(bf16[192,192]{1,0:T(8,128)(2,1)} %w_proj_ref.5) | copy-start | bytes 221188
  0.7 6.6 %copy-start.2 = (bf16[192,576]{1,0:T(8,128)(2,1)S(1)}, bf16[192,576]{1,0:T(8,128)(2,1)}, u32[]{:S(2)}) copy-start(bf16[192,576]{1,0:T(8,128)(2,1)} %w_qkv_ref.5) | copy-start | bytes 663556
  0.7 6.6 %copy-start.6 = (f32[192]{0:T(256)S(1)}, f32[192]{0:T(256)}, u32[]{:S(2)}) copy-start(f32[192]{0:T(256)} %param.22) | copy-start | bytes 2308
  17.3 0.8 copy-start.19
  18.2 0.7 copy-start.21
  18.9 0.7 copy-start.23
  19.6 0.7 copy-start.25
  20.3 0.7 copy-start.27
  21.0 15.2 %copy-start.1 = (bf16[192,576]{1,0:T(8,128)(2,1)S(1)}, bf16[192,576]{1,0:T(8,128)(2,1)}, u32[]{:S(2)}) copy-start(bf16[192,576]{1,0:T(8,128)(2,1)} %w_qkv_ref.4) | copy-start | bytes 663556
  21.0 15.2 %copy-start.3 = (bf16[192,192]{1,0:T(8,128)(2,1)S(1)}, bf16[192,192]{1,0:T(8,128)(2,1)}, u32[]{:S(2)}) copy-start(bf16[192,192]{1,0:T(8,128)(2,1)} %w_proj_ref.4) | copy-start | bytes 221188
  21.0 15.2 %copy-start.5 = (f32[192]{0:T(256)S(1)}, f32[192]{0:T(256)}, u32[]{:S(2)}) copy-start(f32[192]{0:T(256)} %param.26) | copy-start | bytes 2308
  21.0 15.2 %copy-start.12 = (bf16[192,144]{1,0:T(8,128)(2,1)S(1)}, bf16[192,144]{1,0:T(8,128)(2,1)}, u32[]{:S(2)}) copy-start(bf16[192,144]{1,0:T(8,128)(2,1)} %constant.36.clone.join_t_ref) | copy-start | bytes 165892
  21.0 12.2 %collective-permute-start = (bf16[2,4,48,192]{3,2,1,0:T(8,128)(2,1)S(1)}, bf16[2,4,48,192]{3,2,1,0:T(8,128)(2,1)S(1)}, u32[]{:S(2)}, u32[]{:S(2)}) collective-permute-start(bf16[2,4,48,192]{3,2,1,0:T(8,128)(2,1)S(1)} %get-tuple-element.30), channel_id=1, source_target_pairs={{0,15},{1,0},{2,1},{3,2},{4,3},{5,4},{6,5},{7,6},{8,7},{9,8},{10,9... | collective-permute-start | bytes 442376 | tf_op jit(solution)/shard_map/ppermute | solution.py:275
  27.8 5.3 %collective-permute-start.1 = (bf16[2,4,48,192]{3,2,1,0:T(8,128)(2,1)S(1)}, bf16[2,4,48,192]{3,2,1,0:T(8,128)(2,1)S(1)}, u32[]{:S(2)}, u32[]{:S(2)}) collective-permute-start(bf16[2,4,48,192]{3,2,1,0:T(8,128)(2,1)S(1)} %get-tuple-element.31), channel_id=1, source_target_pairs={{0,240},{16,0},{32,16},{48,32},{64,48},{80,64},{96,80},{112,96},{1... | collective-permute-start | bytes 442376 | tf_op jit(solution)/shard_map/ppermute | solution.py:276
  27.9 8.4 %collective-permute-start.2 = (bf16[2,4,48,192]{3,2,1,0:T(8,128)(2,1)S(1)}, bf16[2,4,48,192]{3,2,1,0:T(8,128)(2,1)S(1)}, u32[]{:S(2)}, u32[]{:S(2)}) collective-permute-start(bf16[2,4,48,192]{3,2,1,0:T(8,128)(2,1)S(1)} %get-tuple-element.32), channel_id=1, source_target_pairs={{0,255},{1,240},{2,241},{3,242},{4,243},{5,244},{6,245},{7,246},{8... | collective-permute-start | bytes 442376 | tf_op jit(solution)/shard_map/ppermute | solution.py:277
  28.7 7.6 %copy-start.10 = (bf16[192,864]{1,0:T(8,128)(2,1)S(1)}, bf16[192,864]{1,0:T(8,128)(2,1)}, u32[]{:S(2)}) copy-start(bf16[192,864]{1,0:T(8,128)(2,1)} %constant.31.clone.mask_t_ref) | copy-start | bytes 995332
  28.7 7.6 %copy-start.17 = (bf16[144,192]{1,0:T(8,128)(2,1)S(1)}, bf16[144,192]{1,0:T(8,128)(2,1)}, u32[]{:S(2)}) copy-start(bf16[144,192]{1,0:T(8,128)(2,1)} %constant.35.clone.join_ref) | copy-start | bytes 165892
  28.7 7.6 %copy-start.28 = (bf16[2,4,48,192]{3,2,1,0:T(8,128)(2,1)S(1)}, bf16[2,4,48,192]{3,2,1,0:T(8,128)(2,1)}, u32[]{:S(2)}) copy-start(bf16[2,4,48,192]{3,2,1,0:T(8,128)(2,1)} %copy-done.27) | copy-start | bytes 442372
  46.6 0.6 copy-start.29
  47.2 10.2 %copy-start.11 = (bf16[192,864]{1,0:T(8,128)(2,1)S(1)}, bf16[192,864]{1,0:T(8,128)(2,1)}, u32[]{:S(2)}) copy-start(bf16[192,864]{1,0:T(8,128)(2,1)} %constant.31.clone.mask_t_ref) | copy-start | bytes 995332
  47.2 10.2 %copy-start.15 = (bf16[144,144]{1,0:T(8,128)(2,1)S(1)}, bf16[144,144]{1,0:T(8,128)(2,1)}, u32[]{:S(2)}) copy-start(bf16[144,144]{1,0:T(8,128)(2,1)} %constant.37.clone.turn_ref) | copy-start | bytes 124420
  47.2 10.2 %copy-start.16 = (bf16[144,192]{1,0:T(8,128)(2,1)S(1)}, bf16[144,192]{1,0:T(8,128)(2,1)}, u32[]{:S(2)}) copy-start(bf16[144,192]{1,0:T(8,128)(2,1)} %constant.33.clone.split_ref) | copy-start | bytes 165892
  47.2 10.2 %copy-start.22 = (f32[4,144,128]{2,1,0:T(8,128)S(1)}, f32[4,144,128]{2,1,0:T(8,128)}, u32[]{:S(2)}) copy-start(f32[4,144,128]{2,1,0:T(8,128)} %copy-done.21) | copy-start | bytes 884740
  47.2 10.2 %copy-start.30 = (bf16[4,48,192]{2,1,0:T(8,128)(2,1)S(1)}, bf16[4,48,192]{2,1,0:T(8,128)(2,1)}, u32[]{:S(2)}) copy-start(bf16[4,48,192]{2,1,0:T(8,128)(2,1)} %copy-done.29) | copy-start | bytes 221188
  47.2 6.8 %collective-permute-start.3 = (bf16[4,48,192]{2,1,0:T(8,128)(2,1)S(1)}, bf16[4,48,192]{2,1,0:T(8,128)(2,1)S(1)}, u32[]{:S(2)}, u32[]{:S(2)}) collective-permute-start(bf16[4,48,192]{2,1,0:T(8,128)(2,1)S(1)} %get-tuple-element.35), channel_id=1, source_target_pairs={{0,1},{1,2},{2,3},{3,4},{4,5},{5,6},{6,7},{7,8},{8,9},{9,10},{10,1... | collective-permute-start | bytes 221192 | tf_op jit(solution)/shard_map/ppermute | solution.py:275
  47.3 6.7 %collective-permute-start.4 = (bf16[4,48,192]{2,1,0:T(8,128)(2,1)S(1)}, bf16[4,48,192]{2,1,0:T(8,128)(2,1)S(1)}, u32[]{:S(2)}, u32[]{:S(2)}) collective-permute-start(bf16[4,48,192]{2,1,0:T(8,128)(2,1)S(1)} %get-tuple-element.36), channel_id=1, source_target_pairs={{0,16},{16,32},{32,48},{48,64},{64,80},{80,96},{96,112},{112,128},... | collective-permute-start | bytes 221192 | tf_op jit(solution)/shard_map/ppermute | solution.py:276
  49.6 7.7 %collective-permute-start.5 = (bf16[4,48,192]{2,1,0:T(8,128)(2,1)S(1)}, bf16[4,48,192]{2,1,0:T(8,128)(2,1)S(1)}, u32[]{:S(2)}, u32[]{:S(2)}) collective-permute-start(bf16[4,48,192]{2,1,0:T(8,128)(2,1)S(1)} %get-tuple-element.37), channel_id=1, source_target_pairs={{0,17},{1,18},{2,19},{3,20},{4,21},{5,22},{6,23},{7,24},{8,25},{9,... | collective-permute-start | bytes 221192 | tf_op jit(solution)/shard_map/ppermute | solution.py:277
  57.4 1.2 %copy-start.18 = (bf16[4,144,864]{2,1,0:T(8,128)(2,1)S(1)}, bf16[4,144,864]{2,1,0:T(8,128)(2,1)}, u32[]{:S(2)}) copy-start(bf16[4,144,864]{2,1,0:T(8,128)(2,1)} %get-tuple-element.43.probs_ref) | copy-start | bytes 2985988
  58.6 1.1 %copy-start.20 = (f32[4,144,192]{2,1,0:T(8,128)S(1)}, f32[4,144,192]{2,1,0:T(8,128)}, u32[]{:S(2)}) copy-start(f32[4,144,192]{2,1,0:T(8,128)} %copy-done.19) | copy-start | bytes 1327108
  59.7 1.0 copy-start.24
  60.7 1.0 copy-start.26
  72.8 21.6 %all-to-all-start = ((bf16[16,2,18,276]{3,1,2,0:T(2,128)(2,1)}), bf16[16,2,18,276]{3,1,2,0:T(2,128)(2,1)S(1)}, u32[]{:S(2)}, u32[]{:S(2)}) async-start(bf16[16,2,18,276]{3,1,2,0:T(2,128)(2,1)} %copy.35), calls=%async_computation | async-start | bytes 884736 | tf_op jit(solution)/shard_map/all_to_all | solution.py:358

commit v2 on v1

v2 whole, which is shorter than its diff:
```python
import math

import jax
import jax.numpy as jnp
import numpy as np
from jax import lax
from jax.experimental import pallas as pl
from jax.experimental.pallas import tpu as pltpu
from jax.sharding import PartitionSpec as P

D = 192
HEADS = 6
HEAD_DIM = 32
WIN_LEV = 2
WIN_LAT = 6
WIN_LON = 12
WIN_TOK = 144
LEV = 8
LEV_WIN = LEV // WIN_LEV
BAND = WIN_LEV * WIN_LAT
OFFSETS = 2 * WIN_LON - 1
ROWS = OFFSETS * BAND
SLAB = HEADS * BAND
LANES = WIN_LON * SLAB
PIECE = 36
FLAT = 128
TERM = 40
SHARE = 18
REST = ROWS - 2 * FLAT
LOG2E = math.log2(math.e)
SCALE = HEAD_DIM ** (-0.5)
BF16 = jnp.bfloat16
F32 = jnp.float32
LEVELS = range(LEV_WIN)


def constants():
    lanes = np.arange(LANES)
    lane_lon, lane_head, lane_pair = lanes // SLAB, lanes // BAND % HEADS, lanes % BAND
    rep = (lane_lon * BAND + lane_pair)[:, None] == np.arange(WIN_TOK)[None, :]
    mask = lane_head[:, None] == (np.arange(D) // HEAD_DIM)[None, :]
    rows = np.arange(ROWS)
    source = (rows % BAND) * OFFSETS + (OFFSETS - 1 - rows // BAND)
    perm = source[:, None] == np.arange(3 * FLAT)[None, :]
    tok = np.arange(WIN_TOK)
    lon, lev, lat = tok // BAND, tok // WIN_LAT % WIN_LEV, tok % WIN_LAT
    within = (lon % 6) * 6 + lev * 3 + lat % 3
    cut = 2 * (lat < 3) + (lon < 6)
    joined = 2 * (lat >= 3) + (lon >= 6)
    split = (cut * PIECE + within)[:, None] == tok[None, :]
    join = (joined * PIECE + within)[:, None] == tok[None, :]
    turn = ((lev * WIN_LAT + lat) * WIN_LON + lon)[:, None] == tok[None, :]
    return dict(
        rep=rep, mask=mask, mask_t=mask.T, perm=perm, split=split, split_t=split.T, join=join, join_t=join.T,
        turn=turn, turn_t=turn.T,
    )


CONST = {name: value.astype(jnp.bfloat16) for name, value in constants().items()}


def dot(a, b, contract=((1,), (0,))):
    return lax.dot_general(a, b, (contract, ((), ())), preferred_element_type=F32)


NT = ((1,), (1,))
TN = ((0,), (0,))


def expand_table(flat_ref, perm_ref, parts, spread_ref):
    lane = lax.broadcasted_iota(jnp.int32, (9, FLAT), 1)
    for first in range(32):
        base, off = ROWS * first // FLAT, ROWS * first % FLAT
        count = -(-(off + ROWS) // FLAT)
        rows = [flat_ref[pl.ds(base + k, 9, stride=69), :] for k in range(count)]
        if off:
            rows = [pltpu.roll(row, FLAT - off, 1) for row in rows]
        for place, part in enumerate(parts):
            value = rows[place]
            if off and place + 1 < count:
                value = jnp.where(lane < FLAT - off, value, rows[place + 1])
            part[pl.ds(first, 9, stride=32), :] = value
    table = jnp.concatenate([part[...] for part in parts], 1)
    high = table.astype(BF16)
    rest = table - high.astype(F32)
    middle = rest.astype(BF16)
    low = (rest - middle.astype(F32)).astype(BF16)
    perm = perm_ref[...]
    spread_ref[...] = (dot(perm, high, NT) + dot(perm, middle, NT) + dot(perm, low, NT)) * LOG2E


def write_bias(spread_ref, bias_ref, apart=None):
    for query_lon in range(WIN_LON):
        first = (WIN_LON - 1 - query_lon) * BAND
        for v in LEVELS:
            block = spread_ref[first : first + WIN_TOK, v * SLAB : (v + 1) * SLAB]
            if apart is not None:
                block = block + apart
            bias_ref[v, :, query_lon * SLAB : (query_lon + 1) * SLAB] = block


def fold_scores(lows, perm_ref, folded_ref, table_ref, pack_ref):
    folded_ref[...] = jnp.zeros_like(folded_ref)
    wide = [low.astype(F32) for low in lows]
    for query_lon in range(WIN_LON):
        first = (WIN_LON - 1 - query_lon) * BAND
        block = jnp.concatenate([low[:, query_lon * SLAB : (query_lon + 1) * SLAB] for low in wide], 1)
        folded_ref[first : first + WIN_TOK, :] += block
    folded = (folded_ref[...] * (1.0 / SCALE)).astype(BF16)
    table_ref[...] = dot(folded, perm_ref[...], TN)
    for tile in range(LEV_WIN * SLAB // SHARE):
        top = tile * SHARE
        pack_ref[tile, :SHARE, :] = table_ref[top : top + SHARE, :FLAT]
        pack_ref[tile, SHARE : 2 * SHARE, :] = table_ref[top : top + SHARE, FLAT : 2 * FLAT]
        pack_ref[tile, 2 * SHARE : TERM, :] = jnp.zeros((TERM - 2 * SHARE, FLAT), F32)
        for group in range(5):
            count = min(4, SHARE - 4 * group)
            pack_ref[tile, 2 * SHARE : 2 * SHARE + count, group * REST : (group + 1) * REST] = table_ref[
                top + 4 * group : top + 4 * group + count, 2 * FLAT : ROWS
            ]


def load_windows(grid_ref, left_ref, right_ref):
    wide = grid_ref[...].astype(F32).reshape(LEV * BAND // WIN_LEV * WIN_LON, D)
    left_ref[...] = wide[:, :FLAT]
    right_ref[:, : D - FLAT] = wide[:, FLAT:]
    windows = []
    for v in LEVELS:
        halves = []
        for lev in range(WIN_LEV):
            rows = pl.ds(WIN_LEV * v + lev, WIN_LAT * WIN_LON, stride=LEV)
            halves.append(jnp.concatenate([left_ref[rows, :], right_ref[rows, :][:, : D - FLAT]], 1))
        windows.append(jnp.concatenate(halves, 0).astype(BF16))
    return windows


def store_windows(windows, grid_ref, left_ref, right_ref):
    for v in LEVELS:
        for lev in range(WIN_LEV):
            rows = pl.ds(WIN_LEV * v + lev, WIN_LAT * WIN_LON, stride=LEV)
            half = windows[v][lev * WIN_LAT * WIN_LON : (lev + 1) * WIN_LAT * WIN_LON]
            left_ref[rows, :] = half[:, :FLAT]
            right_ref[rows, :] = jnp.concatenate([half[:, FLAT:], jnp.zeros((WIN_LAT * WIN_LON, 2 * FLAT - D), F32)], 1)
    wide = jnp.concatenate([left_ref[...], right_ref[:, : D - FLAT]], 1)
    grid_ref[...] = wide.reshape(WIN_LAT * WIN_LON, LEV, D).astype(BF16)


def forward(inputs, biases, gain, w_qkv, rep, mask):
    centred = [x - jnp.mean(x, -1, keepdims=True) for x in inputs]
    inv_std = [lax.rsqrt(jnp.mean(x * x, -1, keepdims=True) + 1e-05) for x in centred]
    normed = [x * inv for x, inv in zip(centred, inv_std)]
    hidden = [(x * gain).astype(BF16) for x in normed]
    packed = [dot(x, w_qkv).astype(BF16) for x in hidden]
    k_rows = [x[:, D : 2 * D] for x in packed]
    v_rows = [x[:, 2 * D :] for x in packed]
    q_spread = [dot(rep, x[:, :D]).astype(BF16) * mask for x in packed]
    scores = [dot(k, q, NT) * (SCALE * LOG2E) + bias[...] for k, q, bias in zip(k_rows, q_spread, biases)]
    exp_scores = [jnp.exp2(x - jnp.max(x, 0, keepdims=True)) for x in scores]
    attn_probs = [x * (1.0 / jnp.sum(x, 0, keepdims=True)) for x in exp_scores]
    probs_low = [x.astype(BF16) for x in attn_probs]
    return list(zip(normed, inv_std, q_spread, k_rows, v_rows, attn_probs, probs_low))


def gathered(values, weights, rep, mask_t):
    spread = [dot(x, w, TN).astype(BF16) * mask_t for x, w in zip(values, weights)]
    return [dot(x, rep).T.astype(BF16) for x in spread]


def backward(saved, grads, gain, w_qkv_ref, w_proj, rep, mask, mask_t):
    normed, inv_std, q_spread, k_rows, v_rows, attn_probs, probs_low = zip(*saved)
    grad_mixed = [dot(x, w_proj, NT).astype(BF16) for x in grads]
    mixed_spread = [dot(rep, x).astype(BF16) * mask for x in grad_mixed]
    grad_probs = [dot(v, m, NT) for v, m in zip(v_rows, mixed_spread)]
    grad_v = [dot(p, m).astype(BF16) for p, m in zip(probs_low, mixed_spread)]
    lows = [
        ((p * (x - jnp.sum(x * p, 0, keepdims=True))) * SCALE).astype(BF16) for p, x in zip(attn_probs, grad_probs)
    ]
    grad_k = [dot(low, q).astype(BF16) for low, q in zip(lows, q_spread)]
    grad_q = gathered(k_rows, lows, rep, mask_t)
    w_q, w_k, w_v = w_qkv_ref[:, :D], w_qkv_ref[:, D : 2 * D], w_qkv_ref[:, 2 * D :]
    results = []
    for v, grad in enumerate(grads):
        grad_hidden = dot(grad_q[v], w_q, NT) + dot(grad_k[v], w_k, NT) + dot(grad_v[v], w_v, NT)
        grad_normed = grad_hidden * gain
        grad_local = inv_std[v] * (
            grad_normed
            - jnp.mean(grad_normed, -1, keepdims=True)
            - normed[v] * jnp.mean(grad_normed * normed[v], -1, keepdims=True)
        )
        results.append((grad.astype(F32) + grad_local).astype(BF16))
    return results, lows


def first_kernel(
    tokens_ref, grad_ref, flat_ref, gain_ref, w_qkv_ref, w_proj_ref, rep_ref, mask_ref, mask_t_ref, perm_ref, split_t_ref, turn_ref,
    stay_ref, lon_ref, lat_ref, both_ref, normed_ref, inv_ref, q_ref, k_ref, v_ref, probs_ref,
    part_a, part_b, part_c, spread_ref, bias_ref, left_ref, right_ref, piece_ref,
):
    turn = turn_ref[...]
    expand_table(flat_ref, perm_ref, (part_a, part_b, part_c), spread_ref)
    write_bias(spread_ref, bias_ref)
    inputs = [dot(turn, x) for x in load_windows(tokens_ref, left_ref, right_ref)]
    grads = [dot(turn, x).astype(BF16) for x in load_windows(grad_ref, left_ref, right_ref)]
    rep, mask, mask_t = rep_ref[...], mask_ref[...], mask_t_ref[...]
    saved = forward(inputs, [bias_ref.at[v] for v in LEVELS], gain_ref[...], w_qkv_ref[...], rep, mask)
    normed, inv_std, q_spread, k_rows, v_rows, attn_probs, probs_low = zip(*saved)
    attended = gathered(v_rows, probs_low, rep, mask_t)
    for v in LEVELS:
        normed_ref[v] = normed[v]
        inv_ref[v] = jnp.broadcast_to(inv_std[v], (WIN_TOK, FLAT))
        q_ref[v] = q_spread[v]
        k_ref[v] = k_rows[v]
        v_ref[v] = v_rows[v]
        probs_ref[v] = probs_low[v]
    split_t = split_t_ref[...]
    for v in LEVELS:
        block_out = (inputs[v] + dot(attended[v], w_proj_ref[...])).astype(BF16)
        piece_ref[:, v * PIECE : (v + 1) * PIECE, :D] = dot(split_t, block_out).reshape(4, PIECE, D)
        piece_ref[:, v * PIECE : (v + 1) * PIECE, D:] = dot(split_t, grads[v]).reshape(4, PIECE, D)
    for place, ref in enumerate((stay_ref, lon_ref, lat_ref, both_ref)):
        ref[...] = piece_ref[place].astype(BF16)


def bias_kernel(active_ref, flat_ref, perm_ref, bias_ref, part_a, part_b, part_c, spread_ref):
    expand_table(flat_ref, perm_ref, (part_a, part_b, part_c), spread_ref)
    blocked = active_ref[0, 0] * (-10000.0 * LOG2E)
    key_lat = lax.broadcasted_iota(jnp.int32, (WIN_TOK, SLAB), 0) % WIN_LAT
    query_lat = lax.broadcasted_iota(jnp.int32, (WIN_TOK, SLAB), 1) % WIN_LAT
    write_bias(spread_ref, bias_ref, jnp.where((key_lat < 3) != (query_lat < 3), blocked, 0.0))


def second_kernel(
    stay_ref, lon_ref, lat_ref, both_ref, bias_ref, gain_ref, w_qkv_ref, w_proj_ref, rep_ref, mask_ref, mask_t_ref, join_ref, join_t_ref,
    stay_out, lon_out, lat_out, both_out, low_ref,
    window_ref, piece_ref,
):
    rep, mask, mask_t = rep_ref[...], mask_ref[...], mask_t_ref[...]
    join, join_t = join_ref[...], join_t_ref[...]
    for place, ref in enumerate((stay_ref, lon_ref, lat_ref, both_ref)):
        wide = ref[...].astype(F32)
        for v in LEVELS:
            window_ref[v, place * PIECE : (place + 1) * PIECE, :] = wide[v * PIECE : (v + 1) * PIECE]
    pairs = [dot(join, window_ref[v].astype(BF16)) for v in LEVELS]
    inputs = [x[:, :D] for x in pairs]
    grads = [x[:, D:].astype(BF16) for x in pairs]
    gain, w_proj = gain_ref[...], w_proj_ref[...]
    saved = forward(inputs, [bias_ref.at[v] for v in LEVELS], gain, w_qkv_ref[...], rep, mask)
    results, lows = backward(saved, grads, gain, w_qkv_ref, w_proj, rep, mask, mask_t)
    for v in LEVELS:
        low_ref[v] = lows[v]
        row, lane = v % 2 * PIECE, v // 2 * D
        piece_ref[:, row : row + PIECE, lane : lane + D] = dot(join_t, results[v]).reshape(4, PIECE, D)
    for place, ref in enumerate((stay_out, lon_out, lat_out, both_out)):
        ref[...] = piece_ref[place].astype(BF16)


def fold_kernel(low_ref, perm_ref, pack_ref, folded_ref, table_ref):
    fold_scores([low_ref[v] for v in LEVELS], perm_ref, folded_ref, table_ref, pack_ref)


def third_kernel(
    stay_ref, lon_ref, lat_ref, both_ref, normed_ref, inv_ref, q_ref, k_ref, v_ref, probs_ref, other_ref,
    gain_ref, w_qkv_ref, w_proj_ref, rep_ref, mask_ref, mask_t_ref, perm_ref, split_ref, turn_t_ref,
    grid_ref, terms_ref,
    window_ref, left_ref, right_ref, folded_ref, table_ref, pack_ref,
):
    rep, mask, mask_t = rep_ref[...], mask_ref[...], mask_t_ref[...]
    split, turn_t = split_ref[...], turn_t_ref[...]
    for place, ref in enumerate((stay_ref, lon_ref, lat_ref, both_ref)):
        wide = ref[...].astype(F32)
        for v in LEVELS:
            row, lane = v % 2 * PIECE, v // 2 * D
            window_ref[v, place * PIECE : (place + 1) * PIECE, :] = wide[row : row + PIECE, lane : lane + D]
    grads = [dot(split, window_ref[v].astype(BF16)).astype(BF16) for v in LEVELS]
    saved = [
        (normed_ref[v], inv_ref[v][:, :1], q_ref[v], k_ref[v], v_ref[v], probs_ref[v].astype(F32), probs_ref[v])
        for v in LEVELS
    ]
    results, lows = backward(saved, grads, gain_ref[...], w_qkv_ref, w_proj_ref[...], rep, mask, mask_t)
    store_windows([dot(turn_t, x) for x in results], grid_ref, left_ref, right_ref)
    fold_scores(lows, perm_ref, folded_ref, table_ref, pack_ref)
    terms_ref[...] = jnp.concatenate([pack_ref[...], other_ref[...]], 1).astype(BF16)


def sum_kernel(arrived_ref, one_ref, two_ref, total_ref):
    total = arrived_ref[0].astype(F32)
    for tile in range(1, arrived_ref.shape[0]):
        total = total + arrived_ref[tile].astype(F32)
    total_ref[...] = total
    for base, out_ref in ((0, one_ref), (TERM, two_ref)):
        for row in range(SHARE):
            lane = ROWS * row
            out_ref[:, lane : lane + FLAT] = total_ref[base + row : base + row + 1, :]
            place = base + SHARE + row
            out_ref[:, lane + FLAT : lane + 2 * FLAT] = total_ref[place : place + 1, :]
            place, shift = base + 2 * SHARE + row % 4, row // 4 * REST
            out_ref[:, lane + 2 * FLAT : lane + ROWS] = total_ref[place : place + 1, shift : shift + REST]


def call(kernel, out_shapes, scratch, flops, scalars=0):
    return pl.pallas_call(
        kernel,
        out_shape=[jax.ShapeDtypeStruct(shape, dtype) for shape, dtype in out_shapes],
        scratch_shapes=[pltpu.VMEM(shape, F32) for shape in scratch],
        compiler_params=pltpu.CompilerParams(vmem_limit_bytes=VMEM_LIMIT),
        cost_estimate=pl.CostEstimate(flops=flops, bytes_accessed=4_000_000, transcendentals=500_000),
    )


VMEM_LIMIT = 40 * 1024 * 1024


def shifted(axes, by):
    sizes = [lax.axis_size(axis) for axis in axes]
    if len(sizes) == 1:
        return [(i, (i + by) % sizes[0]) for i in range(sizes[0])]
    rows, columns = sizes
    return [
        (a * columns + o, (a + by) % rows * columns + (o + by) % columns)
        for a in range(rows)
        for o in range(columns)
    ]


def exchange(pieces, by):
    stay, lon, lat, both = pieces
    return (
        stay,
        lax.ppermute(lon, ("lon",), shifted(("lon",), by)),
        lax.ppermute(lat, ("lat",), shifted(("lat",), by)),
        lax.ppermute(both, ("lat", "lon"), shifted(("lat", "lon"), by)),
    )


def body(
    tokens, grad_out, gain_one, qkv_one, proj_one, bias_one, gain_two, qkv_two, proj_two, bias_two
):
    const = {name: jnp.asarray(value) for name, value in CONST.items()}
    spread = (const["rep"], const["mask"], const["mask_t"])
    perm = const["perm"]
    flat = (LEV_WIN * SLAB * ROWS // FLAT, FLAT)
    block_one = (gain_one.reshape(1, D), qkv_one, proj_one) + spread
    block_two = (gain_two.reshape(1, D), qkv_two, proj_two) + spread
    columns = (WIN_LAT * WIN_LON, LEV, D)

    def level_last(grid):
        return grid.transpose(1, 2, 0, 3).reshape(columns)

    pair = ((LEV_WIN * PIECE, 2 * D), BF16)
    single = ((LEV_WIN * PIECE // 2, 2 * D), BF16)
    rows = (LEV_WIN, WIN_TOK, D)
    scores = (LEV_WIN, WIN_TOK, LANES)
    parts = [(LEV_WIN * SLAB, FLAT)] * 3
    folded = (ROWS, LEV_WIN * SLAB)
    grid = [(LEV * WIN_LAT * WIN_LON, FLAT)] * 2
    table = (LEV_WIN * SLAB, 3 * FLAT)
    tiles = LEV_WIN * SLAB // SHARE

    first = call(
        first_kernel,
        [pair] * 4
        + [(rows, F32), ((LEV_WIN, WIN_TOK, FLAT), F32), ((LEV_WIN, LANES, D), BF16), (rows, BF16), (rows, BF16), (scores, BF16)],
        parts + [folded, scores] + grid + [(4, LEV_WIN * PIECE, 2 * D)],
        2_000_000_000,
    )(level_last(tokens), level_last(grad_out), bias_one.reshape(flat), *block_one, perm, const["split_t"], const["turn"])
    pieces, saved = first[:4], first[4:]
    pieces, bias_two = lax.optimization_barrier((tuple(pieces), bias_two))
    pieces = exchange(pieces, -1)

    active = jnp.where(lax.axis_index("lat") == lax.axis_size("lat") - 1, 1.0, 0.0).astype(F32).reshape(1, 1)
    (bias_full,) = pl.pallas_call(
        bias_kernel,
        in_specs=[pl.BlockSpec(memory_space=pltpu.SMEM)] + [pl.BlockSpec(memory_space=pltpu.VMEM)] * 2,
        out_shape=[jax.ShapeDtypeStruct(scores, F32)],
        scratch_shapes=[pltpu.VMEM(shape, F32) for shape in parts + [folded]],
        compiler_params=pltpu.CompilerParams(vmem_limit_bytes=VMEM_LIMIT),
        cost_estimate=pl.CostEstimate(flops=500_000_000, bytes_accessed=4_000_000, transcendentals=0),
    )(active, bias_two.reshape(flat), perm)

    second = call(
        second_kernel,
        [single] * 4 + [(scores, BF16)],
        [(LEV_WIN, WIN_TOK, 2 * D), (4, LEV_WIN * PIECE // 2, 2 * D)],
        4_000_000_000,
    )(*pieces, bias_full, *block_two, const["join"], const["join_t"])
    grad_pieces, low_two = second[:4], second[4]
    grad_pieces = exchange(grad_pieces, 1)

    (term_two,) = call(fold_kernel, [((tiles, TERM, FLAT), F32)], [folded, table], 500_000_000)(low_two, perm)

    grid_out, terms = call(
        third_kernel,
        [(columns, BF16), ((tiles, 2 * TERM, FLAT), BF16)],
        [rows] + grid + [folded, table, (tiles, TERM, FLAT)],
        4_000_000_000,
    )(*grad_pieces, *saved, term_two, *block_one, perm, const["split"], const["turn_t"])
    grad_tokens = grid_out.reshape(WIN_LAT, WIN_LON, LEV, D).transpose(2, 0, 1, 3)

    arrived = lax.all_to_all(terms, "lon", 0, 0, tiled=True)
    width = SHARE * ROWS
    summed_one, summed_two = call(
        sum_kernel, [((1, width), F32), ((1, width), F32)], [(2 * TERM, FLAT)], 1_000_000
    )(arrived)
    return grad_tokens, summed_one, summed_two


def solution(mesh):
    in_specs = (
        P(None, "lat", "lon", None),
        P(None, "lat", "lon", None),
        P(),
        P(),
        P(),
        P("lat", None),
        P(),
        P(),
        P(),
        P("lat", None),
    )
    out_specs = (P(None, "lat", "lon", None), P("lat", "lon"), P("lat", "lon"))
    return jax.shard_map(body, mesh=mesh, in_specs=in_specs, out_specs=out_specs, check_vma=False)
```

time: 97 us -> 77.3 us (0.80)
  the two profiles are of different devices: /device:TPU:24 before, /device:TPU:2 now
where the time goes in v2:
time: 77.3 us; the launch traced here: 76.2 us
  Pallas kernels  21.9 us (28%)
  blocking collectives  17.5 us (23%)
  local copies, waits for them, and re-layouts  15.2 us (20%)
  starting transfers between devices  12 us (16%)
  waiting for transfers between devices  5.19 us (7%)
  other arithmetic  3.46 us (4%)
  between operations  0.99 us (1%)
    all_to_all x1, blocking collectives, body(): arrived = lax.all_to_all(terms, 'lon', 0, 0, tiled=True)  17.5 us
    unnamed x74, local copies, waits for them, and re-layouts  15.2 us
    pallas_call x1, Pallas kernels, body(): call(second_kernel, [single] * 4 + [(scores, BF16)], [(LEV_WIN, WIN_TOK,...  6.25 us
    ppermute x2, starting transfers between devices, exchange(): lax.ppermute(both, ('lat', 'lon'), shifted(('lat', 'lon'), by))  5.98 us
    pallas_call x1, Pallas kernels, body(): call(first_kernel, [pair] * 4 + [(rows, F32), ((LEV_WIN, WIN_TOK, FLAT),...  5.7 us
    pallas_call x1, Pallas kernels, body(): call(third_kernel, [(columns, BF16), ((tiles, 2 * TERM, FLAT), BF16)], [r...  5.49 us
    ppermute x2, starting transfers between devices, exchange(): lax.ppermute(lat, ('lat',), shifted(('lat',), by))  3.6 us
    ppermute x2, waiting for transfers between devices, exchange(): lax.ppermute(lat, ('lat',), shifted(('lat',), by))  2.92 us
  transfers between devices with their start and end apart: 6, of which 3 were waited for; matrix products, arithmetic and copies ran while one was open for 2% of the time, Pallas kernels for 5%

profile of v2, /device:TPU:2, one launch (start us, length us, event | category | flops | bytes accessed | tf_op | source)
XLA Modules:
  0.0 76.2 jit_solution(622622647141118343)
XLA Ops:
  0.6 1.7 %reduce = f32[79488]{0:T(1024)S(1)} reduce(f32[1,79488]{1,0:T(1,128)} %param.25, f32[]{:T(128)} %constant.42), dimensions={0}, to_apply=%param.25.reduce_sub_computation | reduce | bytes 635908 | tf_op args[5]
  2.4 0.0 copy-start
  2.4 0.9 %copy-done = bf16[276,384]{1,0:T(8,128)(2,1)S(1)} copy-done((bf16[276,384]{1,0:T(8,128)(2,1)S(1)}, bf16[276,384]{1,0:T(8,128)(2,1)}, u32[]{:S(2)}) %copy-start) | copy-done | bytes 211992
  3.3 1.0 %copy-done.2 = bf16[8,6,12,192]{3,0,2,1:T(8,128)(2,1)S(1)} copy-done((bf16[8,6,12,192]{3,0,2,1:T(8,128)(2,1)S(1)}, bf16[8,6,12,192]{3,0,2,1:T(8,128)(2,1)}, u32[]{:S(2)}) %copy-start.2) | copy-done | bytes 221208
  4.3 1.0 %copy-done.3 = bf16[8,6,12,192]{3,0,2,1:T(8,128)(2,1)S(1)} copy-done((bf16[8,6,12,192]{3,0,2,1:T(8,128)(2,1)S(1)}, bf16[8,6,12,192]{3,0,2,1:T(8,128)(2,1)}, u32[]{:S(2)}) %copy-start.3) | copy-done | bytes 221208
  5.2 0.9 %copy-done.5 = bf16[192,576]{1,0:T(8,128)(2,1)S(1)} copy-done((bf16[192,576]{1,0:T(8,128)(2,1)S(1)}, bf16[192,576]{1,0:T(8,128)(2,1)}, u32[]{:S(2)}) %copy-start.5) | copy-done | bytes 221208
  6.2 0.9 %copy-done.8 = bf16[192,192]{1,0:T(8,128)(2,1)S(1)} copy-done((bf16[192,192]{1,0:T(8,128)(2,1)S(1)}, bf16[192,192]{1,0:T(8,128)(2,1)}, u32[]{:S(2)}) %copy-start.8) | copy-done | bytes 73752
  7.1 0.7 copy-done.11
  7.7 1.0 %copy-done.13 = bf16[864,192]{1,0:T(8,128)(2,1)S(1)} copy-done((bf16[864,192]{1,0:T(8,128)(2,1)S(1)}, bf16[864,192]{1,0:T(8,128)(2,1)}, u32[]{:S(2)}) %copy-start.13) | copy-done | bytes 331800
  8.8 1.0 %copy-done.15 = bf16[864,144]{1,0:T(8,128)(2,1)S(1)} copy-done((bf16[864,144]{1,0:T(8,128)(2,1)S(1)}, bf16[864,144]{1,0:T(8,128)(2,1)}, u32[]{:S(2)}) %copy-start.15) | copy-done | bytes 248856
  9.8 1.0 %copy-done.17 = bf16[192,864]{1,0:T(8,128)(2,1)S(1)} copy-done((bf16[192,864]{1,0:T(8,128)(2,1)S(1)}, bf16[192,864]{1,0:T(8,128)(2,1)}, u32[]{:S(2)}) %copy-start.17) | copy-done | bytes 331800
  10.7 0.9 %copy-done.19 = bf16[144,144]{1,0:T(8,128)(2,1)S(1)} copy-done((bf16[144,144]{1,0:T(8,128)(2,1)S(1)}, bf16[144,144]{1,0:T(8,128)(2,1)}, u32[]{:S(2)}) %copy-start.19) | copy-done | bytes 41496
  11.6 0.9 %copy-done.24 = bf16[144,144]{1,0:T(8,128)(2,1)S(1)} copy-done((bf16[144,144]{1,0:T(8,128)(2,1)S(1)}, bf16[144,144]{1,0:T(8,128)(2,1)}, u32[]{:S(2)}) %copy-start.24) | copy-done | bytes 41496
  12.5 5.7 %shard_map.211 = (bf16[144,384]{1,0:T(8,128)(2,1)S(1)}, bf16[144,384]{1,0:T(8,128)(2,1)S(1)}, bf16[144,384]{1,0:T(8,128)(2,1)S(1)}, bf16[144,384]{1,0:T(8,128)(2...) custom-call(bf16[72,8,192]{2,1,0:T(8,128)(2,1)S(1)} %bitcast.16, ...), custom_call_target="tpu_custom_call" | custom-call | flops 2000000000 | bytes 4000000 | tf_op jit(solution)/shard_map/pallas_call | solution.py:359
  18.2 1.2 %copy-done.25 = bf16[4,864,192]{2,1,0:T(8,128)(2,1)} copy-done((bf16[4,864,192]{2,1,0:T(8,128)(2,1)}, bf16[4,864,192]{2,1,0:T(8,128)(2,1)S(1)}, u32[]{:S(2)}) %copy-start.25) | copy-done | bytes 1327128
  19.4 1.0 %copy-done.27 = bf16[4,144,864]{2,1,0:T(8,128)(2,1)} copy-done((bf16[4,144,864]{2,1,0:T(8,128)(2,1)}, bf16[4,144,864]{2,1,0:T(8,128)(2,1)S(1)}, u32[]{:S(2)}) %copy-start.27) | copy-done | bytes 995352
  20.4 0.7 copy-done.29
  21.1 0.7 copy-done.31
  21.8 0.7 copy-done.33
  22.5 0.7 copy-done.35
  23.2 0.0 copy-start.16
  23.2 0.0 copy-start.18
  23.2 0.0 copy-start.22
  23.2 0.0 copy-start.23
  23.3 2.4 %collective-permute-start = (bf16[144,384]{1,0:T(8,128)(2,1)S(1)}, bf16[144,384]{1,0:T(8,128)(2,1)S(1)}, u32[]{:S(2)}, u32[]{:S(2)}) collective-permute-start(bf16[144,384]{1,0:T(8,128)(2,1)S(1)} %get-tuple-element.32), channel_id=1, source_target_pairs={{0,15},{1,0},{2,1},{3,2},{4,3},{5,4},{6,5},{7,6},{8,7},{9,8},{10,9... | collective-permute-start | bytes 331784 | tf_op jit(solution)/shard_map/ppermute | solution.py:329
  25.6 2.3 %collective-permute-start.1 = (bf16[144,384]{1,0:T(8,128)(2,1)S(1)}, bf16[144,384]{1,0:T(8,128)(2,1)S(1)}, u32[]{:S(2)}, u32[]{:S(2)}) collective-permute-start(bf16[144,384]{1,0:T(8,128)(2,1)S(1)} %get-tuple-element.33), channel_id=1, source_target_pairs={{0,240},{16,0},{32,16},{48,32},{64,48},{80,64},{96,80},{112,96},{1... | collective-permute-start | bytes 331784 | tf_op jit(solution)/shard_map/ppermute | solution.py:330
  27.9 6.0 %collective-permute-start.2 = (bf16[144,384]{1,0:T(8,128)(2,1)S(1)}, bf16[144,384]{1,0:T(8,128)(2,1)S(1)}, u32[]{:S(2)}, u32[]{:S(2)}) collective-permute-start(bf16[144,384]{1,0:T(8,128)(2,1)S(1)} %get-tuple-element.34), channel_id=1, source_target_pairs={{0,255},{1,240},{2,241},{3,242},{4,243},{5,244},{6,245},{7,246},{8... | collective-permute-start | bytes 331784 | tf_op jit(solution)/shard_map/ppermute | solution.py:331
  33.9 1.7 %reduce.1 = f32[79488]{0:T(1024)S(1)} reduce(f32[1,79488]{1,0:T(1,128)} %param.29, f32[]{:T(128)} %constant.42), dimensions={0}, to_apply=%get-tuple-element.35.reduce_sub_computation | reduce | bytes 635908 | tf_op jit(solution)/shard_map/optimization_barrier | solution.py:367
  35.6 0.0 copy-start.36
  35.6 0.0 copy-done.1
  35.6 2.4 %shard_map.212.bias_ref = f32[4,144,864]{2,1,0:T(8,128)S(1)} custom-call(f32[1,1]{1,0:T(1,128)} %bitcast.5.active_ref, f32[621,128]{1,0:T(8,128)S(1)} %bitcast.14, bf16[276,384]{1,0:T(8,128)(2,1)S(1)} %copy-done.1), custom_call_target="tpu_custom_call" | custom-call | flops 500000000 | bytes 4000000 | tf_op jit(solution)/shard_map/pallas_call | solution.py:371
  38.0 0.0 collective-permute-done.lon_ref
  38.0 0.0 collective-permute-done.1.lat_ref
  38.0 0.0 collective-permute-done.2.both_ref
  38.0 0.0 copy-done.4
  38.1 0.0 copy-done.7
  38.1 0.0 copy-done.10
  38.1 0.0 copy-done.14
  38.1 0.0 copy-done.16
  38.1 0.0 copy-done.18
  38.1 0.0 copy-done.22
  38.1 0.0 copy-done.23
  38.1 0.0 copy-done.36
  38.1 0.0 copy-start.6
  38.1 0.0 copy-start.9
  38.2 0.0 copy-start.12
  38.2 0.0 copy-start.20
  38.2 0.0 copy-start.21
  38.2 0.0 copy-start.26
  38.2 0.0 copy-start.28
  38.2 0.0 copy-start.30
  38.2 6.2 %shard_map.213 = (bf16[72,384]{1,0:T(8,128)(2,1)S(1)}, bf16[72,384]{1,0:T(8,128)(2,1)S(1)}, bf16[72,384]{1,0:T(8,128)(2,1)S(1)}, bf16[72,384]{1,0:T(8,128)(2,1)S(1)}, bf16[4,144,864]{2,1,0:T(8,128)(2,1)S(1)}) custom-call(bf16[144,384]{1,0:T(8,128)(2,1)S(1)} %copy-done.36, bf16[144,384]{1,0:T(8,128)(2,1)S(1)} %collective-permute-done.lon_ref, ...), custom_call_target="tpu_custom_call" | custom-call | flops 4000000000 | bytes 4000000 | tf_op jit(solution)/shard_map/pallas_call | solution.py:380
  44.5 0.1 collective-permute-start.3
  44.6 1.3 %collective-permute-start.4 = (bf16[72,384]{1,0:T(8,128)(2,1)S(1)}, bf16[72,384]{1,0:T(8,128)(2,1)S(1)}, u32[]{:S(2)}, u32[]{:S(2)}) collective-permute-start(bf16[72,384]{1,0:T(8,128)(2,1)S(1)} %get-tuple-element.38), channel_id=1, source_target_pairs={{0,16},{16,32},{32,48},{48,64},{64,80},{80,96},{96,112},{112,128},... | collective-permute-start | bytes 165896 | tf_op jit(solution)/shard_map/ppermute | solution.py:330
  45.9 0.0 collective-permute-start.5
  45.9 1.2 %shard_map.214.other_ref = f32[16,40,128]{2,1,0:T(8,128)S(1)} custom-call(bf16[4,144,864]{2,1,0:T(8,128)(2,1)S(1)} %get-tuple-element.46.low_ref, bf16[276,384]{1,0:T(8,128)(2,1)S(1)} %copy-done.1), custom_call_target="tpu_custom_call" | custom-call | flops 500000000 | bytes 4000000 | tf_op jit(solution)/shard_map/pallas_call | solution.py:389
  47.2 1.9 %collective-permute-done.3.lon_ref = bf16[72,384]{1,0:T(8,128)(2,1)S(1)} collective-permute-done((bf16[72,384]{1,0:T(8,128)(2,1)S(1)}, bf16[72,384]{1,0:T(8,128)(2,1)S(1)}, u32[]{:S(2)}, u32[]{:S(2)}) %collective-permute-start.3) | collective-permute-done | bytes 55328 | tf_op jit(solution)/shard_map/ppermute | solution.py:329
  49.1 2.9 %collective-permute-done.4.lat_ref = bf16[72,384]{1,0:T(8,128)(2,1)S(1)} collective-permute-done((bf16[72,384]{1,0:T(8,128)(2,1)S(1)}, bf16[72,384]{1,0:T(8,128)(2,1)S(1)}, u32[]{:S(2)}, u32[]{:S(2)}) %collective-permute-start.4) | collective-permute-done | bytes 55328 | tf_op jit(solution)/shard_map/ppermute | solution.py:330
  52.0 0.3 collective-permute-done.5.both_ref
  52.3 0.0 copy-done.12
  52.3 0.0 copy-done.20
  52.4 5.5 %shard_map.215 = (bf16[72,8,192]{2,1,0:T(8,128)(2,1)}, bf16[16,80,128]{2,1,0:T(8,128)(2,1)S(1)}) custom-call(bf16[72,384]{1,0:T(8,128)(2,1)S(1)} %get-tuple-element.36.stay_ref, bf16[72,384]{1,0:T(8,128)(2,1)S(1)} %collective-permute-done.3.lon_ref, bf16[72,384]{1,0:T(8,128)(2,1)S(1)} %collective-permute-done.4.lat_ref, ...), custom_call_target="tpu_custom_call" | custom-call | flops 4000000000 | bytes 4000000 | tf_op jit(solution)/shard_map/pallas_call | solution.py:391
  57.9 17.5 %all_to_all.5.arrived_ref = bf16[16,80,128]{2,1,0:T(8,128)(2,1)S(1)} all-to-all(bf16[16,80,128]{2,1,0:T(8,128)(2,1)S(1)} %get-tuple-element.48), channel_id=1, replica_groups=mesh['lat'=16,'lon'=16] {'lon'}, dimensions={0} | all-to-all | bytes 655360 | tf_op jit(solution)/shard_map/all_to_all | solution.py:399
  75.4 0.8 %shard_map.216 = (f32[1,4968]{1,0:T(1,128)}, f32[1,4968]{1,0:T(1,128)}) custom-call(bf16[16,80,128]{2,1,0:T(8,128)(2,1)S(1)} %all_to_all.5.arrived_ref), custom_call_target="tpu_custom_call" | custom-call | flops 1000000 | bytes 4000000 | tf_op jit(solution)/shard_map/pallas_call | solution.py:401
  (31 shorter events, 0.1 us)
Async XLA Ops:
  2.4 0.9 %copy-start = (bf16[276,384]{1,0:T(8,128)(2,1)S(1)}, bf16[276,384]{1,0:T(8,128)(2,1)}, u32[]{:S(2)}) copy-start(bf16[276,384]{1,0:T(8,128)(2,1)} %constant.32.clone.perm_ref) | copy-start | bytes 635908
  3.3 1.0 %copy-start.2 = (bf16[8,6,12,192]{3,0,2,1:T(8,128)(2,1)S(1)}, bf16[8,6,12,192]{3,0,2,1:T(8,128)(2,1)}, u32[]{:S(2)}) copy-start(bf16[8,6,12,192]{3,0,2,1:T(8,128)(2,1)} %param.20) | copy-start | bytes 663556
  4.3 1.0 %copy-start.3 = (bf16[8,6,12,192]{3,0,2,1:T(8,128)(2,1)S(1)}, bf16[8,6,12,192]{3,0,2,1:T(8,128)(2,1)}, u32[]{:S(2)}) copy-start(bf16[8,6,12,192]{3,0,2,1:T(8,128)(2,1)} %param.21) | copy-start | bytes 663556
  5.2 0.9 %copy-start.5 = (bf16[192,576]{1,0:T(8,128)(2,1)S(1)}, bf16[192,576]{1,0:T(8,128)(2,1)}, u32[]{:S(2)}) copy-start(bf16[192,576]{1,0:T(8,128)(2,1)} %w_qkv_ref.5) | copy-start | bytes 663556
  6.2 0.9 %copy-start.8 = (bf16[192,192]{1,0:T(8,128)(2,1)S(1)}, bf16[192,192]{1,0:T(8,128)(2,1)}, u32[]{:S(2)}) copy-start(bf16[192,192]{1,0:T(8,128)(2,1)} %w_proj_ref.5) | copy-start | bytes 221188
  7.1 0.7 copy-start.11
  7.7 1.0 %copy-start.13 = (bf16[864,192]{1,0:T(8,128)(2,1)S(1)}, bf16[864,192]{1,0:T(8,128)(2,1)}, u32[]{:S(2)}) copy-start(bf16[864,192]{1,0:T(8,128)(2,1)} %constant.30.clone.mask_ref) | copy-start | bytes 995332
  8.8 1.0 %copy-start.15 = (bf16[864,144]{1,0:T(8,128)(2,1)S(1)}, bf16[864,144]{1,0:T(8,128)(2,1)}, u32[]{:S(2)}) copy-start(bf16[864,144]{1,0:T(8,128)(2,1)} %constant.29.clone.rep_ref) | copy-start | bytes 746500
  9.8 1.0 %copy-start.17 = (bf16[192,864]{1,0:T(8,128)(2,1)S(1)}, bf16[192,864]{1,0:T(8,128)(2,1)}, u32[]{:S(2)}) copy-start(bf16[192,864]{1,0:T(8,128)(2,1)} %constant.31.clone.mask_t_ref) | copy-start | bytes 995332
  10.7 0.9 %copy-start.19 = (bf16[144,144]{1,0:T(8,128)(2,1)S(1)}, bf16[144,144]{1,0:T(8,128)(2,1)}, u32[]{:S(2)}) copy-start(bf16[144,144]{1,0:T(8,128)(2,1)} %constant.37.clone.turn_ref.turn_t_ref) | copy-start | bytes 124420
  11.6 0.9 %copy-start.24 = (bf16[144,144]{1,0:T(8,128)(2,1)S(1)}, bf16[144,144]{1,0:T(8,128)(2,1)}, u32[]{:S(2)}) copy-start(bf16[144,144]{1,0:T(8,128)(2,1)} %constant.34.clone.split_t_ref) | copy-start | bytes 124420
  12.5 23.1 %copy-start.1 = (bf16[276,384]{1,0:T(8,128)(2,1)S(1)}, bf16[276,384]{1,0:T(8,128)(2,1)}, u32[]{:S(2)}) copy-start(bf16[276,384]{1,0:T(8,128)(2,1)} %constant.32.clone.perm_ref) | copy-start | bytes 635908
  18.2 1.2 %copy-start.25 = (bf16[4,864,192]{2,1,0:T(8,128)(2,1)}, bf16[4,864,192]{2,1,0:T(8,128)(2,1)S(1)}, u32[]{:S(2)}) copy-start(bf16[4,864,192]{2,1,0:T(8,128)(2,1)S(1)} %get-tuple-element.42.q_ref) | copy-start | bytes 3981316
  19.4 1.0 %copy-start.27 = (bf16[4,144,864]{2,1,0:T(8,128)(2,1)}, bf16[4,144,864]{2,1,0:T(8,128)(2,1)S(1)}, u32[]{:S(2)}) copy-start(bf16[4,144,864]{2,1,0:T(8,128)(2,1)S(1)} %get-tuple-element.45.probs_ref) | copy-start | bytes 2985988
  20.4 0.7 copy-start.29
  21.1 0.7 copy-start.31
  21.8 0.7 copy-start.33
  22.5 0.7 copy-start.35
  23.2 14.8 %copy-start.4 = (bf16[192,576]{1,0:T(8,128)(2,1)S(1)}, bf16[192,576]{1,0:T(8,128)(2,1)}, u32[]{:S(2)}) copy-start(bf16[192,576]{1,0:T(8,128)(2,1)} %w_qkv_ref.4) | copy-start | bytes 663556
  23.2 14.9 %copy-start.7 = (bf16[192,192]{1,0:T(8,128)(2,1)S(1)}, bf16[192,192]{1,0:T(8,128)(2,1)}, u32[]{:S(2)}) copy-start(bf16[192,192]{1,0:T(8,128)(2,1)} %w_proj_ref.4) | copy-start | bytes 221188
  23.2 14.9 %copy-start.10 = (f32[192]{0:T(256)S(1)}, f32[192]{0:T(256)}, u32[]{:S(2)}) copy-start(f32[192]{0:T(256)} %param.26) | copy-start | bytes 2308
  23.2 14.9 %copy-start.14 = (bf16[864,192]{1,0:T(8,128)(2,1)S(1)}, bf16[864,192]{1,0:T(8,128)(2,1)}, u32[]{:S(2)}) copy-start(bf16[864,192]{1,0:T(8,128)(2,1)} %constant.30.clone.mask_ref) | copy-start | bytes 995332
  23.2 14.9 %copy-start.16 = (bf16[864,144]{1,0:T(8,128)(2,1)S(1)}, bf16[864,144]{1,0:T(8,128)(2,1)}, u32[]{:S(2)}) copy-start(bf16[864,144]{1,0:T(8,128)(2,1)} %constant.29.clone.rep_ref) | copy-start | bytes 746500
  23.2 14.9 %copy-start.18 = (bf16[192,864]{1,0:T(8,128)(2,1)S(1)}, bf16[192,864]{1,0:T(8,128)(2,1)}, u32[]{:S(2)}) copy-start(bf16[192,864]{1,0:T(8,128)(2,1)} %constant.31.clone.mask_t_ref) | copy-start | bytes 995332
  23.2 14.9 %copy-start.22 = (bf16[144,144]{1,0:T(8,128)(2,1)S(1)}, bf16[144,144]{1,0:T(8,128)(2,1)}, u32[]{:S(2)}) copy-start(bf16[144,144]{1,0:T(8,128)(2,1)} %constant.36.clone.join_t_ref) | copy-start | bytes 124420
  23.2 14.9 %copy-start.23 = (bf16[144,144]{1,0:T(8,128)(2,1)S(1)}, bf16[144,144]{1,0:T(8,128)(2,1)}, u32[]{:S(2)}) copy-start(bf16[144,144]{1,0:T(8,128)(2,1)} %constant.35.clone.join_ref) | copy-start | bytes 124420
  23.3 14.8 %collective-permute-start = (bf16[144,384]{1,0:T(8,128)(2,1)S(1)}, bf16[144,384]{1,0:T(8,128)(2,1)S(1)}, u32[]{:S(2)}, u32[]{:S(2)}) collective-permute-start(bf16[144,384]{1,0:T(8,128)(2,1)S(1)} %get-tuple-element.32), channel_id=1, source_target_pairs={{0,15},{1,0},{2,1},{3,2},{4,3},{5,4},{6,5},{7,6},{8,7},{9,8},{10,9... | collective-permute-start | bytes 331784 | tf_op jit(solution)/shard_map/ppermute | solution.py:329
  25.6 12.4 %collective-permute-start.1 = (bf16[144,384]{1,0:T(8,128)(2,1)S(1)}, bf16[144,384]{1,0:T(8,128)(2,1)S(1)}, u32[]{:S(2)}, u32[]{:S(2)}) collective-permute-start(bf16[144,384]{1,0:T(8,128)(2,1)S(1)} %get-tuple-element.33), channel_id=1, source_target_pairs={{0,240},{16,0},{32,16},{48,32},{64,48},{80,64},{96,80},{112,96},{1... | collective-permute-start | bytes 331784 | tf_op jit(solution)/shard_map/ppermute | solution.py:330
  27.9 10.1 %collective-permute-start.2 = (bf16[144,384]{1,0:T(8,128)(2,1)S(1)}, bf16[144,384]{1,0:T(8,128)(2,1)S(1)}, u32[]{:S(2)}, u32[]{:S(2)}) collective-permute-start(bf16[144,384]{1,0:T(8,128)(2,1)S(1)} %get-tuple-element.34), channel_id=1, source_target_pairs={{0,255},{1,240},{2,241},{3,242},{4,243},{5,244},{6,245},{7,246},{8... | collective-permute-start | bytes 331784 | tf_op jit(solution)/shard_map/ppermute | solution.py:331
  35.6 2.5 %copy-start.36 = (bf16[144,384]{1,0:T(8,128)(2,1)S(1)}, bf16[144,384]{1,0:T(8,128)(2,1)}, u32[]{:S(2)}) copy-start(bf16[144,384]{1,0:T(8,128)(2,1)} %copy-done.35) | copy-start | bytes 331780
  38.1 14.2 %copy-start.6 = (bf16[192,576]{1,0:T(8,128)(2,1)S(1)}, bf16[192,576]{1,0:T(8,128)(2,1)}, u32[]{:S(2)}) copy-start(bf16[192,576]{1,0:T(8,128)(2,1)} %w_qkv_ref.5) | copy-start | bytes 663556
  38.1 14.2 %copy-start.9 = (bf16[192,192]{1,0:T(8,128)(2,1)S(1)}, bf16[192,192]{1,0:T(8,128)(2,1)}, u32[]{:S(2)}) copy-start(bf16[192,192]{1,0:T(8,128)(2,1)} %w_proj_ref.5) | copy-start | bytes 221188
  38.2 14.2 %copy-start.12 = (f32[192]{0:T(256)S(1)}, f32[192]{0:T(256)}, u32[]{:S(2)}) copy-start(f32[192]{0:T(256)} %param.22) | copy-start | bytes 2308
  38.2 14.2 %copy-start.20 = (bf16[144,144]{1,0:T(8,128)(2,1)S(1)}, bf16[144,144]{1,0:T(8,128)(2,1)}, u32[]{:S(2)}) copy-start(bf16[144,144]{1,0:T(8,128)(2,1)} %constant.37.clone.turn_ref.turn_t_ref) | copy-start | bytes 124420
  38.2 14.2 %copy-start.21 = (bf16[144,144]{1,0:T(8,128)(2,1)S(1)}, bf16[144,144]{1,0:T(8,128)(2,1)}, u32[]{:S(2)}) copy-start(bf16[144,144]{1,0:T(8,128)(2,1)} %constant.33.clone.split_ref) | copy-start | bytes 124420
  38.2 14.2 %copy-start.26 = (bf16[4,864,192]{2,1,0:T(8,128)(2,1)S(1)}, bf16[4,864,192]{2,1,0:T(8,128)(2,1)}, u32[]{:S(2)}) copy-start(bf16[4,864,192]{2,1,0:T(8,128)(2,1)} %copy-done.25) | copy-start | bytes 3981316
  38.2 14.2 %copy-start.28 = (bf16[4,144,864]{2,1,0:T(8,128)(2,1)S(1)}, bf16[4,144,864]{2,1,0:T(8,128)(2,1)}, u32[]{:S(2)}) copy-start(bf16[4,144,864]{2,1,0:T(8,128)(2,1)} %copy-done.27) | copy-start | bytes 2985988
  38.2 14.2 %copy-start.30 = (f32[4,144,128]{2,1,0:T(8,128)S(1)}, f32[4,144,128]{2,1,0:T(8,128)}, u32[]{:S(2)}) copy-start(f32[4,144,128]{2,1,0:T(8,128)} %copy-done.29) | copy-start | bytes 884740
  38.2 14.2 %copy-start.32 = (bf16[4,144,192]{2,1,0:T(8,128)(2,1)S(1)}, bf16[4,144,192]{2,1,0:T(8,128)(2,1)}, u32[]{:S(2)}) copy-start(bf16[4,144,192]{2,1,0:T(8,128)(2,1)} %copy-done.31) | copy-start | bytes 663556
  38.2 14.2 %copy-start.34 = (bf16[4,144,192]{2,1,0:T(8,128)(2,1)S(1)}, bf16[4,144,192]{2,1,0:T(8,128)(2,1)}, u32[]{:S(2)}) copy-start(bf16[4,144,192]{2,1,0:T(8,128)(2,1)} %copy-done.33) | copy-start | bytes 663556
  44.5 4.6 %collective-permute-start.3 = (bf16[72,384]{1,0:T(8,128)(2,1)S(1)}, bf16[72,384]{1,0:T(8,128)(2,1)S(1)}, u32[]{:S(2)}, u32[]{:S(2)}) collective-permute-start(bf16[72,384]{1,0:T(8,128)(2,1)S(1)} %get-tuple-element.37), channel_id=1, source_target_pairs={{0,1},{1,2},{2,3},{3,4},{4,5},{5,6},{6,7},{7,8},{8,9},{9,10},{10,1... | collective-permute-start | bytes 165896 | tf_op jit(solution)/shard_map/ppermute | solution.py:329
  44.6 7.4 %collective-permute-start.4 = (bf16[72,384]{1,0:T(8,128)(2,1)S(1)}, bf16[72,384]{1,0:T(8,128)(2,1)S(1)}, u32[]{:S(2)}, u32[]{:S(2)}) collective-permute-start(bf16[72,384]{1,0:T(8,128)(2,1)S(1)} %get-tuple-element.38), channel_id=1, source_target_pairs={{0,16},{16,32},{32,48},{48,64},{64,80},{80,96},{96,112},{112,128},... | collective-permute-start | bytes 165896 | tf_op jit(solution)/shard_map/ppermute | solution.py:330
  45.9 6.4 %collective-permute-start.5 = (bf16[72,384]{1,0:T(8,128)(2,1)S(1)}, bf16[72,384]{1,0:T(8,128)(2,1)S(1)}, u32[]{:S(2)}, u32[]{:S(2)}) collective-permute-start(bf16[72,384]{1,0:T(8,128)(2,1)S(1)} %get-tuple-element.39), channel_id=1, source_target_pairs={{0,17},{1,18},{2,19},{3,20},{4,21},{5,22},{6,23},{7,24},{8,25},{9,... | collective-permute-start | bytes 165896 | tf_op jit(solution)/shard_map/ppermute | solution.py:331

commit v3 on v2

--- a/solution.py
+++ b/solution.py
@@ -24,6 +24,7 @@
 LANES = WIN_LON * SLAB
 PIECE = 36
 FLAT = 128
+PERIOD = 32 * ROWS
 TERM = 40
 SHARE = 18
 REST = ROWS - 2 * FLAT
@@ -67,19 +68,20 @@
 TN = ((0,), (0,))
 
 
-def expand_table(flat_ref, perm_ref, parts, spread_ref):
-    lane = lax.broadcasted_iota(jnp.int32, (9, FLAT), 1)
+def table_copies(flat_ref, rows_ref, sem):
+    return [
+        pltpu.make_async_copy(flat_ref.at[:, pl.ds(PERIOD * k, PERIOD)], rows_ref.at[pl.ds(k, 1), :], sem.at[k])
+        for k in range(9)
+    ]
+
+
+def expand_table(rows_ref, perm_ref, parts, spread_ref):
     for first in range(32):
-        base, off = ROWS * first // FLAT, ROWS * first % FLAT
-        count = -(-(off + ROWS) // FLAT)
-        rows = [flat_ref[pl.ds(base + k, 9, stride=69), :] for k in range(count)]
-        if off:
-            rows = [pltpu.roll(row, FLAT - off, 1) for row in rows]
-        for place, part in enumerate(parts):
-            value = rows[place]
-            if off and place + 1 < count:
-                value = jnp.where(lane < FLAT - off, value, rows[place + 1])
-            part[pl.ds(first, 9, stride=32), :] = value
+        value = rows_ref[:, ROWS * first : ROWS * (first + 1)]
+        parts[0][pl.ds(first, 9, stride=32), :] = value[:, :FLAT]
+        parts[1][pl.ds(first, 9, stride=32), :] = value[:, FLAT : 2 * FLAT]
+        last = jnp.concatenate([value[:, 2 * FLAT :], jnp.zeros((9, 3 * FLAT - ROWS), F32)], 1)
+        parts[2][pl.ds(first, 9, stride=32), :] = last
     table = jnp.concatenate([part[...] for part in parts], 1)
     high = table.astype(BF16)
     rest = table - high.astype(F32)
@@ -192,19 +194,35 @@
 
 
 def first_kernel(
-    tokens_ref, grad_ref, flat_ref, gain_ref, w_qkv_ref, w_proj_ref, rep_ref, mask_ref, mask_t_ref, perm_ref, split_t_ref, turn_ref,
-    stay_ref, lon_ref, lat_ref, both_ref, normed_ref, inv_ref, q_ref, k_ref, v_ref, probs_ref,
-    part_a, part_b, part_c, spread_ref, bias_ref, left_ref, right_ref, piece_ref,
+    tokens_hbm, grad_hbm, flat_hbm, gain_hbm, w_qkv_hbm, w_proj_hbm, rep_hbm, mask_hbm, mask_t_hbm, perm_hbm, split_t_hbm, turn_hbm,
+    stay_hbm, lon_ref, lat_ref, both_ref, normed_hbm, inv_hbm, q_hbm, k_hbm, v_hbm, probs_hbm,
+    part_a, part_b, part_c, spread_ref, bias_ref, left_ref, right_ref, piece_ref, rows_ref, normed_ref, inv_ref,
+    tokens_ref, grad_ref, w_qkv_ref, w_proj_ref, rep_ref, mask_ref, mask_t_ref, perm_ref, split_t_ref, turn_ref,
+    stay_ref, q_ref, k_ref, v_ref, probs_ref, gain_ref,
+    table_sem, in_sem, out_sem,
 ):
+    table = table_copies(flat_hbm, rows_ref, table_sem)
+    pairs = (
+        (perm_hbm, perm_ref), (tokens_hbm, tokens_ref), (turn_hbm, turn_ref), (gain_hbm, gain_ref), (w_qkv_hbm, w_qkv_ref),
+        (rep_hbm, rep_ref), (mask_hbm, mask_ref), (grad_hbm, grad_ref), (mask_t_hbm, mask_t_ref), (w_proj_hbm, w_proj_ref),
+        (split_t_hbm, split_t_ref),
+    )
+    fetch = [pltpu.make_async_copy(src, dst, in_sem.at[k]) for k, (src, dst) in enumerate(pairs)]
+    for copy in table + fetch:
+        copy.start()
+    for copy in fetch[1:5]:
+        copy.wait()
     turn = turn_ref[...]
-    expand_table(flat_ref, perm_ref, (part_a, part_b, part_c), spread_ref)
+    inputs = [dot(turn, x) for x in load_windows(tokens_ref, left_ref, right_ref)]
+    for copy in table + fetch[:1]:
+        copy.wait()
+    expand_table(rows_ref, perm_ref, (part_a, part_b, part_c), spread_ref)
     write_bias(spread_ref, bias_ref)
-    inputs = [dot(turn, x) for x in load_windows(tokens_ref, left_ref, right_ref)]
-    grads = [dot(turn, x).astype(BF16) for x in load_windows(grad_ref, left_ref, right_ref)]
+    for copy in fetch[5:]:
+        copy.wait()
     rep, mask, mask_t = rep_ref[...], mask_ref[...], mask_t_ref[...]
     saved = forward(inputs, [bias_ref.at[v] for v in LEVELS], gain_ref[...], w_qkv_ref[...], rep, mask)
     normed, inv_std, q_spread, k_rows, v_rows, attn_probs, probs_low = zip(*saved)
-    attended = gathered(v_rows, probs_low, rep, mask_t)
     for v in LEVELS:
         normed_ref[v] = normed[v]
         inv_ref[v] = jnp.broadcast_to(inv_std[v], (WIN_TOK, FLAT))
@@ -212,17 +230,33 @@
         k_ref[v] = k_rows[v]
         v_ref[v] = v_rows[v]
         probs_ref[v] = probs_low[v]
+    pairs = ((normed_ref, normed_hbm), (inv_ref, inv_hbm), (q_ref, q_hbm), (k_ref, k_hbm), (v_ref, v_hbm), (probs_ref, probs_hbm))
+    keep = [pltpu.make_async_copy(src, dst, out_sem.at[k]) for k, (src, dst) in enumerate(pairs)]
+    for copy in keep:
+        copy.start()
+    attended = gathered(v_rows, probs_low, rep, mask_t)
+    grads = [dot(turn, x).astype(BF16) for x in load_windows(grad_ref, left_ref, right_ref)]
     split_t = split_t_ref[...]
     for v in LEVELS:
         block_out = (inputs[v] + dot(attended[v], w_proj_ref[...])).astype(BF16)
         piece_ref[:, v * PIECE : (v + 1) * PIECE, :D] = dot(split_t, block_out).reshape(4, PIECE, D)
         piece_ref[:, v * PIECE : (v + 1) * PIECE, D:] = dot(split_t, grads[v]).reshape(4, PIECE, D)
-    for place, ref in enumerate((stay_ref, lon_ref, lat_ref, both_ref)):
+    stay_ref[...] = piece_ref[0].astype(BF16)
+    stay = pltpu.make_async_copy(stay_ref, stay_hbm, out_sem.at[6])
+    stay.start()
+    for place, ref in ((1, lon_ref), (2, lat_ref), (3, both_ref)):
         ref[...] = piece_ref[place].astype(BF16)
-
-
-def bias_kernel(active_ref, flat_ref, perm_ref, bias_ref, part_a, part_b, part_c, spread_ref):
-    expand_table(flat_ref, perm_ref, (part_a, part_b, part_c), spread_ref)
+    for copy in keep + [stay]:
+        copy.wait()
+
+
+def bias_kernel(active_ref, flat_hbm, perm_ref, bias_ref, part_a, part_b, part_c, spread_ref, rows_ref, sem):
+    table = table_copies(flat_hbm, rows_ref, sem)
+    for copy in table:
+        copy.start()
+    for copy in table:
+        copy.wait()
+    expand_table(rows_ref, perm_ref, (part_a, part_b, part_c), spread_ref)
     blocked = active_ref[0, 0] * (-10000.0 * LOG2E)
     key_lat = lax.broadcasted_iota(jnp.int32, (WIN_TOK, SLAB), 0) % WIN_LAT
     query_lat = lax.broadcasted_iota(jnp.int32, (WIN_TOK, SLAB), 1) % WIN_LAT
@@ -307,7 +341,10 @@
     )
 
 
+ALL_VMEM = 62 * 1024 * 1024
 VMEM_LIMIT = 40 * 1024 * 1024
+HBM = pl.BlockSpec(memory_space=pltpu.HBM)
+VMEM = pl.BlockSpec(memory_space=pltpu.VMEM)
 
 
 def shifted(axes, by):
@@ -338,7 +375,6 @@
     const = {name: jnp.asarray(value) for name, value in CONST.items()}
     spread = (const["rep"], const["mask"], const["mask_t"])
     perm = const["perm"]
-    flat = (LEV_WIN * SLAB * ROWS // FLAT, FLAT)
     block_one = (gain_one.reshape(1, D), qkv_one, proj_one) + spread
     block_two = (gain_two.reshape(1, D), qkv_two, proj_two) + spread
     columns = (WIN_LAT * WIN_LON, LEV, D)
@@ -356,13 +392,34 @@
     table = (LEV_WIN * SLAB, 3 * FLAT)
     tiles = LEV_WIN * SLAB // SHARE
 
-    first = call(
+    outs = (
+        [pair] * 4
+        + [(rows, F32), ((LEV_WIN, WIN_TOK, FLAT), F32), ((LEV_WIN, LANES, D), BF16), (rows, BF16), (rows, BF16), (scores, BF16)]
+    )
+    table_rows = (9, PERIOD)
+    operands = (
+        level_last(tokens), level_last(grad_out), bias_one, *block_one, perm, const["split_t"], const["turn"]
+    )
+    held = [0, 1, 4, 5, 6, 7, 8, 9, 10, 11]
+    first = pl.pallas_call(
         first_kernel,
-        [pair] * 4
-        + [(rows, F32), ((LEV_WIN, WIN_TOK, FLAT), F32), ((LEV_WIN, LANES, D), BF16), (rows, BF16), (rows, BF16), (scores, BF16)],
-        parts + [folded, scores] + grid + [(4, LEV_WIN * PIECE, 2 * D)],
-        2_000_000_000,
-    )(level_last(tokens), level_last(grad_out), bias_one.reshape(flat), *block_one, perm, const["split_t"], const["turn"])
+        in_specs=[HBM] * len(operands),
+        out_specs=[HBM] + [VMEM] * 3 + [HBM] * 6,
+        out_shape=[jax.ShapeDtypeStruct(shape, dtype) for shape, dtype in outs],
+        scratch_shapes=[
+            pltpu.VMEM(shape, F32)
+            for shape in parts
+            + [folded, scores]
+            + grid
+            + [(4, LEV_WIN * PIECE, 2 * D), table_rows, rows, (LEV_WIN, WIN_TOK, FLAT)]
+        ]
+        + [pltpu.VMEM(operands[k].shape, BF16) for k in held]
+        + [pltpu.VMEM(shape, BF16) for shape, _ in [outs[0]] + outs[6:]]
+        + [pltpu.VMEM((1, D), F32)]
+        + [pltpu.SemaphoreType.DMA((9,)), pltpu.SemaphoreType.DMA((11,)), pltpu.SemaphoreType.DMA((7,))],
+        compiler_params=pltpu.CompilerParams(vmem_limit_bytes=ALL_VMEM),
+        cost_estimate=pl.CostEstimate(flops=2_000_000_000, bytes_accessed=4_000_000, transcendentals=500_000),
+    )(*operands)
     pieces, saved = first[:4], first[4:]
     pieces, bias_two = lax.optimization_barrier((tuple(pieces), bias_two))
     pieces = exchange(pieces, -1)
@@ -370,12 +427,12 @@
     active = jnp.where(lax.axis_index("lat") == lax.axis_size("lat") - 1, 1.0, 0.0).astype(F32).reshape(1, 1)
     (bias_full,) = pl.pallas_call(
         bias_kernel,
-        in_specs=[pl.BlockSpec(memory_space=pltpu.SMEM)] + [pl.BlockSpec(memory_space=pltpu.VMEM)] * 2,
+        in_specs=[pl.BlockSpec(memory_space=pltpu.SMEM), HBM, VMEM],
         out_shape=[jax.ShapeDtypeStruct(scores, F32)],
-        scratch_shapes=[pltpu.VMEM(shape, F32) for shape in parts + [folded]],
+        scratch_shapes=[pltpu.VMEM(shape, F32) for shape in parts + [folded, table_rows]] + [pltpu.SemaphoreType.DMA((9,))],
         compiler_params=pltpu.CompilerParams(vmem_limit_bytes=VMEM_LIMIT),
         cost_estimate=pl.CostEstimate(flops=500_000_000, bytes_accessed=4_000_000, transcendentals=0),
-    )(active, bias_two.reshape(flat), perm)
+    )(active, bias_two, perm)
 
     second = call(
         second_kernel,

time: 77.3 us -> 64 us (0.83)
  local copies, waits for them, and re-layouts: 15.2 us -> 0.13 us
  Pallas kernels: 21.9 us -> 25.9 us
  other arithmetic: 3.46 us -> 0 us
  waiting for transfers between devices: 5.19 us -> 7.17 us
  starting transfers between devices: 12 us -> 11.1 us
    unnamed x74 -> x44, local copies, waits for them, and re-layouts: 15.2 us -> 0.13 us
    pallas_call x1, Pallas kernels: 5.7 us -> 9.24 us  [body(): pl.pallas_call(first_kernel, in_specs=[HBM] * len(operands), out_specs=[H...]
    unnamed x1 -> x0, other arithmetic: 1.73 us -> none
    optimization_barrier x1 -> x0, other arithmetic: 1.73 us -> none  [body(): pieces, bias_two = lax.optimization_barrier((tuple(pieces), bias_two))]
    ppermute x2, starting transfers between devices: 3.6 us -> 2.55 us  [exchange(): lax.ppermute(lat, ('lat',), shifted(('lat',), by))]
    ppermute x2, waiting for transfers between devices: 0.35 us -> 1.35 us  [exchange(): lax.ppermute(both, ('lat', 'lon'), shifted(('lat', 'lon'), by))]
    ppermute x2, waiting for transfers between devices: 1.92 us -> 2.89 us  [exchange(): lax.ppermute(lon, ('lon',), shifted(('lon',), by))]
  transfers between devices with their start and end apart: 6 -> 6, of which waited for: 3 -> 4; matrix products, arithmetic and copies ran while one was open for 2% -> 0% of each run, Pallas kernels for 5% -> 6%
where the time goes in v3:
time: 64 us; the launch traced here: 63.3 us
  Pallas kernels  25.9 us (40%)
  blocking collectives  18 us (28%)
  starting transfers between devices  11.1 us (17%)
  waiting for transfers between devices  7.17 us (11%)
  between operations  0.98 us (2%)
    all_to_all x1, blocking collectives, body(): arrived = lax.all_to_all(terms, 'lon', 0, 0, tiled=True)  18 us
    pallas_call x1, Pallas kernels, body(): pl.pallas_call(first_kernel, in_specs=[HBM] * len(operands), out_specs=[H...  9.24 us
    pallas_call x1, Pallas kernels, body(): call(second_kernel, [single] * 4 + [(scores, BF16)], [(LEV_WIN, WIN_TOK,...  6.34 us
    ppermute x2, starting transfers between devices, exchange(): lax.ppermute(both, ('lat', 'lon'), shifted(('lat', 'lon'), by))  6.12 us
    pallas_call x1, Pallas kernels, body(): call(third_kernel, [(columns, BF16), ((tiles, 2 * TERM, FLAT), BF16)], [r...  5.57 us
    ppermute x2, waiting for transfers between devices, exchange(): lax.ppermute(lat, ('lat',), shifted(('lat',), by))  2.93 us
    ppermute x2, waiting for transfers between devices, exchange(): lax.ppermute(lon, ('lon',), shifted(('lon',), by))  2.89 us
    pallas_call x1, Pallas kernels, body(): pl.pallas_call(bias_kernel, in_specs=[pl.BlockSpec(memory_space=pltpu.SME...  2.69 us
  transfers between devices with their start and end apart: 6, of which 4 were waited for; matrix products, arithmetic and copies ran while one was open for 0% of the time, Pallas kernels for 6%

profile of v3, /device:TPU:2, one launch (start us, length us, event | category | flops | bytes accessed | tf_op | source)
XLA Modules:
  0.0 63.3 jit_solution(10987141631823675274)
XLA Ops:
  0.6 0.0 copy-start
  0.6 0.0 copy-start.1
  0.7 9.2 %shard_map.211 = (bf16[144,384]{1,0:T(8,128)(2,1)}, bf16[144,384]{1,0:T(8,128)(2,1)}, bf16[144,384]{1,0:T(8,128)(2,1)}, bf16[144,384]{1,0:T(8,128)(2,1)}, f32[4,...) custom-call(bf16[72,8,192]{2,1,0:T(8,128)(2,1)} %bitcast.15, ...), custom_call_target="tpu_custom_call" | custom-call | flops 2000000000 | bytes 4000000 | tf_op jit(solution)/shard_map/pallas_call | solution.py:404
  9.9 0.0 copy-start.2
  9.9 0.0 copy-start.4
  9.9 0.0 copy-start.6
  9.9 0.0 copy-start.8
  10.0 0.0 copy-start.9
  10.0 0.0 copy-start.10
  10.0 0.0 copy-start.13
  10.0 0.0 copy-start.14
  10.0 0.0 copy-start.21
  10.0 2.3 %collective-permute-start = (bf16[144,384]{1,0:T(8,128)(2,1)}, bf16[144,384]{1,0:T(8,128)(2,1)S(1)}, u32[]{:S(2)}, u32[]{:S(2)}) collective-permute-start(bf16[144,384]{1,0:T(8,128)(2,1)} %get-tuple-element.32), channel_id=1, source_target_pairs={{0,15},{1,0},{2,1},{3,2},{4,3},{5,4},{6,5},{7,6},{8,7},{9,8},{10,9... | collective-permute-start | bytes 331784 | tf_op jit(solution)/shard_map/ppermute | solution.py:366
  12.4 2.3 %collective-permute-start.1 = (bf16[144,384]{1,0:T(8,128)(2,1)}, bf16[144,384]{1,0:T(8,128)(2,1)S(1)}, u32[]{:S(2)}, u32[]{:S(2)}) collective-permute-start(bf16[144,384]{1,0:T(8,128)(2,1)} %get-tuple-element.33), channel_id=1, source_target_pairs={{0,240},{16,0},{32,16},{48,32},{64,48},{80,64},{96,80},{112,96},{1... | collective-permute-start | bytes 331784 | tf_op jit(solution)/shard_map/ppermute | solution.py:367
  14.7 6.0 %collective-permute-start.2 = (bf16[144,384]{1,0:T(8,128)(2,1)}, bf16[144,384]{1,0:T(8,128)(2,1)S(1)}, u32[]{:S(2)}, u32[]{:S(2)}) collective-permute-start(bf16[144,384]{1,0:T(8,128)(2,1)} %get-tuple-element.34), channel_id=1, source_target_pairs={{0,255},{1,240},{2,241},{3,242},{4,243},{5,244},{6,245},{7,246},{8... | collective-permute-start | bytes 331784 | tf_op jit(solution)/shard_map/ppermute | solution.py:368
  20.6 0.0 copy-done
  20.6 0.0 copy-done.1
  20.6 2.7 %shard_map.212.bias_ref = f32[4,144,864]{2,1,0:T(8,128)S(1)} custom-call(f32[1,1]{1,0:T(1,128)} %bitcast.5.active_ref, f32[1,79488]{1,0:T(1,128)S(1)} %copy-done, bf16[276,384]{1,0:T(8,128)(2,1)S(1)} %copy-done.1), custom_call_target="tpu_custom_call" | custom-call | flops 500000000 | bytes 4000000 | tf_op jit(solution)/shard_map/pallas_call | solution.py:428
  23.3 0.0 collective-permute-done.lon_ref
  23.3 0.0 collective-permute-done.1.lat_ref
  23.4 1.1 %collective-permute-done.2.both_ref = bf16[144,384]{1,0:T(8,128)(2,1)S(1)} collective-permute-done((bf16[144,384]{1,0:T(8,128)(2,1)}, bf16[144,384]{1,0:T(8,128)(2,1)S(1)}, u32[]{:S(2)}, u32[]{:S(2)}) %collective-permute-start.2) | collective-permute-done | bytes 110624 | tf_op jit(solution)/shard_map/ppermute | solution.py:368
  24.4 0.0 copy-done.2
  24.4 0.0 copy-done.4
  24.4 0.0 copy-done.6
  24.4 0.0 copy-done.8
  24.4 0.0 copy-done.9
  24.5 0.0 copy-done.10
  24.5 0.0 copy-done.13
  24.5 0.0 copy-done.14
  24.5 0.0 copy-done.21
  24.5 0.0 copy-start.3
  24.5 0.0 copy-start.5
  24.5 0.0 copy-start.7
  24.5 0.0 copy-start.11
  24.5 0.0 copy-start.12
  24.6 0.0 copy-start.15
  24.6 0.0 copy-start.16
  24.6 0.0 copy-start.17
  24.6 0.0 copy-start.18
  24.6 0.0 copy-start.19
  24.6 0.0 copy-start.20
  24.6 6.3 %shard_map.213 = (bf16[72,384]{1,0:T(8,128)(2,1)S(1)}, bf16[72,384]{1,0:T(8,128)(2,1)S(1)}, bf16[72,384]{1,0:T(8,128)(2,1)S(1)}, bf16[72,384]{1,0:T(8,128)(2,1)S(1)}, bf16[4,144,864]{2,1,0:T(8,128)(2,1)S(1)}) custom-call(bf16[144,384]{1,0:T(8,128)(2,1)S(1)} %copy-done.21, bf16[144,384]{1,0:T(8,128)(2,1)S(1)} %collective-permute-done.lon_ref, ...), custom_call_target="tpu_custom_call" | custom-call | flops 4000000000 | bytes 4000000 | tf_op jit(solution)/shard_map/pallas_call | solution.py:437
  31.0 0.1 collective-permute-start.3
  31.1 0.3 collective-permute-start.4
  31.3 0.1 collective-permute-start.5
  31.5 1.2 %shard_map.214.other_ref = f32[16,40,128]{2,1,0:T(8,128)S(1)} custom-call(bf16[4,144,864]{2,1,0:T(8,128)(2,1)S(1)} %get-tuple-element.46.low_ref, bf16[276,384]{1,0:T(8,128)(2,1)S(1)} %copy-done.1), custom_call_target="tpu_custom_call" | custom-call | flops 500000000 | bytes 4000000 | tf_op jit(solution)/shard_map/pallas_call | solution.py:446
  32.7 2.9 %collective-permute-done.3.lon_ref = bf16[72,384]{1,0:T(8,128)(2,1)S(1)} collective-permute-done((bf16[72,384]{1,0:T(8,128)(2,1)S(1)}, bf16[72,384]{1,0:T(8,128)(2,1)S(1)}, u32[]{:S(2)}, u32[]{:S(2)}) %collective-permute-start.3) | collective-permute-done | bytes 55328 | tf_op jit(solution)/shard_map/ppermute | solution.py:366
  35.6 2.9 %collective-permute-done.4.lat_ref = bf16[72,384]{1,0:T(8,128)(2,1)S(1)} collective-permute-done((bf16[72,384]{1,0:T(8,128)(2,1)S(1)}, bf16[72,384]{1,0:T(8,128)(2,1)S(1)}, u32[]{:S(2)}, u32[]{:S(2)}) %collective-permute-start.4) | collective-permute-done | bytes 55328 | tf_op jit(solution)/shard_map/ppermute | solution.py:367
  38.5 0.3 collective-permute-done.5.both_ref
  38.8 0.0 copy-done.3
  38.8 0.0 copy-done.5
  38.8 0.0 copy-done.7
  38.8 0.0 copy-done.11
  38.8 0.0 copy-done.12
  38.8 0.0 copy-done.15
  38.8 0.0 copy-done.16
  38.8 0.0 copy-done.17
  38.9 0.0 copy-done.18
  38.9 0.0 copy-done.19
  38.9 0.0 copy-done.20
  38.9 5.6 %shard_map.215 = (bf16[72,8,192]{2,1,0:T(8,128)(2,1)}, bf16[16,80,128]{2,1,0:T(8,128)(2,1)S(1)}) custom-call(bf16[72,384]{1,0:T(8,128)(2,1)S(1)} %get-tuple-element.36.stay_ref, bf16[72,384]{1,0:T(8,128)(2,1)S(1)} %collective-permute-done.3.lon_ref, bf16[72,384]{1,0:T(8,128)(2,1)S(1)} %collective-permute-done.4.lat_ref, ...), custom_call_target="tpu_custom_call" | custom-call | flops 4000000000 | bytes 4000000 | tf_op jit(solution)/shard_map/pallas_call | solution.py:448
  44.5 18.0 %all_to_all.5.arrived_ref = bf16[16,80,128]{2,1,0:T(8,128)(2,1)S(1)} all-to-all(bf16[16,80,128]{2,1,0:T(8,128)(2,1)S(1)} %get-tuple-element.48), channel_id=1, replica_groups=mesh['lat'=16,'lon'=16] {'lon'}, dimensions={0} | all-to-all | bytes 655360 | tf_op jit(solution)/shard_map/all_to_all | solution.py:456
  62.5 0.8 %shard_map.216 = (f32[1,4968]{1,0:T(1,128)}, f32[1,4968]{1,0:T(1,128)}) custom-call(bf16[16,80,128]{2,1,0:T(8,128)(2,1)S(1)} %all_to_all.5.arrived_ref), custom_call_target="tpu_custom_call" | custom-call | flops 1000000 | bytes 4000000 | tf_op jit(solution)/shard_map/pallas_call | solution.py:458
Async XLA Ops:
  0.6 20.0 %copy-start = (f32[1,79488]{1,0:T(1,128)S(1)}, f32[1,79488]{1,0:T(1,128)}, u32[]{:S(2)}) copy-start(f32[1,79488]{1,0:T(1,128)} %flat_hbm.2) | copy-start | bytes 953860
  0.6 20.0 %copy-start.1 = (bf16[276,384]{1,0:T(8,128)(2,1)S(1)}, bf16[276,384]{1,0:T(8,128)(2,1)}, u32[]{:S(2)}) copy-start(bf16[276,384]{1,0:T(8,128)(2,1)} %constant.32.clone.perm_hbm.perm_ref) | copy-start | bytes 635908
  9.9 14.5 %copy-start.2 = (bf16[192,576]{1,0:T(8,128)(2,1)S(1)}, bf16[192,576]{1,0:T(8,128)(2,1)}, u32[]{:S(2)}) copy-start(bf16[192,576]{1,0:T(8,128)(2,1)} %w_qkv_ref.2) | copy-start | bytes 663556
  9.9 14.5 %copy-start.4 = (bf16[192,192]{1,0:T(8,128)(2,1)S(1)}, bf16[192,192]{1,0:T(8,128)(2,1)}, u32[]{:S(2)}) copy-start(bf16[192,192]{1,0:T(8,128)(2,1)} %w_proj_ref.2) | copy-start | bytes 221188
  9.9 14.5 %copy-start.6 = (f32[192]{0:T(256)S(1)}, f32[192]{0:T(256)}, u32[]{:S(2)}) copy-start(f32[192]{0:T(256)} %param.26) | copy-start | bytes 2308
  9.9 14.5 %copy-start.8 = (bf16[864,192]{1,0:T(8,128)(2,1)S(1)}, bf16[864,192]{1,0:T(8,128)(2,1)}, u32[]{:S(2)}) copy-start(bf16[864,192]{1,0:T(8,128)(2,1)} %constant.30.clone.mask_hbm.mask_ref) | copy-start | bytes 995332
  10.0 14.5 %copy-start.9 = (bf16[864,144]{1,0:T(8,128)(2,1)S(1)}, bf16[864,144]{1,0:T(8,128)(2,1)}, u32[]{:S(2)}) copy-start(bf16[864,144]{1,0:T(8,128)(2,1)} %constant.29.clone.rep_hbm.rep_ref) | copy-start | bytes 746500
  10.0 14.5 %copy-start.10 = (bf16[192,864]{1,0:T(8,128)(2,1)S(1)}, bf16[192,864]{1,0:T(8,128)(2,1)}, u32[]{:S(2)}) copy-start(bf16[192,864]{1,0:T(8,128)(2,1)} %constant.31.clone.mask_t_hbm.mask_t_ref) | copy-start | bytes 995332
  10.0 14.5 %copy-start.13 = (bf16[144,144]{1,0:T(8,128)(2,1)S(1)}, bf16[144,144]{1,0:T(8,128)(2,1)}, u32[]{:S(2)}) copy-start(bf16[144,144]{1,0:T(8,128)(2,1)} %constant.36.clone.join_t_ref) | copy-start | bytes 124420
  10.0 14.5 %copy-start.14 = (bf16[144,144]{1,0:T(8,128)(2,1)S(1)}, bf16[144,144]{1,0:T(8,128)(2,1)}, u32[]{:S(2)}) copy-start(bf16[144,144]{1,0:T(8,128)(2,1)} %constant.35.clone.join_ref) | copy-start | bytes 124420
  10.0 14.5 %copy-start.21 = (bf16[144,384]{1,0:T(8,128)(2,1)S(1)}, bf16[144,384]{1,0:T(8,128)(2,1)}, u32[]{:S(2)}) copy-start(bf16[144,384]{1,0:T(8,128)(2,1)} %get-tuple-element.31.stay_ref) | copy-start | bytes 331780
  10.0 13.3 %collective-permute-start = (bf16[144,384]{1,0:T(8,128)(2,1)}, bf16[144,384]{1,0:T(8,128)(2,1)S(1)}, u32[]{:S(2)}, u32[]{:S(2)}) collective-permute-start(bf16[144,384]{1,0:T(8,128)(2,1)} %get-tuple-element.32), channel_id=1, source_target_pairs={{0,15},{1,0},{2,1},{3,2},{4,3},{5,4},{6,5},{7,6},{8,7},{9,8},{10,9... | collective-permute-start | bytes 331784 | tf_op jit(solution)/shard_map/ppermute | solution.py:366
  12.4 11.0 %collective-permute-start.1 = (bf16[144,384]{1,0:T(8,128)(2,1)}, bf16[144,384]{1,0:T(8,128)(2,1)S(1)}, u32[]{:S(2)}, u32[]{:S(2)}) collective-permute-start(bf16[144,384]{1,0:T(8,128)(2,1)} %get-tuple-element.33), channel_id=1, source_target_pairs={{0,240},{16,0},{32,16},{48,32},{64,48},{80,64},{96,80},{112,96},{1... | collective-permute-start | bytes 331784 | tf_op jit(solution)/shard_map/ppermute | solution.py:367
  14.7 9.8 %collective-permute-start.2 = (bf16[144,384]{1,0:T(8,128)(2,1)}, bf16[144,384]{1,0:T(8,128)(2,1)S(1)}, u32[]{:S(2)}, u32[]{:S(2)}) collective-permute-start(bf16[144,384]{1,0:T(8,128)(2,1)} %get-tuple-element.34), channel_id=1, source_target_pairs={{0,255},{1,240},{2,241},{3,242},{4,243},{5,244},{6,245},{7,246},{8... | collective-permute-start | bytes 331784 | tf_op jit(solution)/shard_map/ppermute | solution.py:368
  24.5 14.3 %copy-start.3 = (bf16[192,576]{1,0:T(8,128)(2,1)S(1)}, bf16[192,576]{1,0:T(8,128)(2,1)}, u32[]{:S(2)}) copy-start(bf16[192,576]{1,0:T(8,128)(2,1)} %w_qkv_ref.3) | copy-start | bytes 663556
  24.5 14.3 %copy-start.5 = (bf16[192,192]{1,0:T(8,128)(2,1)S(1)}, bf16[192,192]{1,0:T(8,128)(2,1)}, u32[]{:S(2)}) copy-start(bf16[192,192]{1,0:T(8,128)(2,1)} %w_proj_ref.3) | copy-start | bytes 221188
  24.5 14.3 %copy-start.7 = (f32[192]{0:T(256)S(1)}, f32[192]{0:T(256)}, u32[]{:S(2)}) copy-start(f32[192]{0:T(256)} %param.22) | copy-start | bytes 2308
  24.5 14.3 %copy-start.11 = (bf16[144,144]{1,0:T(8,128)(2,1)S(1)}, bf16[144,144]{1,0:T(8,128)(2,1)}, u32[]{:S(2)}) copy-start(bf16[144,144]{1,0:T(8,128)(2,1)} %constant.37.clone.turn_hbm.turn_t_ref) | copy-start | bytes 124420
  24.5 14.3 %copy-start.12 = (bf16[144,144]{1,0:T(8,128)(2,1)S(1)}, bf16[144,144]{1,0:T(8,128)(2,1)}, u32[]{:S(2)}) copy-start(bf16[144,144]{1,0:T(8,128)(2,1)} %constant.33.clone.split_ref) | copy-start | bytes 124420
  24.6 14.3 %copy-start.15 = (bf16[4,864,192]{2,1,0:T(8,128)(2,1)S(1)}, bf16[4,864,192]{2,1,0:T(8,128)(2,1)}, u32[]{:S(2)}) copy-start(bf16[4,864,192]{2,1,0:T(8,128)(2,1)} %get-tuple-element.42.q_ref) | copy-start | bytes 3981316
  24.6 14.3 %copy-start.16 = (bf16[4,144,864]{2,1,0:T(8,128)(2,1)S(1)}, bf16[4,144,864]{2,1,0:T(8,128)(2,1)}, u32[]{:S(2)}) copy-start(bf16[4,144,864]{2,1,0:T(8,128)(2,1)} %get-tuple-element.45.probs_ref) | copy-start | bytes 2985988
  24.6 14.3 %copy-start.17 = (f32[4,144,192]{2,1,0:T(8,128)S(1)}, f32[4,144,192]{2,1,0:T(8,128)}, u32[]{:S(2)}) copy-start(f32[4,144,192]{2,1,0:T(8,128)} %get-tuple-element.40.normed_ref) | copy-start | bytes 1327108
  24.6 14.3 %copy-start.18 = (f32[4,144,128]{2,1,0:T(8,128)S(1)}, f32[4,144,128]{2,1,0:T(8,128)}, u32[]{:S(2)}) copy-start(f32[4,144,128]{2,1,0:T(8,128)} %get-tuple-element.41.inv_ref) | copy-start | bytes 884740
  24.6 14.3 %copy-start.19 = (bf16[4,144,192]{2,1,0:T(8,128)(2,1)S(1)}, bf16[4,144,192]{2,1,0:T(8,128)(2,1)}, u32[]{:S(2)}) copy-start(bf16[4,144,192]{2,1,0:T(8,128)(2,1)} %get-tuple-element.43.k_ref) | copy-start | bytes 663556
  24.6 14.3 %copy-start.20 = (bf16[4,144,192]{2,1,0:T(8,128)(2,1)S(1)}, bf16[4,144,192]{2,1,0:T(8,128)(2,1)}, u32[]{:S(2)}) copy-start(bf16[4,144,192]{2,1,0:T(8,128)(2,1)} %get-tuple-element.44.v_ref) | copy-start | bytes 663556
  31.0 4.6 %collective-permute-start.3 = (bf16[72,384]{1,0:T(8,128)(2,1)S(1)}, bf16[72,384]{1,0:T(8,128)(2,1)S(1)}, u32[]{:S(2)}, u32[]{:S(2)}) collective-permute-start(bf16[72,384]{1,0:T(8,128)(2,1)S(1)} %get-tuple-element.37), channel_id=1, source_target_pairs={{0,1},{1,2},{2,3},{3,4},{4,5},{5,6},{6,7},{7,8},{8,9},{9,10},{10,1... | collective-permute-start | bytes 165896 | tf_op jit(solution)/shard_map/ppermute | solution.py:366
  31.1 7.5 %collective-permute-start.4 = (bf16[72,384]{1,0:T(8,128)(2,1)S(1)}, bf16[72,384]{1,0:T(8,128)(2,1)S(1)}, u32[]{:S(2)}, u32[]{:S(2)}) collective-permute-start(bf16[72,384]{1,0:T(8,128)(2,1)S(1)} %get-tuple-element.38), channel_id=1, source_target_pairs={{0,16},{16,32},{32,48},{48,64},{64,80},{80,96},{96,112},{112,128},... | collective-permute-start | bytes 165896 | tf_op jit(solution)/shard_map/ppermute | solution.py:367
  31.3 7.5 %collective-permute-start.5 = (bf16[72,384]{1,0:T(8,128)(2,1)S(1)}, bf16[72,384]{1,0:T(8,128)(2,1)S(1)}, u32[]{:S(2)}, u32[]{:S(2)}) collective-permute-start(bf16[72,384]{1,0:T(8,128)(2,1)S(1)} %get-tuple-element.39), channel_id=1, source_target_pairs={{0,17},{1,18},{2,19},{3,20},{4,21},{5,22},{6,23},{7,24},{8,25},{9,... | collective-permute-start | bytes 165896 | tf_op jit(solution)/shard_map/ppermute | solution.py:368

commit v4 on v3

--- a/solution.py
+++ b/solution.py
@@ -25,6 +25,7 @@
 PIECE = 36
 FLAT = 128
 PERIOD = 32 * ROWS
+COLUMNS = LEV * WIN_LAT * WIN_LON
 TERM = 40
 SHARE = 18
 REST = ROWS - 2 * FLAT
@@ -39,7 +40,9 @@
     lanes = np.arange(LANES)
     lane_lon, lane_head, lane_pair = lanes // SLAB, lanes // BAND % HEADS, lanes % BAND
     rep = (lane_lon * BAND + lane_pair)[:, None] == np.arange(WIN_TOK)[None, :]
-    mask = lane_head[:, None] == (np.arange(D) // HEAD_DIM)[None, :]
+    mask_t = (np.arange(D) // HEAD_DIM)[:, None] == lane_head[None, :]
+    pairs = np.arange(2 * WIN_TOK)
+    twice = (pairs // (2 * BAND) * BAND + pairs % BAND)[:, None] == np.arange(WIN_TOK)[None, :]
     rows = np.arange(ROWS)
     source = (rows % BAND) * OFFSETS + (OFFSETS - 1 - rows // BAND)
     perm = source[:, None] == np.arange(3 * FLAT)[None, :]
@@ -50,10 +53,8 @@
     joined = 2 * (lat >= 3) + (lon >= 6)
     split = (cut * PIECE + within)[:, None] == tok[None, :]
     join = (joined * PIECE + within)[:, None] == tok[None, :]
-    turn = ((lev * WIN_LAT + lat) * WIN_LON + lon)[:, None] == tok[None, :]
     return dict(
-        rep=rep, mask=mask, mask_t=mask.T, perm=perm, split=split, split_t=split.T, join=join, join_t=join.T,
-        turn=turn, turn_t=turn.T,
+        rep=rep, twice=twice, mask_t=mask_t, perm=perm, split=split, split_t=split.T, join=join, join_t=join.T,
     )
 
 
@@ -122,45 +123,76 @@
             ]
 
 
-def load_windows(grid_ref, left_ref, right_ref):
-    wide = grid_ref[...].astype(F32).reshape(LEV * BAND // WIN_LEV * WIN_LON, D)
-    left_ref[...] = wide[:, :FLAT]
-    right_ref[:, : D - FLAT] = wide[:, FLAT:]
-    windows = []
-    for v in LEVELS:
-        halves = []
-        for lev in range(WIN_LEV):
-            rows = pl.ds(WIN_LEV * v + lev, WIN_LAT * WIN_LON, stride=LEV)
-            halves.append(jnp.concatenate([left_ref[rows, :], right_ref[rows, :][:, : D - FLAT]], 1))
-        windows.append(jnp.concatenate(halves, 0).astype(BF16))
-    return windows
-
-
-def store_windows(windows, grid_ref, left_ref, right_ref):
-    for v in LEVELS:
-        for lev in range(WIN_LEV):
-            rows = pl.ds(WIN_LEV * v + lev, WIN_LAT * WIN_LON, stride=LEV)
-            half = windows[v][lev * WIN_LAT * WIN_LON : (lev + 1) * WIN_LAT * WIN_LON]
-            left_ref[rows, :] = half[:, :FLAT]
-            right_ref[rows, :] = jnp.concatenate([half[:, FLAT:], jnp.zeros((WIN_LAT * WIN_LON, 2 * FLAT - D), F32)], 1)
-    wide = jnp.concatenate([left_ref[...], right_ref[:, : D - FLAT]], 1)
+def picks():
+    row = lax.broadcasted_iota(jnp.int32, (WIN_TOK, COLUMNS), 0)
+    lane = lax.broadcasted_iota(jnp.int32, (WIN_TOK, COLUMNS), 1)
+    lon, pair = row // BAND, row % BAND
+    place = (pair % WIN_LAT * WIN_LON + lon) * LEV + pair // WIN_LAT
+    return [jnp.where(place + WIN_LEV * v == lane, 1.0, 0.0).astype(BF16) for v in LEVELS]
+
+
+def spreaders():
+    row = lax.broadcasted_iota(jnp.int32, (LANES, WIN_TOK), 0)
+    lane = lax.broadcasted_iota(jnp.int32, (LANES, WIN_TOK), 1)
+    rep = jnp.where(row // SLAB * BAND + row % BAND == lane, 1.0, 0.0).astype(BF16)
+    row = lax.broadcasted_iota(jnp.int32, (D, LANES), 0)
+    lane = lax.broadcasted_iota(jnp.int32, (D, LANES), 1)
+    return rep, jnp.where(row // HEAD_DIM == lane // BAND % HEADS, 1.0, 0.0).astype(BF16)
+
+
+def load_windows(grid_ref, picked):
+    wide = grid_ref[...].astype(F32).reshape(COLUMNS, D).astype(BF16)
+    return [dot(pick, wide) for pick in picked]
+
+
+def store_windows(windows, picked, grid_ref):
+    wide = sum(dot(pick, x, TN) for pick, x in zip(picked, windows))
     grid_ref[...] = wide.reshape(WIN_LAT * WIN_LON, LEV, D).astype(BF16)
 
 
-def forward(inputs, biases, gain, w_qkv, rep, mask):
+class Fetch:
+    def __init__(self, pairs, sem):
+        self.copies = [pltpu.make_async_copy(src, dst, sem.at[k]) for k, (src, dst) in enumerate(pairs)]
+        for copy in self.copies:
+            copy.start()
+
+    def wait(self, first=0, last=None):
+        for copy in self.copies[first:last]:
+            copy.wait()
+
+
+def spread_heads(rows, twice):
+    row = lax.broadcasted_iota(jnp.int32, (SLAB, D), 0)
+    lane = lax.broadcasted_iota(jnp.int32, (SLAB, D), 1)
+    own = jnp.zeros((SLAB, D), F32)
+    for head in range(HEADS):
+        in_rows = (row >= head * BAND) & (row < (head + 1) * BAND)
+        own = jnp.where(in_rows & (lane >= head * HEAD_DIM) & (lane < (head + 1) * HEAD_DIM), 1.0, own)
+    own = own.reshape(1, HEADS // 2, 2 * BAND, D)
+    spread = []
+    for x in rows:
+        doubled = dot(twice, x).reshape(WIN_LON, 1, 2 * BAND, D)
+        spread.append((doubled * own).reshape(LANES, D).astype(BF16))
+    return spread
+
+
+def project(inputs, gain, w_qkv):
     centred = [x - jnp.mean(x, -1, keepdims=True) for x in inputs]
     inv_std = [lax.rsqrt(jnp.mean(x * x, -1, keepdims=True) + 1e-05) for x in centred]
     normed = [x * inv for x, inv in zip(centred, inv_std)]
     hidden = [(x * gain).astype(BF16) for x in normed]
     packed = [dot(x, w_qkv).astype(BF16) for x in hidden]
-    k_rows = [x[:, D : 2 * D] for x in packed]
-    v_rows = [x[:, 2 * D :] for x in packed]
-    q_spread = [dot(rep, x[:, :D]).astype(BF16) * mask for x in packed]
+    return normed, inv_std, *([x[:, k * D : (k + 1) * D] for x in packed] for k in range(3))
+
+
+def forward(inputs, biases, gain, w_qkv, twice):
+    normed, inv_std, q_rows, k_rows, v_rows = project(inputs, gain, w_qkv)
+    q_spread = spread_heads(q_rows, twice)
     scores = [dot(k, q, NT) * (SCALE * LOG2E) + bias[...] for k, q, bias in zip(k_rows, q_spread, biases)]
     exp_scores = [jnp.exp2(x - jnp.max(x, 0, keepdims=True)) for x in scores]
     attn_probs = [x * (1.0 / jnp.sum(x, 0, keepdims=True)) for x in exp_scores]
     probs_low = [x.astype(BF16) for x in attn_probs]
-    return list(zip(normed, inv_std, q_spread, k_rows, v_rows, attn_probs, probs_low))
+    return normed, inv_std, q_rows, q_spread, k_rows, v_rows, attn_probs, probs_low
 
 
 def gathered(values, weights, rep, mask_t):
@@ -168,17 +200,20 @@
     return [dot(x, rep).T.astype(BF16) for x in spread]
 
 
-def backward(saved, grads, gain, w_qkv_ref, w_proj, rep, mask, mask_t):
-    normed, inv_std, q_spread, k_rows, v_rows, attn_probs, probs_low = zip(*saved)
+def score_grads(v_rows, attn_probs, grads, w_proj, twice):
     grad_mixed = [dot(x, w_proj, NT).astype(BF16) for x in grads]
-    mixed_spread = [dot(rep, x).astype(BF16) * mask for x in grad_mixed]
+    mixed_spread = spread_heads(grad_mixed, twice)
     grad_probs = [dot(v, m, NT) for v, m in zip(v_rows, mixed_spread)]
-    grad_v = [dot(p, m).astype(BF16) for p, m in zip(probs_low, mixed_spread)]
     lows = [
         ((p * (x - jnp.sum(x * p, 0, keepdims=True))) * SCALE).astype(BF16) for p, x in zip(attn_probs, grad_probs)
     ]
+    return grad_mixed, mixed_spread, lows
+
+
+def input_grads(normed, inv_std, q_spread, k_rows, probs_low, mixed_spread, lows, grads, gain, w_qkv_ref, rep, mask_t):
+    grad_q = gathered(k_rows, lows, rep, mask_t)
     grad_k = [dot(low, q).astype(BF16) for low, q in zip(lows, q_spread)]
-    grad_q = gathered(k_rows, lows, rep, mask_t)
+    grad_v = [dot(p, m).astype(BF16) for p, m in zip(probs_low, mixed_spread)]
     w_q, w_k, w_v = w_qkv_ref[:, :D], w_qkv_ref[:, D : 2 * D], w_qkv_ref[:, 2 * D :]
     results = []
     for v, grad in enumerate(grads):
@@ -190,64 +225,51 @@
             - normed[v] * jnp.mean(grad_normed * normed[v], -1, keepdims=True)
         )
         results.append((grad.astype(F32) + grad_local).astype(BF16))
-    return results, lows
+    return results
 
 
 def first_kernel(
-    tokens_hbm, grad_hbm, flat_hbm, gain_hbm, w_qkv_hbm, w_proj_hbm, rep_hbm, mask_hbm, mask_t_hbm, perm_hbm, split_t_hbm, turn_hbm,
-    stay_hbm, lon_ref, lat_ref, both_ref, normed_hbm, inv_hbm, q_hbm, k_hbm, v_hbm, probs_hbm,
-    part_a, part_b, part_c, spread_ref, bias_ref, left_ref, right_ref, piece_ref, rows_ref, normed_ref, inv_ref,
-    tokens_ref, grad_ref, w_qkv_ref, w_proj_ref, rep_ref, mask_ref, mask_t_ref, perm_ref, split_t_ref, turn_ref,
-    stay_ref, q_ref, k_ref, v_ref, probs_ref, gain_ref,
+    tokens_hbm, grad_hbm, flat_hbm, gain_hbm, w_qkv_hbm, w_proj_hbm, twice_hbm, perm_hbm, split_t_hbm,
+    stay_hbm, lon_hbm, lat_hbm, both_hbm, v_hbm, probs_hbm,
+    part_a, part_b, part_c, spread_ref, bias_ref, piece_ref, rows_ref, gain_ref,
+    tokens_ref, grad_ref, w_qkv_ref, w_proj_ref, twice_ref, perm_ref, split_t_ref, rep_ref, mask_t_ref,
+    out_ref, v_ref, probs_ref,
     table_sem, in_sem, out_sem,
 ):
     table = table_copies(flat_hbm, rows_ref, table_sem)
-    pairs = (
-        (perm_hbm, perm_ref), (tokens_hbm, tokens_ref), (turn_hbm, turn_ref), (gain_hbm, gain_ref), (w_qkv_hbm, w_qkv_ref),
-        (rep_hbm, rep_ref), (mask_hbm, mask_ref), (grad_hbm, grad_ref), (mask_t_hbm, mask_t_ref), (w_proj_hbm, w_proj_ref),
-        (split_t_hbm, split_t_ref),
-    )
-    fetch = [pltpu.make_async_copy(src, dst, in_sem.at[k]) for k, (src, dst) in enumerate(pairs)]
-    for copy in table + fetch:
+    for copy in table:
         copy.start()
-    for copy in fetch[1:5]:
+    fetch = Fetch(
+        (
+            (perm_hbm, perm_ref), (tokens_hbm, tokens_ref), (gain_hbm, gain_ref), (w_qkv_hbm, w_qkv_ref),
+            (twice_hbm, twice_ref), (grad_hbm, grad_ref), (w_proj_hbm, w_proj_ref), (split_t_hbm, split_t_ref),
+        ),
+        in_sem,
+    )
+    picked = picks()
+    rep_ref[...], mask_t_ref[...] = spreaders()
+    for copy in table:
         copy.wait()
-    turn = turn_ref[...]
-    inputs = [dot(turn, x) for x in load_windows(tokens_ref, left_ref, right_ref)]
-    for copy in table + fetch[:1]:
-        copy.wait()
+    fetch.wait()
     expand_table(rows_ref, perm_ref, (part_a, part_b, part_c), spread_ref)
     write_bias(spread_ref, bias_ref)
-    for copy in fetch[5:]:
-        copy.wait()
-    rep, mask, mask_t = rep_ref[...], mask_ref[...], mask_t_ref[...]
-    saved = forward(inputs, [bias_ref.at[v] for v in LEVELS], gain_ref[...], w_qkv_ref[...], rep, mask)
-    normed, inv_std, q_spread, k_rows, v_rows, attn_probs, probs_low = zip(*saved)
+    inputs = load_windows(tokens_ref, picked)
+    _, _, _, _, _, v_rows, _, probs_low = forward(
+        inputs, [bias_ref.at[v] for v in LEVELS], gain_ref[...], w_qkv_ref[...], twice_ref[...]
+    )
     for v in LEVELS:
-        normed_ref[v] = normed[v]
-        inv_ref[v] = jnp.broadcast_to(inv_std[v], (WIN_TOK, FLAT))
-        q_ref[v] = q_spread[v]
-        k_ref[v] = k_rows[v]
         v_ref[v] = v_rows[v]
         probs_ref[v] = probs_low[v]
-    pairs = ((normed_ref, normed_hbm), (inv_ref, inv_hbm), (q_ref, q_hbm), (k_ref, k_hbm), (v_ref, v_hbm), (probs_ref, probs_hbm))
-    keep = [pltpu.make_async_copy(src, dst, out_sem.at[k]) for k, (src, dst) in enumerate(pairs)]
-    for copy in keep:
-        copy.start()
-    attended = gathered(v_rows, probs_low, rep, mask_t)
-    grads = [dot(turn, x).astype(BF16) for x in load_windows(grad_ref, left_ref, right_ref)]
+    grads = [x.astype(BF16) for x in load_windows(grad_ref, picked)]
+    attended = gathered(v_rows, probs_low, rep_ref[...], mask_t_ref[...])
     split_t = split_t_ref[...]
     for v in LEVELS:
         block_out = (inputs[v] + dot(attended[v], w_proj_ref[...])).astype(BF16)
         piece_ref[:, v * PIECE : (v + 1) * PIECE, :D] = dot(split_t, block_out).reshape(4, PIECE, D)
         piece_ref[:, v * PIECE : (v + 1) * PIECE, D:] = dot(split_t, grads[v]).reshape(4, PIECE, D)
-    stay_ref[...] = piece_ref[0].astype(BF16)
-    stay = pltpu.make_async_copy(stay_ref, stay_hbm, out_sem.at[6])
-    stay.start()
-    for place, ref in ((1, lon_ref), (2, lat_ref), (3, both_ref)):
-        ref[...] = piece_ref[place].astype(BF16)
-    for copy in keep + [stay]:
-        copy.wait()
+    out_ref[...] = piece_ref[...].astype(BF16)
+    pairs = [(out_ref.at[k], ref) for k, ref in enumerate((stay_hbm, lon_hbm, lat_hbm, both_hbm))]
+    Fetch(pairs + [(v_ref, v_hbm), (probs_ref, probs_hbm)], out_sem).wait()
 
 
 def bias_kernel(active_ref, flat_hbm, perm_ref, bias_ref, part_a, part_b, part_c, spread_ref, rows_ref, sem):
@@ -264,11 +286,11 @@
 
 
 def second_kernel(
-    stay_ref, lon_ref, lat_ref, both_ref, bias_ref, gain_ref, w_qkv_ref, w_proj_ref, rep_ref, mask_ref, mask_t_ref, join_ref, join_t_ref,
+    stay_ref, lon_ref, lat_ref, both_ref, bias_ref, gain_ref, w_qkv_ref, w_proj_ref, rep_ref, twice_ref, mask_t_ref, join_ref, join_t_ref,
     stay_out, lon_out, lat_out, both_out, low_ref,
     window_ref, piece_ref,
 ):
-    rep, mask, mask_t = rep_ref[...], mask_ref[...], mask_t_ref[...]
+    twice = twice_ref[...]
     join, join_t = join_ref[...], join_t_ref[...]
     for place, ref in enumerate((stay_ref, lon_ref, lat_ref, both_ref)):
         wide = ref[...].astype(F32)
@@ -278,8 +300,13 @@
     inputs = [x[:, :D] for x in pairs]
     grads = [x[:, D:].astype(BF16) for x in pairs]
     gain, w_proj = gain_ref[...], w_proj_ref[...]
-    saved = forward(inputs, [bias_ref.at[v] for v in LEVELS], gain, w_qkv_ref[...], rep, mask)
-    results, lows = backward(saved, grads, gain, w_qkv_ref, w_proj, rep, mask, mask_t)
+    normed, inv_std, _, q_spread, k_rows, v_rows, attn_probs, probs_low = forward(
+        inputs, [bias_ref.at[v] for v in LEVELS], gain, w_qkv_ref[...], twice
+    )
+    _, mixed_spread, lows = score_grads(v_rows, attn_probs, grads, w_proj, twice)
+    results = input_grads(
+        normed, inv_std, q_spread, k_rows, probs_low, mixed_spread, lows, grads, gain, w_qkv_ref, rep_ref[...], mask_t_ref[...]
+    )
     for v in LEVELS:
         low_ref[v] = lows[v]
         row, lane = v % 2 * PIECE, v // 2 * D
@@ -293,27 +320,61 @@
 
 
 def third_kernel(
-    stay_ref, lon_ref, lat_ref, both_ref, normed_ref, inv_ref, q_ref, k_ref, v_ref, probs_ref, other_ref,
-    gain_ref, w_qkv_ref, w_proj_ref, rep_ref, mask_ref, mask_t_ref, perm_ref, split_ref, turn_t_ref,
-    grid_ref, terms_ref,
-    window_ref, left_ref, right_ref, folded_ref, table_ref, pack_ref,
+    stay_ref, lon_ref, lat_ref, both_ref, v_ref, probs_ref, other_ref, w_proj_ref, twice_ref, perm_ref, split_ref,
+    terms_ref, grad_ref,
+    window_ref, folded_ref, table_ref, pack_ref,
 ):
-    rep, mask, mask_t = rep_ref[...], mask_ref[...], mask_t_ref[...]
-    split, turn_t = split_ref[...], turn_t_ref[...]
+    split = split_ref[...]
     for place, ref in enumerate((stay_ref, lon_ref, lat_ref, both_ref)):
         wide = ref[...].astype(F32)
         for v in LEVELS:
             row, lane = v % 2 * PIECE, v // 2 * D
             window_ref[v, place * PIECE : (place + 1) * PIECE, :] = wide[row : row + PIECE, lane : lane + D]
     grads = [dot(split, window_ref[v].astype(BF16)).astype(BF16) for v in LEVELS]
-    saved = [
-        (normed_ref[v], inv_ref[v][:, :1], q_ref[v], k_ref[v], v_ref[v], probs_ref[v].astype(F32), probs_ref[v])
-        for v in LEVELS
-    ]
-    results, lows = backward(saved, grads, gain_ref[...], w_qkv_ref, w_proj_ref[...], rep, mask, mask_t)
-    store_windows([dot(turn_t, x) for x in results], grid_ref, left_ref, right_ref)
+    attn_probs = [probs_ref[v].astype(F32) for v in LEVELS]
+    _, _, lows = score_grads([v_ref[v] for v in LEVELS], attn_probs, grads, w_proj_ref[...], twice_ref[...])
+    for v in LEVELS:
+        grad_ref[v] = grads[v]
     fold_scores(lows, perm_ref, folded_ref, table_ref, pack_ref)
     terms_ref[...] = jnp.concatenate([pack_ref[...], other_ref[...]], 1).astype(BF16)
+
+
+def last_kernel(
+    tokens_hbm, probs_hbm, grad_hbm, gain_hbm, w_qkv_hbm, w_proj_hbm, twice_hbm,
+    grid_ref,
+    tokens_ref, probs_ref, grad_ref, gain_ref, w_qkv_ref, w_proj_ref, twice_ref,
+    sem,
+):
+    fetch = Fetch(
+        (
+            (tokens_hbm, tokens_ref), (gain_hbm, gain_ref), (w_qkv_hbm, w_qkv_ref), (twice_hbm, twice_ref), (w_proj_hbm, w_proj_ref),
+            (grad_hbm, grad_ref), (probs_hbm, probs_ref),
+        ),
+        sem,
+    )
+    picked = picks()
+    rep, mask_t = spreaders()
+    fetch.wait()
+    twice, gain = twice_ref[...], gain_ref[...]
+    normed, inv_std, q_rows, k_rows, v_rows = project(load_windows(tokens_ref, picked), gain, w_qkv_ref[...])
+    grads = [grad_ref[v] for v in LEVELS]
+    probs = [probs_ref[v] for v in LEVELS]
+    _, mixed_spread, lows = score_grads(v_rows, [x.astype(F32) for x in probs], grads, w_proj_ref[...], twice)
+    results = input_grads(
+        normed,
+        inv_std,
+        spread_heads(q_rows, twice),
+        k_rows,
+        probs,
+        mixed_spread,
+        lows,
+        grads,
+        gain,
+        w_qkv_ref,
+        rep,
+        mask_t,
+    )
+    store_windows(results, picked, grid_ref)
 
 
 def sum_kernel(arrived_ref, one_ref, two_ref, total_ref):
@@ -373,9 +434,8 @@
     tokens, grad_out, gain_one, qkv_one, proj_one, bias_one, gain_two, qkv_two, proj_two, bias_two
 ):
     const = {name: jnp.asarray(value) for name, value in CONST.items()}
-    spread = (const["rep"], const["mask"], const["mask_t"])
+    spread = (const["rep"], const["twice"], const["mask_t"])
     perm = const["perm"]
-    block_one = (gain_one.reshape(1, D), qkv_one, proj_one) + spread
     block_two = (gain_two.reshape(1, D), qkv_two, proj_two) + spread
     columns = (WIN_LAT * WIN_LON, LEV, D)
 
@@ -388,35 +448,28 @@
     scores = (LEV_WIN, WIN_TOK, LANES)
     parts = [(LEV_WIN * SLAB, FLAT)] * 3
     folded = (ROWS, LEV_WIN * SLAB)
-    grid = [(LEV * WIN_LAT * WIN_LON, FLAT)] * 2
     table = (LEV_WIN * SLAB, 3 * FLAT)
     tiles = LEV_WIN * SLAB // SHARE
 
-    outs = (
-        [pair] * 4
-        + [(rows, F32), ((LEV_WIN, WIN_TOK, FLAT), F32), ((LEV_WIN, LANES, D), BF16), (rows, BF16), (rows, BF16), (scores, BF16)]
-    )
+    outs = [pair[0]] * 4 + [rows, scores]
     table_rows = (9, PERIOD)
     operands = (
-        level_last(tokens), level_last(grad_out), bias_one, *block_one, perm, const["split_t"], const["turn"]
-    )
-    held = [0, 1, 4, 5, 6, 7, 8, 9, 10, 11]
+        level_last(tokens), level_last(grad_out), bias_one, gain_one.reshape(1, D), qkv_one, proj_one,
+        const["twice"], perm, const["split_t"],
+    )
+    held = [0, 1, 4, 5, 6, 7, 8]
     first = pl.pallas_call(
         first_kernel,
         in_specs=[HBM] * len(operands),
-        out_specs=[HBM] + [VMEM] * 3 + [HBM] * 6,
-        out_shape=[jax.ShapeDtypeStruct(shape, dtype) for shape, dtype in outs],
+        out_specs=[HBM] * len(outs),
+        out_shape=[jax.ShapeDtypeStruct(shape, BF16) for shape in outs],
         scratch_shapes=[
             pltpu.VMEM(shape, F32)
-            for shape in parts
-            + [folded, scores]
-            + grid
-            + [(4, LEV_WIN * PIECE, 2 * D), table_rows, rows, (LEV_WIN, WIN_TOK, FLAT)]
+            for shape in parts + [folded, scores, (4, LEV_WIN * PIECE, 2 * D), table_rows, (1, D)]
         ]
         + [pltpu.VMEM(operands[k].shape, BF16) for k in held]
-        + [pltpu.VMEM(shape, BF16) for shape, _ in [outs[0]] + outs[6:]]
-        + [pltpu.VMEM((1, D), F32)]
-        + [pltpu.SemaphoreType.DMA((9,)), pltpu.SemaphoreType.DMA((11,)), pltpu.SemaphoreType.DMA((7,))],
+        + [pltpu.VMEM(shape, BF16) for shape in ((LANES, WIN_TOK), (D, LANES), (4,) + pair[0], rows, scores)]
+        + [pltpu.SemaphoreType.DMA((9,)), pltpu.SemaphoreType.DMA((8,)), pltpu.SemaphoreType.DMA((6,))],
         compiler_params=pltpu.CompilerParams(vmem_limit_bytes=ALL_VMEM),
         cost_estimate=pl.CostEstimate(flops=2_000_000_000, bytes_accessed=4_000_000, transcendentals=500_000),
     )(*operands)
@@ -445,15 +498,27 @@
 
     (term_two,) = call(fold_kernel, [((tiles, TERM, FLAT), F32)], [folded, table], 500_000_000)(low_two, perm)
 
-    grid_out, terms = call(
+    v_rows, probs = saved
+    operands = (*grad_pieces, v_rows, probs, term_two, proj_one, const["twice"], perm, const["split"])
+    terms, grads = call(
         third_kernel,
-        [(columns, BF16), ((tiles, 2 * TERM, FLAT), BF16)],
-        [rows] + grid + [folded, table, (tiles, TERM, FLAT)],
-        4_000_000_000,
-    )(*grad_pieces, *saved, term_two, *block_one, perm, const["split"], const["turn_t"])
+        [((tiles, 2 * TERM, FLAT), BF16), (rows, BF16)],
+        [rows, folded, table, (tiles, TERM, FLAT)],
+        2_000_000_000,
+    )(*operands)
+
+    arrived = lax.all_to_all(terms, "lon", 0, 0, tiled=True)
+    operands = (level_last(tokens), probs, grads, gain_one.reshape(1, D), qkv_one, proj_one, const["twice"])
+    grid_out = pl.pallas_call(
+        last_kernel,
+        in_specs=[HBM] * len(operands),
+        out_shape=jax.ShapeDtypeStruct(columns, BF16),
+        scratch_shapes=[pltpu.VMEM(x.shape, x.dtype) for x in operands]
+        + [pltpu.SemaphoreType.DMA((len(operands),))],
+        compiler_params=pltpu.CompilerParams(vmem_limit_bytes=ALL_VMEM),
+        cost_estimate=pl.CostEstimate(flops=3_000_000_000, bytes_accessed=5_000_000, transcendentals=0),
+    )(*operands)
     grad_tokens = grid_out.reshape(WIN_LAT, WIN_LON, LEV, D).transpose(2, 0, 1, 3)
-
-    arrived = lax.all_to_all(terms, "lon", 0, 0, tiled=True)
     width = SHARE * ROWS
     summed_one, summed_two = call(
         sum_kernel, [((1, width), F32), ((1, width), F32)], [(2 * TERM, FLAT)], 1_000_000

time: 64 us -> 61.1 us (0.955)
  blocking collectives: 18 us -> 0 us
  starting transfers between devices: 11.1 us -> 19.5 us
  Pallas kernels: 25.9 us -> 29 us
  waiting for transfers between devices: 7.17 us -> 10.2 us
  local copies, waits for them, and re-layouts: 0.13 us -> 0.81 us
    all_to_all x1 -> x0, blocking collectives: 18 us -> none  [body(): arrived = lax.all_to_all(terms, 'lon', 0, 0, tiled=True)]
    all_to_all x0 -> x1, starting transfers between devices: none -> 8.38 us  [body(): arrived = lax.all_to_all(terms, 'lon', 0, 0, tiled=True)]
    pallas_call x1 -> x2, Pallas kernels: 5.57 us -> 10.2 us  [the longest x1 6.83 us: body(): pl.pallas_call(last_kernel, in_specs=[HBM] * len(operands), out_shape=jax...]
    all_to_all x0 -> x1, waiting for transfers between devices: none -> 3 us  [body(): arrived = lax.all_to_all(terms, 'lon', 0, 0, tiled=True)]
    pallas_call x1, Pallas kernels: 6.34 us -> 5.47 us  [body(): call(second_kernel, [single] * 4 + [(scores, BF16)], [(LEV_WIN, WIN_TOK,...]
    pallas_call x1, Pallas kernels: 9.24 us -> 8.51 us  [body(): pl.pallas_call(first_kernel, in_specs=[HBM] * len(operands), out_specs=[H...]
    unnamed x44 -> x32, local copies, waits for them, and re-layouts: 0.13 us -> 0.81 us
  transfers between devices with their start and end apart: 6 -> 7, of which waited for: 4 -> 5; matrix products, arithmetic and copies ran while one was open for 0% -> 0% of each run, Pallas kernels for 6% -> 18%
where the time goes in v4:
time: 61.1 us; the launch traced here: 60.3 us
  Pallas kernels  29 us (47%)
  starting transfers between devices  19.5 us (32%)
  waiting for transfers between devices  10.2 us (17%)
  between operations  0.87 us (1%)
  local copies, waits for them, and re-layouts  0.81 us (1%)
    pallas_call x1, Pallas kernels, body(): pl.pallas_call(first_kernel, in_specs=[HBM] * len(operands), out_specs=[H...  8.51 us
    all_to_all x1, starting transfers between devices, body(): arrived = lax.all_to_all(terms, 'lon', 0, 0, tiled=True)  8.38 us
    pallas_call x1, Pallas kernels, body(): pl.pallas_call(last_kernel, in_specs=[HBM] * len(operands), out_shape=jax...  6.83 us
    ppermute x2, starting transfers between devices, exchange(): lax.ppermute(both, ('lat', 'lon'), shifted(('lat', 'lon'), by))  6.08 us
    pallas_call x1, Pallas kernels, body(): call(second_kernel, [single] * 4 + [(scores, BF16)], [(LEV_WIN, WIN_TOK,...  5.47 us
    pallas_call x1, Pallas kernels, body(): call(third_kernel, [((tiles, 2 * TERM, FLAT), BF16), (rows, BF16)], [rows...  3.4 us
    all_to_all x1, waiting for transfers between devices, body(): arrived = lax.all_to_all(terms, 'lon', 0, 0, tiled=True)  3 us
    ppermute x2, waiting for transfers between devices, exchange(): lax.ppermute(lat, ('lat',), shifted(('lat',), by))  2.92 us
  transfers between devices with their start and end apart: 7, of which 5 were waited for; matrix products, arithmetic and copies ran while one was open for 0% of the time, Pallas kernels for 18%

profile of v4, /device:TPU:2, one launch (start us, length us, event | category | flops | bytes accessed | tf_op | source)
XLA Modules:
  0.0 60.3 jit_solution(8913526551954324109)
XLA Ops:
  0.6 0.0 copy-start
  0.6 0.0 copy-start.1
  0.7 8.5 %shard_map.193 = (bf16[144,384]{1,0:T(8,128)(2,1)}, bf16[144,384]{1,0:T(8,128)(2,1)}, bf16[144,384]{1,0:T(8,128)(2,1)}, bf16[144,384]{1,0:T(8,128)(2,1)}, bf16[4...) custom-call(bf16[72,8,192]{2,1,0:T(8,128)(2,1)} %bitcast.14, bf16[72,8,192]{2,1,0:T(8,128)(2,1)} %bitcast.13, ...), custom_call_target="tpu_custom_call" | custom-call | flops 2000000000 | bytes 4000000 | tf_op jit(solution)/shard_map/pallas_call | solution.py:461
  9.2 0.0 copy-start.2
  9.2 0.0 copy-start.3
  9.2 0.0 copy-start.5
  9.2 0.0 copy-start.6
  9.2 0.0 copy-start.7
  9.2 0.0 copy-start.8
  9.2 0.0 copy-start.10
  9.3 0.0 copy-start.11
  9.3 2.3 %collective-permute-start = (bf16[144,384]{1,0:T(8,128)(2,1)}, bf16[144,384]{1,0:T(8,128)(2,1)S(1)}, u32[]{:S(2)}, u32[]{:S(2)}) collective-permute-start(bf16[144,384]{1,0:T(8,128)(2,1)} %get-tuple-element.29), channel_id=1, source_target_pairs={{0,15},{1,0},{2,1},{3,2},{4,3},{5,4},{6,5},{7,6},{8,7},{9,8},{10,9... | collective-permute-start | bytes 331784 | tf_op jit(solution)/shard_map/ppermute | solution.py:427
  11.6 2.3 %collective-permute-start.1 = (bf16[144,384]{1,0:T(8,128)(2,1)}, bf16[144,384]{1,0:T(8,128)(2,1)S(1)}, u32[]{:S(2)}, u32[]{:S(2)}) collective-permute-start(bf16[144,384]{1,0:T(8,128)(2,1)} %get-tuple-element.30), channel_id=1, source_target_pairs={{0,240},{16,0},{32,16},{48,32},{64,48},{80,64},{96,80},{112,96},{1... | collective-permute-start | bytes 331784 | tf_op jit(solution)/shard_map/ppermute | solution.py:428
  13.9 6.0 %collective-permute-start.2 = (bf16[144,384]{1,0:T(8,128)(2,1)}, bf16[144,384]{1,0:T(8,128)(2,1)S(1)}, u32[]{:S(2)}, u32[]{:S(2)}) collective-permute-start(bf16[144,384]{1,0:T(8,128)(2,1)} %get-tuple-element.31), channel_id=1, source_target_pairs={{0,255},{1,240},{2,241},{3,242},{4,243},{5,244},{6,245},{7,246},{8... | collective-permute-start | bytes 331784 | tf_op jit(solution)/shard_map/ppermute | solution.py:429
  19.9 0.0 copy-start.15
  19.9 0.0 copy-done
  19.9 0.0 copy-done.1
  19.9 2.7 %shard_map.194.bias_ref = f32[4,144,864]{2,1,0:T(8,128)S(1)} custom-call(f32[1,1]{1,0:T(1,128)} %bitcast.6.active_ref, f32[1,79488]{1,0:T(1,128)S(1)} %copy-done, bf16[276,384]{1,0:T(8,128)(2,1)S(1)} %copy-done.1), custom_call_target="tpu_custom_call" | custom-call | flops 500000000 | bytes 4000000 | tf_op jit(solution)/shard_map/pallas_call | solution.py:481
  22.6 0.0 collective-permute-done.lon_ref
  22.6 0.0 collective-permute-done.1.lat_ref
  22.6 1.1 %collective-permute-done.2.both_ref = bf16[144,384]{1,0:T(8,128)(2,1)S(1)} collective-permute-done((bf16[144,384]{1,0:T(8,128)(2,1)}, bf16[144,384]{1,0:T(8,128)(2,1)S(1)}, u32[]{:S(2)}, u32[]{:S(2)}) %collective-permute-start.2) | collective-permute-done | bytes 110624 | tf_op jit(solution)/shard_map/ppermute | solution.py:429
  23.7 0.0 copy-done.2
  23.7 0.0 copy-done.3
  23.7 0.0 copy-done.5
  23.7 0.0 copy-done.6
  23.7 0.0 copy-done.7
  23.7 0.0 copy-done.8
  23.7 0.0 copy-done.10
  23.7 0.0 copy-done.11
  23.7 0.0 copy-done.15
  23.7 0.0 copy-start.4
  23.8 0.0 copy-start.9
  23.8 0.0 copy-start.12
  23.8 0.0 copy-start.13
  23.8 5.5 %shard_map.195 = (bf16[72,384]{1,0:T(8,128)(2,1)S(1)}, bf16[72,384]{1,0:T(8,128)(2,1)S(1)}, bf16[72,384]{1,0:T(8,128)(2,1)S(1)}, bf16[72,384]{1,0:T(8,128)(2,1)S(1)}, bf16[4,144,864]{2,1,0:T(8,128)(2,1)S(1)}) custom-call(bf16[144,384]{1,0:T(8,128)(2,1)S(1)} %copy-done.15, bf16[144,384]{1,0:T(8,128)(2,1)S(1)} %collective-permute-done.lon_ref, ...), custom_call_target="tpu_custom_call" | custom-call | flops 4000000000 | bytes 4000000 | tf_op jit(solution)/shard_map/pallas_call | solution.py:490
  29.3 0.1 collective-permute-start.3
  29.4 0.3 collective-permute-start.4
  29.7 0.1 collective-permute-start.5
  29.8 1.2 %shard_map.196.other_ref = f32[16,40,128]{2,1,0:T(8,128)S(1)} custom-call(bf16[4,144,864]{2,1,0:T(8,128)(2,1)S(1)} %get-tuple-element.38.low_ref, bf16[276,384]{1,0:T(8,128)(2,1)S(1)} %copy-done.1), custom_call_target="tpu_custom_call" | custom-call | flops 500000000 | bytes 4000000 | tf_op jit(solution)/shard_map/pallas_call | solution.py:499
  31.0 2.9 %collective-permute-done.3.lon_ref = bf16[72,384]{1,0:T(8,128)(2,1)S(1)} collective-permute-done((bf16[72,384]{1,0:T(8,128)(2,1)S(1)}, bf16[72,384]{1,0:T(8,128)(2,1)S(1)}, u32[]{:S(2)}, u32[]{:S(2)}) %collective-permute-start.3) | collective-permute-done | bytes 55328 | tf_op jit(solution)/shard_map/ppermute | solution.py:427
  33.9 2.9 %collective-permute-done.4.lat_ref = bf16[72,384]{1,0:T(8,128)(2,1)S(1)} collective-permute-done((bf16[72,384]{1,0:T(8,128)(2,1)S(1)}, bf16[72,384]{1,0:T(8,128)(2,1)S(1)}, u32[]{:S(2)}, u32[]{:S(2)}) %collective-permute-start.4) | collective-permute-done | bytes 55328 | tf_op jit(solution)/shard_map/ppermute | solution.py:428
  36.9 0.3 collective-permute-done.5.both_ref
  37.1 0.0 copy-done.4
  37.1 0.0 copy-done.9
  37.1 0.0 copy-done.12
  37.1 0.0 copy-done.13
  37.1 3.4 %shard_map.197 = (bf16[16,80,128]{2,1,0:T(8,128)(2,1)}, bf16[4,144,192]{2,1,0:T(8,128)(2,1)S(1)}) custom-call(bf16[72,384]{1,0:T(8,128)(2,1)S(1)} %get-tuple-element.33.stay_ref, bf16[72,384]{1,0:T(8,128)(2,1)S(1)} %collective-permute-done.3.lon_ref, bf16[72,384]{1,0:T(8,128)(2,1)S(1)} %collective-permute-done.4.lat_ref, ...), custom_call_target="tpu_custom_call" | custom-call | flops 2000000000 | bytes 4000000 | tf_op jit(solution)/shard_map/pallas_call | solution.py:503
  40.5 0.0 copy-start.14
  40.5 0.7 %copy-done.14 = bf16[4,144,192]{2,1,0:T(8,128)(2,1)} copy-done((bf16[4,144,192]{2,1,0:T(8,128)(2,1)}, bf16[4,144,192]{2,1,0:T(8,128)(2,1)S(1)}, u32[]{:S(2)}) %copy-start.14) | copy-done | bytes 221208
  41.2 8.4 %all-to-all-start = ((bf16[16,80,128]{2,1,0:T(8,128)(2,1)}), bf16[16,80,128]{2,1,0:T(8,128)(2,1)S(1)}, u32[]{:S(2)}, u32[]{:S(2)}) async-start(bf16[16,80,128]{2,1,0:T(8,128)(2,1)} %get-tuple-element.40), calls=%async_computation | async-start | bytes 655360 | tf_op jit(solution)/shard_map/all_to_all | solution.py:510
  49.6 6.8 %shard_map.198 = bf16[72,8,192]{2,1,0:T(8,128)(2,1)} custom-call(bf16[72,8,192]{2,1,0:T(8,128)(2,1)} %bitcast.15, bf16[4,144,864]{2,1,0:T(8,128)(2,1)} %get-tuple-element.23.probs_ref.probs_hbm, bf16[4,144,192]{2,1,0:T(8,128)(2,1)} %copy-done.14, f32[1,192]{1,0:T(1,128)} %bitcast.17, bf16[192,576]{1,0:T(8,128)(2,1)} %w_qkv_hbm.3, ...), custom_call_target="tpu_custom_call" | custom-call | flops 3000000000 | bytes 5000000 | tf_op jit(solution)/shard_map/pallas_call | solution.py:512
  56.5 3.0 %all-to-all-done.arrived_ref = bf16[16,80,128]{2,1,0:T(8,128)(2,1)S(1)} async-done(((bf16[16,80,128]{2,1,0:T(8,128)(2,1)}), bf16[16,80,128]{2,1,0:T(8,128)(2,1)S(1)}, u32[]{:S(2)}, u32[]{:S(2)}) %all-to-all-start) | async-done | bytes 327712 | tf_op jit(solution)/shard_map/all_to_all | solution.py:510
  59.5 0.8 %shard_map.199 = (f32[1,4968]{1,0:T(1,128)}, f32[1,4968]{1,0:T(1,128)}) custom-call(bf16[16,80,128]{2,1,0:T(8,128)(2,1)S(1)} %all-to-all-done.arrived_ref), custom_call_target="tpu_custom_call" | custom-call | flops 1000000 | bytes 4000000 | tf_op jit(solution)/shard_map/pallas_call | solution.py:523
Async XLA Ops:
  0.6 19.3 %copy-start = (f32[1,79488]{1,0:T(1,128)S(1)}, f32[1,79488]{1,0:T(1,128)}, u32[]{:S(2)}) copy-start(f32[1,79488]{1,0:T(1,128)} %flat_hbm.2) | copy-start | bytes 953860
  0.6 19.2 %copy-start.1 = (bf16[276,384]{1,0:T(8,128)(2,1)S(1)}, bf16[276,384]{1,0:T(8,128)(2,1)}, u32[]{:S(2)}) copy-start(bf16[276,384]{1,0:T(8,128)(2,1)} %constant.30.clone.perm_hbm.perm_ref) | copy-start | bytes 635908
  9.2 14.5 %copy-start.2 = (bf16[192,576]{1,0:T(8,128)(2,1)S(1)}, bf16[192,576]{1,0:T(8,128)(2,1)}, u32[]{:S(2)}) copy-start(bf16[192,576]{1,0:T(8,128)(2,1)} %w_qkv_ref.1) | copy-start | bytes 663556
  9.2 14.5 %copy-start.3 = (bf16[192,192]{1,0:T(8,128)(2,1)S(1)}, bf16[192,192]{1,0:T(8,128)(2,1)}, u32[]{:S(2)}) copy-start(bf16[192,192]{1,0:T(8,128)(2,1)} %w_proj_ref.2) | copy-start | bytes 221188
  9.2 14.5 %copy-start.5 = (f32[192]{0:T(256)S(1)}, f32[192]{0:T(256)}, u32[]{:S(2)}) copy-start(f32[192]{0:T(256)} %param.24) | copy-start | bytes 2308
  9.2 14.5 %copy-start.6 = (bf16[864,144]{1,0:T(8,128)(2,1)S(1)}, bf16[864,144]{1,0:T(8,128)(2,1)}, u32[]{:S(2)}) copy-start(bf16[864,144]{1,0:T(8,128)(2,1)} %constant.27.clone.rep_ref) | copy-start | bytes 746500
  9.2 14.5 %copy-start.7 = (bf16[192,864]{1,0:T(8,128)(2,1)S(1)}, bf16[192,864]{1,0:T(8,128)(2,1)}, u32[]{:S(2)}) copy-start(bf16[192,864]{1,0:T(8,128)(2,1)} %constant.29.clone.mask_t_ref) | copy-start | bytes 995332
  9.2 14.5 %copy-start.8 = (bf16[288,144]{1,0:T(8,128)(2,1)S(1)}, bf16[288,144]{1,0:T(8,128)(2,1)}, u32[]{:S(2)}) copy-start(bf16[288,144]{1,0:T(8,128)(2,1)} %constant.28.clone.twice_hbm.twice_ref) | copy-start | bytes 248836
  9.2 14.5 %copy-start.10 = (bf16[144,144]{1,0:T(8,128)(2,1)S(1)}, bf16[144,144]{1,0:T(8,128)(2,1)}, u32[]{:S(2)}) copy-start(bf16[144,144]{1,0:T(8,128)(2,1)} %constant.34.clone.join_t_ref) | copy-start | bytes 124420
  9.3 14.5 %copy-start.11 = (bf16[144,144]{1,0:T(8,128)(2,1)S(1)}, bf16[144,144]{1,0:T(8,128)(2,1)}, u32[]{:S(2)}) copy-start(bf16[144,144]{1,0:T(8,128)(2,1)} %constant.33.clone.join_ref) | copy-start | bytes 124420
  9.3 13.3 %collective-permute-start = (bf16[144,384]{1,0:T(8,128)(2,1)}, bf16[144,384]{1,0:T(8,128)(2,1)S(1)}, u32[]{:S(2)}, u32[]{:S(2)}) collective-permute-start(bf16[144,384]{1,0:T(8,128)(2,1)} %get-tuple-element.29), channel_id=1, source_target_pairs={{0,15},{1,0},{2,1},{3,2},{4,3},{5,4},{6,5},{7,6},{8,7},{9,8},{10,9... | collective-permute-start | bytes 331784 | tf_op jit(solution)/shard_map/ppermute | solution.py:427
  11.6 11.0 %collective-permute-start.1 = (bf16[144,384]{1,0:T(8,128)(2,1)}, bf16[144,384]{1,0:T(8,128)(2,1)S(1)}, u32[]{:S(2)}, u32[]{:S(2)}) collective-permute-start(bf16[144,384]{1,0:T(8,128)(2,1)} %get-tuple-element.30), channel_id=1, source_target_pairs={{0,240},{16,0},{32,16},{48,32},{64,48},{80,64},{96,80},{112,96},{1... | collective-permute-start | bytes 331784 | tf_op jit(solution)/shard_map/ppermute | solution.py:428
  13.9 9.8 %collective-permute-start.2 = (bf16[144,384]{1,0:T(8,128)(2,1)}, bf16[144,384]{1,0:T(8,128)(2,1)S(1)}, u32[]{:S(2)}, u32[]{:S(2)}) collective-permute-start(bf16[144,384]{1,0:T(8,128)(2,1)} %get-tuple-element.31), channel_id=1, source_target_pairs={{0,255},{1,240},{2,241},{3,242},{4,243},{5,244},{6,245},{7,246},{8... | collective-permute-start | bytes 331784 | tf_op jit(solution)/shard_map/ppermute | solution.py:429
  19.9 3.9 %copy-start.15 = (bf16[144,384]{1,0:T(8,128)(2,1)S(1)}, bf16[144,384]{1,0:T(8,128)(2,1)}, u32[]{:S(2)}) copy-start(bf16[144,384]{1,0:T(8,128)(2,1)} %get-tuple-element.28.stay_ref) | copy-start | bytes 331780
  23.7 13.4 %copy-start.4 = (bf16[192,192]{1,0:T(8,128)(2,1)S(1)}, bf16[192,192]{1,0:T(8,128)(2,1)}, u32[]{:S(2)}) copy-start(bf16[192,192]{1,0:T(8,128)(2,1)} %w_proj_hbm.3) | copy-start | bytes 221188
  23.8 13.3 %copy-start.9 = (bf16[144,144]{1,0:T(8,128)(2,1)S(1)}, bf16[144,144]{1,0:T(8,128)(2,1)}, u32[]{:S(2)}) copy-start(bf16[144,144]{1,0:T(8,128)(2,1)} %constant.31.clone.split_ref) | copy-start | bytes 124420
  23.8 13.3 %copy-start.12 = (bf16[4,144,864]{2,1,0:T(8,128)(2,1)S(1)}, bf16[4,144,864]{2,1,0:T(8,128)(2,1)}, u32[]{:S(2)}) copy-start(bf16[4,144,864]{2,1,0:T(8,128)(2,1)} %get-tuple-element.23.probs_ref.probs_hbm) | copy-start | bytes 2985988
  23.8 13.3 %copy-start.13 = (bf16[4,144,192]{2,1,0:T(8,128)(2,1)S(1)}, bf16[4,144,192]{2,1,0:T(8,128)(2,1)}, u32[]{:S(2)}) copy-start(bf16[4,144,192]{2,1,0:T(8,128)(2,1)} %get-tuple-element.37.v_ref) | copy-start | bytes 663556
  29.3 4.7 %collective-permute-start.3 = (bf16[72,384]{1,0:T(8,128)(2,1)S(1)}, bf16[72,384]{1,0:T(8,128)(2,1)S(1)}, u32[]{:S(2)}, u32[]{:S(2)}) collective-permute-start(bf16[72,384]{1,0:T(8,128)(2,1)S(1)} %get-tuple-element.34), channel_id=1, source_target_pairs={{0,1},{1,2},{2,3},{3,4},{4,5},{5,6},{6,7},{7,8},{8,9},{9,10},{10,1... | collective-permute-start | bytes 165896 | tf_op jit(solution)/shard_map/ppermute | solution.py:427
  29.4 7.5 %collective-permute-start.4 = (bf16[72,384]{1,0:T(8,128)(2,1)S(1)}, bf16[72,384]{1,0:T(8,128)(2,1)S(1)}, u32[]{:S(2)}, u32[]{:S(2)}) collective-permute-start(bf16[72,384]{1,0:T(8,128)(2,1)S(1)} %get-tuple-element.35), channel_id=1, source_target_pairs={{0,16},{16,32},{32,48},{48,64},{64,80},{80,96},{96,112},{112,128},... | collective-permute-start | bytes 165896 | tf_op jit(solution)/shard_map/ppermute | solution.py:428
  29.7 7.5 %collective-permute-start.5 = (bf16[72,384]{1,0:T(8,128)(2,1)S(1)}, bf16[72,384]{1,0:T(8,128)(2,1)S(1)}, u32[]{:S(2)}, u32[]{:S(2)}) collective-permute-start(bf16[72,384]{1,0:T(8,128)(2,1)S(1)} %get-tuple-element.36), channel_id=1, source_target_pairs={{0,17},{1,18},{2,19},{3,20},{4,21},{5,22},{6,23},{7,24},{8,25},{9,... | collective-permute-start | bytes 165896 | tf_op jit(solution)/shard_map/ppermute | solution.py:429
  40.5 0.7 %copy-start.14 = (bf16[4,144,192]{2,1,0:T(8,128)(2,1)}, bf16[4,144,192]{2,1,0:T(8,128)(2,1)S(1)}, u32[]{:S(2)}) copy-start(bf16[4,144,192]{2,1,0:T(8,128)(2,1)S(1)} %get-tuple-element.39.grad_hbm) | copy-start | bytes 663556
  41.2 18.2 %all-to-all-start = ((bf16[16,80,128]{2,1,0:T(8,128)(2,1)}), bf16[16,80,128]{2,1,0:T(8,128)(2,1)S(1)}, u32[]{:S(2)}, u32[]{:S(2)}) async-start(bf16[16,80,128]{2,1,0:T(8,128)(2,1)} %get-tuple-element.40), calls=%async_computation | async-start | bytes 655360 | tf_op jit(solution)/shard_map/all_to_all | solution.py:510

commit v5 on v4

--- a/solution.py
+++ b/solution.py
@@ -89,14 +89,18 @@
     middle = rest.astype(BF16)
     low = (rest - middle.astype(F32)).astype(BF16)
     perm = perm_ref[...]
-    spread_ref[...] = (dot(perm, high, NT) + dot(perm, middle, NT) + dot(perm, low, NT)) * LOG2E
+    spread = (dot(perm, high, NT) + dot(perm, middle, NT) + dot(perm, low, NT)) * LOG2E
+    for v in LEVELS:
+        own = spread[:, v * SLAB : (v + 1) * SLAB]
+        spread_ref[0, v] = own[: ROWS - BAND]
+        spread_ref[1, v] = own[BAND:]
 
 
 def write_bias(spread_ref, bias_ref, apart=None):
     for query_lon in range(WIN_LON):
-        first = (WIN_LON - 1 - query_lon) * BAND
+        first = WIN_LON - 1 - query_lon
         for v in LEVELS:
-            block = spread_ref[first : first + WIN_TOK, v * SLAB : (v + 1) * SLAB]
+            block = spread_ref[first % 2, v, first // 2 * 2 * BAND : first // 2 * 2 * BAND + WIN_TOK, :]
             if apart is not None:
                 block = block + apart
             bias_ref[v, :, query_lon * SLAB : (query_lon + 1) * SLAB] = block
@@ -185,14 +189,11 @@
     return normed, inv_std, *([x[:, k * D : (k + 1) * D] for x in packed] for k in range(3))
 
 
-def forward(inputs, biases, gain, w_qkv, twice):
-    normed, inv_std, q_rows, k_rows, v_rows = project(inputs, gain, w_qkv)
-    q_spread = spread_heads(q_rows, twice)
+def attend(q_spread, k_rows, biases):
     scores = [dot(k, q, NT) * (SCALE * LOG2E) + bias[...] for k, q, bias in zip(k_rows, q_spread, biases)]
     exp_scores = [jnp.exp2(x - jnp.max(x, 0, keepdims=True)) for x in scores]
     attn_probs = [x * (1.0 / jnp.sum(x, 0, keepdims=True)) for x in exp_scores]
-    probs_low = [x.astype(BF16) for x in attn_probs]
-    return normed, inv_std, q_rows, q_spread, k_rows, v_rows, attn_probs, probs_low
+    return attn_probs, [x.astype(BF16) for x in attn_probs]
 
 
 def gathered(values, weights, rep, mask_t):
@@ -234,7 +235,7 @@
     part_a, part_b, part_c, spread_ref, bias_ref, piece_ref, rows_ref, gain_ref,
     tokens_ref, grad_ref, w_qkv_ref, w_proj_ref, twice_ref, perm_ref, split_t_ref, rep_ref, mask_t_ref,
     out_ref, v_ref, probs_ref,
-    table_sem, in_sem, out_sem,
+    table_sem, in_sem, out_sem, keep_sem,
 ):
     table = table_copies(flat_hbm, rows_ref, table_sem)
     for copy in table:
@@ -251,16 +252,17 @@
     for copy in table:
         copy.wait()
     fetch.wait()
+    inputs = load_windows(tokens_ref, picked)
     expand_table(rows_ref, perm_ref, (part_a, part_b, part_c), spread_ref)
+    _, _, q_rows, k_rows, v_rows = project(inputs, gain_ref[...], w_qkv_ref[...])
+    q_spread = spread_heads(q_rows, twice_ref[...])
     write_bias(spread_ref, bias_ref)
-    inputs = load_windows(tokens_ref, picked)
-    _, _, _, _, _, v_rows, _, probs_low = forward(
-        inputs, [bias_ref.at[v] for v in LEVELS], gain_ref[...], w_qkv_ref[...], twice_ref[...]
-    )
+    _, probs_low = attend(q_spread, k_rows, [bias_ref.at[v] for v in LEVELS])
     for v in LEVELS:
         v_ref[v] = v_rows[v]
         probs_ref[v] = probs_low[v]
     grads = [x.astype(BF16) for x in load_windows(grad_ref, picked)]
+    keep = Fetch([(v_ref, v_hbm), (probs_ref, probs_hbm)], keep_sem)
     attended = gathered(v_rows, probs_low, rep_ref[...], mask_t_ref[...])
     split_t = split_t_ref[...]
     for v in LEVELS:
@@ -269,7 +271,9 @@
         piece_ref[:, v * PIECE : (v + 1) * PIECE, D:] = dot(split_t, grads[v]).reshape(4, PIECE, D)
     out_ref[...] = piece_ref[...].astype(BF16)
     pairs = [(out_ref.at[k], ref) for k, ref in enumerate((stay_hbm, lon_hbm, lat_hbm, both_hbm))]
-    Fetch(pairs + [(v_ref, v_hbm), (probs_ref, probs_hbm)], out_sem).wait()
+    sent = Fetch(pairs, out_sem)
+    keep.wait()
+    sent.wait()
 
 
 def bias_kernel(active_ref, flat_hbm, perm_ref, bias_ref, part_a, part_b, part_c, spread_ref, rows_ref, sem):
@@ -300,9 +304,9 @@
     inputs = [x[:, :D] for x in pairs]
     grads = [x[:, D:].astype(BF16) for x in pairs]
     gain, w_proj = gain_ref[...], w_proj_ref[...]
-    normed, inv_std, _, q_spread, k_rows, v_rows, attn_probs, probs_low = forward(
-        inputs, [bias_ref.at[v] for v in LEVELS], gain, w_qkv_ref[...], twice
-    )
+    normed, inv_std, q_rows, k_rows, v_rows = project(inputs, gain, w_qkv_ref[...])
+    q_spread = spread_heads(q_rows, twice)
+    attn_probs, probs_low = attend(q_spread, k_rows, [bias_ref.at[v] for v in LEVELS])
     _, mixed_spread, lows = score_grads(v_rows, attn_probs, grads, w_proj, twice)
     results = input_grads(
         normed, inv_std, q_spread, k_rows, probs_low, mixed_spread, lows, grads, gain, w_qkv_ref, rep_ref[...], mask_t_ref[...]
@@ -447,6 +451,7 @@
     rows = (LEV_WIN, WIN_TOK, D)
     scores = (LEV_WIN, WIN_TOK, LANES)
     parts = [(LEV_WIN * SLAB, FLAT)] * 3
+    spread_rows = (2, LEV_WIN, ROWS - BAND, SLAB)
     folded = (ROWS, LEV_WIN * SLAB)
     table = (LEV_WIN * SLAB, 3 * FLAT)
     tiles = LEV_WIN * SLAB // SHARE
@@ -465,11 +470,11 @@
         out_shape=[jax.ShapeDtypeStruct(shape, BF16) for shape in outs],
         scratch_shapes=[
             pltpu.VMEM(shape, F32)
-            for shape in parts + [folded, scores, (4, LEV_WIN * PIECE, 2 * D), table_rows, (1, D)]
+            for shape in parts + [spread_rows, scores, (4, LEV_WIN * PIECE, 2 * D), table_rows, (1, D)]
         ]
         + [pltpu.VMEM(operands[k].shape, BF16) for k in held]
         + [pltpu.VMEM(shape, BF16) for shape in ((LANES, WIN_TOK), (D, LANES), (4,) + pair[0], rows, scores)]
-        + [pltpu.SemaphoreType.DMA((9,)), pltpu.SemaphoreType.DMA((8,)), pltpu.SemaphoreType.DMA((6,))],
+        + [pltpu.SemaphoreType.DMA((9,)), pltpu.SemaphoreType.DMA((8,)), pltpu.SemaphoreType.DMA((4,)), pltpu.SemaphoreType.DMA((2,))],
         compiler_params=pltpu.CompilerParams(vmem_limit_bytes=ALL_VMEM),
         cost_estimate=pl.CostEstimate(flops=2_000_000_000, bytes_accessed=4_000_000, transcendentals=500_000),
     )(*operands)
@@ -482,7 +487,7 @@
         bias_kernel,
         in_specs=[pl.BlockSpec(memory_space=pltpu.SMEM), HBM, VMEM],
         out_shape=[jax.ShapeDtypeStruct(scores, F32)],
-        scratch_shapes=[pltpu.VMEM(shape, F32) for shape in parts + [folded, table_rows]] + [pltpu.SemaphoreType.DMA((9,))],
+        scratch_shapes=[pltpu.VMEM(shape, F32) for shape in parts + [spread_rows, table_rows]] + [pltpu.SemaphoreType.DMA((9,))],
         compiler_params=pltpu.CompilerParams(vmem_limit_bytes=VMEM_LIMIT),
         cost_estimate=pl.CostEstimate(flops=500_000_000, bytes_accessed=4_000_000, transcendentals=0),
     )(active, bias_two, perm)

time: 61.1 us -> 60 us (0.982)
  Pallas kernels: 29 us -> 27.6 us
    pallas_call x1, Pallas kernels: 8.51 us -> 7.38 us  [body(): pl.pallas_call(first_kernel, in_specs=[HBM] * len(operands), out_specs=[H...]
where the time goes in v5:
time: 60 us; the launch traced here: 59.1 us
  Pallas kernels  27.6 us (46%)
  starting transfers between devices  19.4 us (32%)
  waiting for transfers between devices  10.4 us (17%)
  between operations  0.88 us (1%)
  local copies, waits for them, and re-layouts  0.81 us (1%)
    all_to_all x1, starting transfers between devices, body(): arrived = lax.all_to_all(terms, 'lon', 0, 0, tiled=True)  8.32 us
    pallas_call x1, Pallas kernels, body(): pl.pallas_call(first_kernel, in_specs=[HBM] * len(operands), out_specs=[H...  7.38 us
    pallas_call x1, Pallas kernels, body(): pl.pallas_call(last_kernel, in_specs=[HBM] * len(operands), out_shape=jax...  6.83 us
    ppermute x2, starting transfers between devices, exchange(): lax.ppermute(both, ('lat', 'lon'), shifted(('lat', 'lon'), by))  6.29 us
    pallas_call x1, Pallas kernels, body(): call(second_kernel, [single] * 4 + [(scores, BF16)], [(LEV_WIN, WIN_TOK,...  5.48 us
    pallas_call x1, Pallas kernels, body(): call(third_kernel, [((tiles, 2 * TERM, FLAT), BF16), (rows, BF16)], [rows...  3.41 us
    ppermute x2, waiting for transfers between devices, exchange(): lax.ppermute(lat, ('lat',), shifted(('lat',), by))  3.15 us
    all_to_all x1, waiting for transfers between devices, body(): arrived = lax.all_to_all(terms, 'lon', 0, 0, tiled=True)  3 us
  transfers between devices with their start and end apart: 7, of which 5 were waited for; matrix products, arithmetic and copies ran while one was open for 0% of the time, Pallas kernels for 18%

profile of v5, /device:TPU:2, one launch (start us, length us, event | category | flops | bytes accessed | tf_op | source)
XLA Modules:
  0.0 59.1 jit_solution(17591069492002899549)
XLA Ops:
  0.6 0.0 copy-start
  0.6 0.0 copy-start.1
  0.7 7.4 %shard_map.193 = (bf16[144,384]{1,0:T(8,128)(2,1)}, bf16[144,384]{1,0:T(8,128)(2,1)}, bf16[144,384]{1,0:T(8,128)(2,1)}, bf16[144,384]{1,0:T(8,128)(2,1)}, bf16[4...) custom-call(bf16[72,8,192]{2,1,0:T(8,128)(2,1)} %bitcast.14, bf16[72,8,192]{2,1,0:T(8,128)(2,1)} %bitcast.13, ...), custom_call_target="tpu_custom_call" | custom-call | flops 2000000000 | bytes 4000000 | tf_op jit(solution)/shard_map/pallas_call | solution.py:466
  8.0 0.0 copy-start.2
  8.1 0.0 copy-start.3
  8.1 0.0 copy-start.5
  8.1 0.0 copy-start.6
  8.1 0.0 copy-start.7
  8.1 0.0 copy-start.8
  8.1 0.0 copy-start.10
  8.1 0.0 copy-start.11
  8.1 2.3 %collective-permute-start = (bf16[144,384]{1,0:T(8,128)(2,1)}, bf16[144,384]{1,0:T(8,128)(2,1)S(1)}, u32[]{:S(2)}, u32[]{:S(2)}) collective-permute-start(bf16[144,384]{1,0:T(8,128)(2,1)} %get-tuple-element.29), channel_id=1, source_target_pairs={{0,15},{1,0},{2,1},{3,2},{4,3},{5,4},{6,5},{7,6},{8,7},{9,8},{10,9... | collective-permute-start | bytes 331784 | tf_op jit(solution)/shard_map/ppermute | solution.py:431
  10.5 2.3 %collective-permute-start.1 = (bf16[144,384]{1,0:T(8,128)(2,1)}, bf16[144,384]{1,0:T(8,128)(2,1)S(1)}, u32[]{:S(2)}, u32[]{:S(2)}) collective-permute-start(bf16[144,384]{1,0:T(8,128)(2,1)} %get-tuple-element.30), channel_id=1, source_target_pairs={{0,240},{16,0},{32,16},{48,32},{64,48},{80,64},{96,80},{112,96},{1... | collective-permute-start | bytes 331784 | tf_op jit(solution)/shard_map/ppermute | solution.py:432
  12.8 6.0 %collective-permute-start.2 = (bf16[144,384]{1,0:T(8,128)(2,1)}, bf16[144,384]{1,0:T(8,128)(2,1)S(1)}, u32[]{:S(2)}, u32[]{:S(2)}) collective-permute-start(bf16[144,384]{1,0:T(8,128)(2,1)} %get-tuple-element.31), channel_id=1, source_target_pairs={{0,255},{1,240},{2,241},{3,242},{4,243},{5,244},{6,245},{7,246},{8... | collective-permute-start | bytes 331784 | tf_op jit(solution)/shard_map/ppermute | solution.py:433
  18.8 0.0 copy-start.15
  18.8 0.0 copy-done
  18.8 0.0 copy-done.1
  18.8 2.5 %shard_map.194.bias_ref = f32[4,144,864]{2,1,0:T(8,128)S(1)} custom-call(f32[1,1]{1,0:T(1,128)} %bitcast.6.active_ref, f32[1,79488]{1,0:T(1,128)S(1)} %copy-done, bf16[276,384]{1,0:T(8,128)(2,1)S(1)} %copy-done.1), custom_call_target="tpu_custom_call" | custom-call | flops 500000000 | bytes 4000000 | tf_op jit(solution)/shard_map/pallas_call | solution.py:486
  21.2 0.0 collective-permute-done.lon_ref
  21.2 0.0 collective-permute-done.1.lat_ref
  21.3 1.3 %collective-permute-done.2.both_ref = bf16[144,384]{1,0:T(8,128)(2,1)S(1)} collective-permute-done((bf16[144,384]{1,0:T(8,128)(2,1)}, bf16[144,384]{1,0:T(8,128)(2,1)S(1)}, u32[]{:S(2)}, u32[]{:S(2)}) %collective-permute-start.2) | collective-permute-done | bytes 110624 | tf_op jit(solution)/shard_map/ppermute | solution.py:433
  22.6 0.0 copy-done.2
  22.6 0.0 copy-done.3
  22.6 0.0 copy-done.5
  22.6 0.0 copy-done.6
  22.6 0.0 copy-done.7
  22.6 0.0 copy-done.8
  22.6 0.0 copy-done.10
  22.6 0.0 copy-done.11
  22.6 0.0 copy-done.15
  22.6 0.0 copy-start.4
  22.6 0.0 copy-start.9
  22.6 0.0 copy-start.12
  22.7 0.0 copy-start.13
  22.7 5.5 %shard_map.195 = (bf16[72,384]{1,0:T(8,128)(2,1)S(1)}, bf16[72,384]{1,0:T(8,128)(2,1)S(1)}, bf16[72,384]{1,0:T(8,128)(2,1)S(1)}, bf16[72,384]{1,0:T(8,128)(2,1)S(1)}, bf16[4,144,864]{2,1,0:T(8,128)(2,1)S(1)}) custom-call(bf16[144,384]{1,0:T(8,128)(2,1)S(1)} %copy-done.15, bf16[144,384]{1,0:T(8,128)(2,1)S(1)} %collective-permute-done.lon_ref, ...), custom_call_target="tpu_custom_call" | custom-call | flops 4000000000 | bytes 4000000 | tf_op jit(solution)/shard_map/pallas_call | solution.py:495
  28.2 0.1 collective-permute-start.3
  28.2 0.1 collective-permute-start.4
  28.3 0.3 collective-permute-start.5
  28.6 1.2 %shard_map.196.other_ref = f32[16,40,128]{2,1,0:T(8,128)S(1)} custom-call(bf16[4,144,864]{2,1,0:T(8,128)(2,1)S(1)} %get-tuple-element.38.low_ref, bf16[276,384]{1,0:T(8,128)(2,1)S(1)} %copy-done.1), custom_call_target="tpu_custom_call" | custom-call | flops 500000000 | bytes 4000000 | tf_op jit(solution)/shard_map/pallas_call | solution.py:504
  29.9 2.7 %collective-permute-done.3.lon_ref = bf16[72,384]{1,0:T(8,128)(2,1)S(1)} collective-permute-done((bf16[72,384]{1,0:T(8,128)(2,1)S(1)}, bf16[72,384]{1,0:T(8,128)(2,1)S(1)}, u32[]{:S(2)}, u32[]{:S(2)}) %collective-permute-start.3) | collective-permute-done | bytes 55328 | tf_op jit(solution)/shard_map/ppermute | solution.py:431
  32.6 3.1 %collective-permute-done.4.lat_ref = bf16[72,384]{1,0:T(8,128)(2,1)S(1)} collective-permute-done((bf16[72,384]{1,0:T(8,128)(2,1)S(1)}, bf16[72,384]{1,0:T(8,128)(2,1)S(1)}, u32[]{:S(2)}, u32[]{:S(2)}) %collective-permute-start.4) | collective-permute-done | bytes 55328 | tf_op jit(solution)/shard_map/ppermute | solution.py:432
  35.7 0.3 collective-permute-done.5.both_ref
  36.0 0.0 copy-done.4
  36.0 0.0 copy-done.9
  36.0 0.0 copy-done.12
  36.0 0.0 copy-done.13
  36.0 3.4 %shard_map.197 = (bf16[16,80,128]{2,1,0:T(8,128)(2,1)}, bf16[4,144,192]{2,1,0:T(8,128)(2,1)S(1)}) custom-call(bf16[72,384]{1,0:T(8,128)(2,1)S(1)} %get-tuple-element.33.stay_ref, bf16[72,384]{1,0:T(8,128)(2,1)S(1)} %collective-permute-done.3.lon_ref, bf16[72,384]{1,0:T(8,128)(2,1)S(1)} %collective-permute-done.4.lat_ref, ...), custom_call_target="tpu_custom_call" | custom-call | flops 2000000000 | bytes 4000000 | tf_op jit(solution)/shard_map/pallas_call | solution.py:508
  39.4 0.0 copy-start.14
  39.4 0.7 %copy-done.14 = bf16[4,144,192]{2,1,0:T(8,128)(2,1)} copy-done((bf16[4,144,192]{2,1,0:T(8,128)(2,1)}, bf16[4,144,192]{2,1,0:T(8,128)(2,1)S(1)}, u32[]{:S(2)}) %copy-start.14) | copy-done | bytes 221208
  40.1 8.3 %all-to-all-start = ((bf16[16,80,128]{2,1,0:T(8,128)(2,1)}), bf16[16,80,128]{2,1,0:T(8,128)(2,1)S(1)}, u32[]{:S(2)}, u32[]{:S(2)}) async-start(bf16[16,80,128]{2,1,0:T(8,128)(2,1)} %get-tuple-element.40), calls=%async_computation | async-start | bytes 655360 | tf_op jit(solution)/shard_map/all_to_all | solution.py:515
  48.5 6.8 %shard_map.198 = bf16[72,8,192]{2,1,0:T(8,128)(2,1)} custom-call(bf16[72,8,192]{2,1,0:T(8,128)(2,1)} %bitcast.15, bf16[4,144,864]{2,1,0:T(8,128)(2,1)} %get-tuple-element.23.probs_ref.probs_hbm, bf16[4,144,192]{2,1,0:T(8,128)(2,1)} %copy-done.14, f32[1,192]{1,0:T(1,128)} %bitcast.17, bf16[192,576]{1,0:T(8,128)(2,1)} %w_qkv_hbm.3, ...), custom_call_target="tpu_custom_call" | custom-call | flops 3000000000 | bytes 5000000 | tf_op jit(solution)/shard_map/pallas_call | solution.py:517
  55.3 3.0 %all-to-all-done.arrived_ref = bf16[16,80,128]{2,1,0:T(8,128)(2,1)S(1)} async-done(((bf16[16,80,128]{2,1,0:T(8,128)(2,1)}), bf16[16,80,128]{2,1,0:T(8,128)(2,1)S(1)}, u32[]{:S(2)}, u32[]{:S(2)}) %all-to-all-start) | async-done | bytes 327712 | tf_op jit(solution)/shard_map/all_to_all | solution.py:515
  58.3 0.8 %shard_map.199 = (f32[1,4968]{1,0:T(1,128)}, f32[1,4968]{1,0:T(1,128)}) custom-call(bf16[16,80,128]{2,1,0:T(8,128)(2,1)S(1)} %all-to-all-done.arrived_ref), custom_call_target="tpu_custom_call" | custom-call | flops 1000000 | bytes 4000000 | tf_op jit(solution)/shard_map/pallas_call | solution.py:528
Async XLA Ops:
  0.6 18.1 %copy-start = (f32[1,79488]{1,0:T(1,128)S(1)}, f32[1,79488]{1,0:T(1,128)}, u32[]{:S(2)}) copy-start(f32[1,79488]{1,0:T(1,128)} %flat_hbm.2) | copy-start | bytes 953860
  0.6 18.1 %copy-start.1 = (bf16[276,384]{1,0:T(8,128)(2,1)S(1)}, bf16[276,384]{1,0:T(8,128)(2,1)}, u32[]{:S(2)}) copy-start(bf16[276,384]{1,0:T(8,128)(2,1)} %constant.30.clone.perm_hbm.perm_ref) | copy-start | bytes 635908
  8.0 14.5 %copy-start.2 = (bf16[192,576]{1,0:T(8,128)(2,1)S(1)}, bf16[192,576]{1,0:T(8,128)(2,1)}, u32[]{:S(2)}) copy-start(bf16[192,576]{1,0:T(8,128)(2,1)} %w_qkv_ref.1) | copy-start | bytes 663556
  8.1 14.5 %copy-start.3 = (bf16[192,192]{1,0:T(8,128)(2,1)S(1)}, bf16[192,192]{1,0:T(8,128)(2,1)}, u32[]{:S(2)}) copy-start(bf16[192,192]{1,0:T(8,128)(2,1)} %w_proj_ref.2) | copy-start | bytes 221188
  8.1 14.5 %copy-start.5 = (f32[192]{0:T(256)S(1)}, f32[192]{0:T(256)}, u32[]{:S(2)}) copy-start(f32[192]{0:T(256)} %param.24) | copy-start | bytes 2308
  8.1 14.5 %copy-start.6 = (bf16[864,144]{1,0:T(8,128)(2,1)S(1)}, bf16[864,144]{1,0:T(8,128)(2,1)}, u32[]{:S(2)}) copy-start(bf16[864,144]{1,0:T(8,128)(2,1)} %constant.27.clone.rep_ref) | copy-start | bytes 746500
  8.1 14.5 %copy-start.7 = (bf16[192,864]{1,0:T(8,128)(2,1)S(1)}, bf16[192,864]{1,0:T(8,128)(2,1)}, u32[]{:S(2)}) copy-start(bf16[192,864]{1,0:T(8,128)(2,1)} %constant.29.clone.mask_t_ref) | copy-start | bytes 995332
  8.1 14.5 %copy-start.8 = (bf16[288,144]{1,0:T(8,128)(2,1)S(1)}, bf16[288,144]{1,0:T(8,128)(2,1)}, u32[]{:S(2)}) copy-start(bf16[288,144]{1,0:T(8,128)(2,1)} %constant.28.clone.twice_hbm.twice_ref) | copy-start | bytes 248836
  8.1 14.5 %copy-start.10 = (bf16[144,144]{1,0:T(8,128)(2,1)S(1)}, bf16[144,144]{1,0:T(8,128)(2,1)}, u32[]{:S(2)}) copy-start(bf16[144,144]{1,0:T(8,128)(2,1)} %constant.34.clone.join_t_ref) | copy-start | bytes 124420
  8.1 14.5 %copy-start.11 = (bf16[144,144]{1,0:T(8,128)(2,1)S(1)}, bf16[144,144]{1,0:T(8,128)(2,1)}, u32[]{:S(2)}) copy-start(bf16[144,144]{1,0:T(8,128)(2,1)} %constant.33.clone.join_ref) | copy-start | bytes 124420
  8.1 13.1 %collective-permute-start = (bf16[144,384]{1,0:T(8,128)(2,1)}, bf16[144,384]{1,0:T(8,128)(2,1)S(1)}, u32[]{:S(2)}, u32[]{:S(2)}) collective-permute-start(bf16[144,384]{1,0:T(8,128)(2,1)} %get-tuple-element.29), channel_id=1, source_target_pairs={{0,15},{1,0},{2,1},{3,2},{4,3},{5,4},{6,5},{7,6},{8,7},{9,8},{10,9... | collective-permute-start | bytes 331784 | tf_op jit(solution)/shard_map/ppermute | solution.py:431
  10.5 10.8 %collective-permute-start.1 = (bf16[144,384]{1,0:T(8,128)(2,1)}, bf16[144,384]{1,0:T(8,128)(2,1)S(1)}, u32[]{:S(2)}, u32[]{:S(2)}) collective-permute-start(bf16[144,384]{1,0:T(8,128)(2,1)} %get-tuple-element.30), channel_id=1, source_target_pairs={{0,240},{16,0},{32,16},{48,32},{64,48},{80,64},{96,80},{112,96},{1... | collective-permute-start | bytes 331784 | tf_op jit(solution)/shard_map/ppermute | solution.py:432
  12.8 9.8 %collective-permute-start.2 = (bf16[144,384]{1,0:T(8,128)(2,1)}, bf16[144,384]{1,0:T(8,128)(2,1)S(1)}, u32[]{:S(2)}, u32[]{:S(2)}) collective-permute-start(bf16[144,384]{1,0:T(8,128)(2,1)} %get-tuple-element.31), channel_id=1, source_target_pairs={{0,255},{1,240},{2,241},{3,242},{4,243},{5,244},{6,245},{7,246},{8... | collective-permute-start | bytes 331784 | tf_op jit(solution)/shard_map/ppermute | solution.py:433
  18.8 3.9 %copy-start.15 = (bf16[144,384]{1,0:T(8,128)(2,1)S(1)}, bf16[144,384]{1,0:T(8,128)(2,1)}, u32[]{:S(2)}) copy-start(bf16[144,384]{1,0:T(8,128)(2,1)} %get-tuple-element.28.stay_ref) | copy-start | bytes 331780
  22.6 13.4 %copy-start.4 = (bf16[192,192]{1,0:T(8,128)(2,1)S(1)}, bf16[192,192]{1,0:T(8,128)(2,1)}, u32[]{:S(2)}) copy-start(bf16[192,192]{1,0:T(8,128)(2,1)} %w_proj_hbm.3) | copy-start | bytes 221188
  22.6 13.4 %copy-start.9 = (bf16[144,144]{1,0:T(8,128)(2,1)S(1)}, bf16[144,144]{1,0:T(8,128)(2,1)}, u32[]{:S(2)}) copy-start(bf16[144,144]{1,0:T(8,128)(2,1)} %constant.31.clone.split_ref) | copy-start | bytes 124420
  22.6 13.4 %copy-start.12 = (bf16[4,144,864]{2,1,0:T(8,128)(2,1)S(1)}, bf16[4,144,864]{2,1,0:T(8,128)(2,1)}, u32[]{:S(2)}) copy-start(bf16[4,144,864]{2,1,0:T(8,128)(2,1)} %get-tuple-element.23.probs_ref.probs_hbm) | copy-start | bytes 2985988
  22.7 13.4 %copy-start.13 = (bf16[4,144,192]{2,1,0:T(8,128)(2,1)S(1)}, bf16[4,144,192]{2,1,0:T(8,128)(2,1)}, u32[]{:S(2)}) copy-start(bf16[4,144,192]{2,1,0:T(8,128)(2,1)} %get-tuple-element.37.v_ref) | copy-start | bytes 663556
  28.2 4.4 %collective-permute-start.3 = (bf16[72,384]{1,0:T(8,128)(2,1)S(1)}, bf16[72,384]{1,0:T(8,128)(2,1)S(1)}, u32[]{:S(2)}, u32[]{:S(2)}) collective-permute-start(bf16[72,384]{1,0:T(8,128)(2,1)S(1)} %get-tuple-element.34), channel_id=1, source_target_pairs={{0,1},{1,2},{2,3},{3,4},{4,5},{5,6},{6,7},{7,8},{8,9},{9,10},{10,1... | collective-permute-start | bytes 165896 | tf_op jit(solution)/shard_map/ppermute | solution.py:431
  28.2 7.5 %collective-permute-start.4 = (bf16[72,384]{1,0:T(8,128)(2,1)S(1)}, bf16[72,384]{1,0:T(8,128)(2,1)S(1)}, u32[]{:S(2)}, u32[]{:S(2)}) collective-permute-start(bf16[72,384]{1,0:T(8,128)(2,1)S(1)} %get-tuple-element.35), channel_id=1, source_target_pairs={{0,16},{16,32},{32,48},{48,64},{64,80},{80,96},{96,112},{112,128},... | collective-permute-start | bytes 165896 | tf_op jit(solution)/shard_map/ppermute | solution.py:432
  28.3 7.7 %collective-permute-start.5 = (bf16[72,384]{1,0:T(8,128)(2,1)S(1)}, bf16[72,384]{1,0:T(8,128)(2,1)S(1)}, u32[]{:S(2)}, u32[]{:S(2)}) collective-permute-start(bf16[72,384]{1,0:T(8,128)(2,1)S(1)} %get-tuple-element.36), channel_id=1, source_target_pairs={{0,17},{1,18},{2,19},{3,20},{4,21},{5,22},{6,23},{7,24},{8,25},{9,... | collective-permute-start | bytes 165896 | tf_op jit(solution)/shard_map/ppermute | solution.py:433
  39.4 0.7 %copy-start.14 = (bf16[4,144,192]{2,1,0:T(8,128)(2,1)}, bf16[4,144,192]{2,1,0:T(8,128)(2,1)S(1)}, u32[]{:S(2)}) copy-start(bf16[4,144,192]{2,1,0:T(8,128)(2,1)S(1)} %get-tuple-element.39.grad_hbm) | copy-start | bytes 663556
  40.1 18.2 %all-to-all-start = ((bf16[16,80,128]{2,1,0:T(8,128)(2,1)}), bf16[16,80,128]{2,1,0:T(8,128)(2,1)S(1)}, u32[]{:S(2)}, u32[]{:S(2)}) async-start(bf16[16,80,128]{2,1,0:T(8,128)(2,1)} %get-tuple-element.40), calls=%async_computation | async-start | bytes 655360 | tf_op jit(solution)/shard_map/all_to_all | solution.py:515

commit v6 on v5

--- a/solution.py
+++ b/solution.py
@@ -344,21 +344,11 @@
 
 
 def last_kernel(
-    tokens_hbm, probs_hbm, grad_hbm, gain_hbm, w_qkv_hbm, w_proj_hbm, twice_hbm,
+    tokens_ref, probs_ref, grad_ref, gain_ref, w_qkv_ref, w_proj_ref, twice_ref,
     grid_ref,
-    tokens_ref, probs_ref, grad_ref, gain_ref, w_qkv_ref, w_proj_ref, twice_ref,
-    sem,
 ):
-    fetch = Fetch(
-        (
-            (tokens_hbm, tokens_ref), (gain_hbm, gain_ref), (w_qkv_hbm, w_qkv_ref), (twice_hbm, twice_ref), (w_proj_hbm, w_proj_ref),
-            (grad_hbm, grad_ref), (probs_hbm, probs_ref),
-        ),
-        sem,
-    )
     picked = picks()
     rep, mask_t = spreaders()
-    fetch.wait()
     twice, gain = twice_ref[...], gain_ref[...]
     normed, inv_std, q_rows, k_rows, v_rows = project(load_windows(tokens_ref, picked), gain, w_qkv_ref[...])
     grads = [grad_ref[v] for v in LEVELS]
@@ -514,15 +504,7 @@
 
     arrived = lax.all_to_all(terms, "lon", 0, 0, tiled=True)
     operands = (level_last(tokens), probs, grads, gain_one.reshape(1, D), qkv_one, proj_one, const["twice"])
-    grid_out = pl.pallas_call(
-        last_kernel,
-        in_specs=[HBM] * len(operands),
-        out_shape=jax.ShapeDtypeStruct(columns, BF16),
-        scratch_shapes=[pltpu.VMEM(x.shape, x.dtype) for x in operands]
-        + [pltpu.SemaphoreType.DMA((len(operands),))],
-        compiler_params=pltpu.CompilerParams(vmem_limit_bytes=ALL_VMEM),
-        cost_estimate=pl.CostEstimate(flops=3_000_000_000, bytes_accessed=5_000_000, transcendentals=0),
-    )(*operands)
+    (grid_out,) = call(last_kernel, [(columns, BF16)], [], 3_000_000_000)(*operands)
     grad_tokens = grid_out.reshape(WIN_LAT, WIN_LON, LEV, D).transpose(2, 0, 1, 3)
     width = SHARE * ROWS
     summed_one, summed_two = call(

time: 60 us -> 59.3 us (0.988)
  Pallas kernels: 27.6 us -> 26.3 us
    pallas_call x1, Pallas kernels: 6.83 us -> 5.58 us  [body(): grid_out, = call(last_kernel, [(columns, BF16)], [], 3000000000)(*operands)]
    unnamed x32 -> x38, local copies, waits for them, and re-layouts: 0.81 us -> 1.32 us
  transfers between devices with their start and end apart: 7 -> 7, of which waited for: 5 -> 5; matrix products, arithmetic and copies ran while one was open for 0% -> 0% of each run, Pallas kernels for 18% -> 16%
where the time goes in v6:
time: 59.3 us; the launch traced here: 58.4 us
  Pallas kernels  26.3 us (44%)
  starting transfers between devices  19.4 us (33%)
  waiting for transfers between devices  10.4 us (18%)
  local copies, waits for them, and re-layouts  1.32 us (2%)
  between operations  0.93 us (2%)
    all_to_all x1, starting transfers between devices, body(): arrived = lax.all_to_all(terms, 'lon', 0, 0, tiled=True)  8.32 us
    pallas_call x1, Pallas kernels, body(): pl.pallas_call(first_kernel, in_specs=[HBM] * len(operands), out_specs=[H...  7.37 us
    ppermute x2, starting transfers between devices, exchange(): lax.ppermute(both, ('lat', 'lon'), shifted(('lat', 'lon'), by))  6.29 us
    pallas_call x1, Pallas kernels, body(): grid_out, = call(last_kernel, [(columns, BF16)], [], 3000000000)(*operands)  5.58 us
    pallas_call x1, Pallas kernels, body(): call(second_kernel, [single] * 4 + [(scores, BF16)], [(LEV_WIN, WIN_TOK,...  5.43 us
    pallas_call x1, Pallas kernels, body(): call(third_kernel, [((tiles, 2 * TERM, FLAT), BF16), (rows, BF16)], [rows...  3.39 us
    ppermute x2, waiting for transfers between devices, exchange(): lax.ppermute(lat, ('lat',), shifted(('lat',), by))  3.15 us
    all_to_all x1, waiting for transfers between devices, body(): arrived = lax.all_to_all(terms, 'lon', 0, 0, tiled=True)  3.02 us
  transfers between devices with their start and end apart: 7, of which 5 were waited for; matrix products, arithmetic and copies ran while one was open for 0% of the time, Pallas kernels for 16%

profile of v6, /device:TPU:2, one launch (start us, length us, event | category | flops | bytes accessed | tf_op | source)
XLA Modules:
  0.0 58.4 jit_solution(1942276613694046767)
XLA Ops:
  0.6 0.0 copy-start
  0.6 0.0 copy-start.1
  0.7 7.4 %shard_map.193 = (bf16[144,384]{1,0:T(8,128)(2,1)}, bf16[144,384]{1,0:T(8,128)(2,1)}, bf16[144,384]{1,0:T(8,128)(2,1)}, bf16[144,384]{1,0:T(8,128)(2,1)}, bf16[4...) custom-call(bf16[72,8,192]{2,1,0:T(8,128)(2,1)} %bitcast.12, bf16[72,8,192]{2,1,0:T(8,128)(2,1)} %bitcast.17, ...), custom_call_target="tpu_custom_call" | custom-call | flops 2000000000 | bytes 4000000 | tf_op jit(solution)/shard_map/pallas_call | solution.py:456
  8.0 0.0 copy-start.3
  8.0 0.0 copy-start.5
  8.1 0.0 copy-start.7
  8.1 0.0 copy-start.9
  8.1 0.0 copy-start.10
  8.1 0.0 copy-start.11
  8.1 0.0 copy-start.13
  8.1 0.0 copy-start.14
  8.1 0.0 copy-start.18
  8.1 2.3 %collective-permute-start = (bf16[144,384]{1,0:T(8,128)(2,1)}, bf16[144,384]{1,0:T(8,128)(2,1)S(1)}, u32[]{:S(2)}, u32[]{:S(2)}) collective-permute-start(bf16[144,384]{1,0:T(8,128)(2,1)} %get-tuple-element.29), channel_id=1, source_target_pairs={{0,15},{1,0},{2,1},{3,2},{4,3},{5,4},{6,5},{7,6},{8,7},{9,8},{10,9... | collective-permute-start | bytes 331784 | tf_op jit(solution)/shard_map/ppermute | solution.py:421
  10.5 2.3 %collective-permute-start.1 = (bf16[144,384]{1,0:T(8,128)(2,1)}, bf16[144,384]{1,0:T(8,128)(2,1)S(1)}, u32[]{:S(2)}, u32[]{:S(2)}) collective-permute-start(bf16[144,384]{1,0:T(8,128)(2,1)} %get-tuple-element.30), channel_id=1, source_target_pairs={{0,240},{16,0},{32,16},{48,32},{64,48},{80,64},{96,80},{112,96},{1... | collective-permute-start | bytes 331784 | tf_op jit(solution)/shard_map/ppermute | solution.py:422
  12.8 6.0 %collective-permute-start.2 = (bf16[144,384]{1,0:T(8,128)(2,1)}, bf16[144,384]{1,0:T(8,128)(2,1)S(1)}, u32[]{:S(2)}, u32[]{:S(2)}) collective-permute-start(bf16[144,384]{1,0:T(8,128)(2,1)} %get-tuple-element.31), channel_id=1, source_target_pairs={{0,255},{1,240},{2,241},{3,242},{4,243},{5,244},{6,245},{7,246},{8... | collective-permute-start | bytes 331784 | tf_op jit(solution)/shard_map/ppermute | solution.py:423
  18.8 0.0 copy-done
  18.8 0.0 copy-done.1
  18.8 2.5 %shard_map.194.bias_ref = f32[4,144,864]{2,1,0:T(8,128)S(1)} custom-call(f32[1,1]{1,0:T(1,128)} %bitcast.6.active_ref, f32[1,79488]{1,0:T(1,128)S(1)} %copy-done, bf16[276,384]{1,0:T(8,128)(2,1)S(1)} %copy-done.1), custom_call_target="tpu_custom_call" | custom-call | flops 500000000 | bytes 4000000 | tf_op jit(solution)/shard_map/pallas_call | solution.py:476
  21.2 0.0 collective-permute-done.lon_ref
  21.2 0.0 collective-permute-done.1.lat_ref
  21.3 1.3 %collective-permute-done.2.both_ref = bf16[144,384]{1,0:T(8,128)(2,1)S(1)} collective-permute-done((bf16[144,384]{1,0:T(8,128)(2,1)}, bf16[144,384]{1,0:T(8,128)(2,1)S(1)}, u32[]{:S(2)}, u32[]{:S(2)}) %collective-permute-start.2) | collective-permute-done | bytes 110624 | tf_op jit(solution)/shard_map/ppermute | solution.py:423
  22.6 0.0 copy-done.3
  22.6 0.0 copy-done.5
  22.6 0.0 copy-done.7
  22.6 0.0 copy-done.9
  22.6 0.0 copy-done.10
  22.6 0.0 copy-done.11
  22.6 0.0 copy-done.13
  22.6 0.0 copy-done.14
  22.6 0.0 copy-done.18
  22.6 0.0 copy-start.6
  22.6 0.0 copy-start.12
  22.6 0.0 copy-start.15
  22.7 0.0 copy-start.17
  22.7 5.4 %shard_map.195 = (bf16[72,384]{1,0:T(8,128)(2,1)S(1)}, bf16[72,384]{1,0:T(8,128)(2,1)S(1)}, bf16[72,384]{1,0:T(8,128)(2,1)S(1)}, bf16[72,384]{1,0:T(8,128)(2,1)S(1)}, bf16[4,144,864]{2,1,0:T(8,128)(2,1)S(1)}) custom-call(bf16[144,384]{1,0:T(8,128)(2,1)S(1)} %copy-done.18, bf16[144,384]{1,0:T(8,128)(2,1)S(1)} %collective-permute-done.lon_ref, ...), custom_call_target="tpu_custom_call" | custom-call | flops 4000000000 | bytes 4000000 | tf_op jit(solution)/shard_map/pallas_call | solution.py:485
  28.1 0.1 collective-permute-start.3
  28.2 0.1 collective-permute-start.4
  28.3 0.3 collective-permute-start.5
  28.6 1.2 %shard_map.196.other_ref = f32[16,40,128]{2,1,0:T(8,128)S(1)} custom-call(bf16[4,144,864]{2,1,0:T(8,128)(2,1)S(1)} %get-tuple-element.38.low_ref, bf16[276,384]{1,0:T(8,128)(2,1)S(1)} %copy-done.1), custom_call_target="tpu_custom_call" | custom-call | flops 500000000 | bytes 4000000 | tf_op jit(solution)/shard_map/pallas_call | solution.py:494
  29.9 2.7 %collective-permute-done.3.lon_ref = bf16[72,384]{1,0:T(8,128)(2,1)S(1)} collective-permute-done((bf16[72,384]{1,0:T(8,128)(2,1)S(1)}, bf16[72,384]{1,0:T(8,128)(2,1)S(1)}, u32[]{:S(2)}, u32[]{:S(2)}) %collective-permute-start.3) | collective-permute-done | bytes 55328 | tf_op jit(solution)/shard_map/ppermute | solution.py:421
  32.5 3.1 %collective-permute-done.4.lat_ref = bf16[72,384]{1,0:T(8,128)(2,1)S(1)} collective-permute-done((bf16[72,384]{1,0:T(8,128)(2,1)S(1)}, bf16[72,384]{1,0:T(8,128)(2,1)S(1)}, u32[]{:S(2)}, u32[]{:S(2)}) %collective-permute-start.4) | collective-permute-done | bytes 55328 | tf_op jit(solution)/shard_map/ppermute | solution.py:422
  35.7 0.3 collective-permute-done.5.both_ref
  36.0 0.0 copy-done.6
  36.0 0.0 copy-done.12
  36.0 0.0 copy-done.15
  36.0 0.0 copy-done.17
  36.0 0.0 copy-start.2
  36.0 0.0 copy-start.4
  36.0 0.0 copy-start.8
  36.0 3.4 %shard_map.197 = (bf16[16,80,128]{2,1,0:T(8,128)(2,1)}, bf16[4,144,192]{2,1,0:T(8,128)(2,1)S(1)}) custom-call(bf16[72,384]{1,0:T(8,128)(2,1)S(1)} %get-tuple-element.33.stay_ref, bf16[72,384]{1,0:T(8,128)(2,1)S(1)} %collective-permute-done.3.lon_ref, bf16[72,384]{1,0:T(8,128)(2,1)S(1)} %collective-permute-done.4.lat_ref, ...), custom_call_target="tpu_custom_call" | custom-call | flops 2000000000 | bytes 4000000 | tf_op jit(solution)/shard_map/pallas_call | solution.py:498
  39.4 8.3 %all-to-all-start = ((bf16[16,80,128]{2,1,0:T(8,128)(2,1)}), bf16[16,80,128]{2,1,0:T(8,128)(2,1)S(1)}, u32[]{:S(2)}, u32[]{:S(2)}) async-start(bf16[16,80,128]{2,1,0:T(8,128)(2,1)} %get-tuple-element.40), calls=%async_computation | async-start | bytes 655360 | tf_op jit(solution)/shard_map/all_to_all | solution.py:505
  47.7 0.0 copy-done.2
  47.7 0.0 copy-done.4
  47.7 0.0 copy-done.8
  47.8 0.0 copy-start.16
  47.8 1.2 %copy-done.16 = bf16[4,144,864]{2,1,0:T(8,128)(2,1)S(1)} copy-done((bf16[4,144,864]{2,1,0:T(8,128)(2,1)S(1)}, bf16[4,144,864]{2,1,0:T(8,128)(2,1)}, u32[]{:S(2)}) %copy-start.16) | copy-done | bytes 995352
  49.0 5.6 %shard_map.198 = bf16[72,8,192]{2,1,0:T(8,128)(2,1)} custom-call(bf16[72,8,192]{2,1,0:T(8,128)(2,1)S(1)} %bitcast.13, bf16[4,144,864]{2,1,0:T(8,128)(2,1)S(1)} %copy-done.16, bf16[4,144,192]{2,1,0:T(8,128)(2,1)S(1)} %get-tuple-element.39.grad_ref, f32[1,192]{1,0:T(1,128)S(1)} %bitcast.16, bf16[192,576]{1,0:T(8,128)(2,1)S(1)} %copy-done.4, ...), custom_call_target="tpu_custom_call" | custom-call | flops 3000000000 | bytes 4000000 | tf_op jit(solution)/shard_map/pallas_call | solution.py:507
  54.6 3.0 %all-to-all-done.arrived_ref = bf16[16,80,128]{2,1,0:T(8,128)(2,1)S(1)} async-done(((bf16[16,80,128]{2,1,0:T(8,128)(2,1)}), bf16[16,80,128]{2,1,0:T(8,128)(2,1)S(1)}, u32[]{:S(2)}, u32[]{:S(2)}) %all-to-all-start) | async-done | bytes 327712 | tf_op jit(solution)/shard_map/all_to_all | solution.py:505
  57.6 0.8 %shard_map.199 = (f32[1,4968]{1,0:T(1,128)}, f32[1,4968]{1,0:T(1,128)}) custom-call(bf16[16,80,128]{2,1,0:T(8,128)(2,1)S(1)} %all-to-all-done.arrived_ref), custom_call_target="tpu_custom_call" | custom-call | flops 1000000 | bytes 4000000 | tf_op jit(solution)/shard_map/pallas_call | solution.py:510
Async XLA Ops:
  0.6 18.1 %copy-start = (f32[1,79488]{1,0:T(1,128)S(1)}, f32[1,79488]{1,0:T(1,128)}, u32[]{:S(2)}) copy-start(f32[1,79488]{1,0:T(1,128)} %flat_hbm.2) | copy-start | bytes 953860
  0.6 18.1 %copy-start.1 = (bf16[276,384]{1,0:T(8,128)(2,1)S(1)}, bf16[276,384]{1,0:T(8,128)(2,1)}, u32[]{:S(2)}) copy-start(bf16[276,384]{1,0:T(8,128)(2,1)} %constant.30.clone.perm_hbm.perm_ref) | copy-start | bytes 635908
  8.0 14.5 %copy-start.3 = (bf16[192,576]{1,0:T(8,128)(2,1)S(1)}, bf16[192,576]{1,0:T(8,128)(2,1)}, u32[]{:S(2)}) copy-start(bf16[192,576]{1,0:T(8,128)(2,1)} %w_qkv_ref.2) | copy-start | bytes 663556
  8.0 14.5 %copy-start.5 = (bf16[192,192]{1,0:T(8,128)(2,1)S(1)}, bf16[192,192]{1,0:T(8,128)(2,1)}, u32[]{:S(2)}) copy-start(bf16[192,192]{1,0:T(8,128)(2,1)} %w_proj_ref.3) | copy-start | bytes 221188
  8.1 14.5 %copy-start.7 = (f32[192]{0:T(256)S(1)}, f32[192]{0:T(256)}, u32[]{:S(2)}) copy-start(f32[192]{0:T(256)} %param.24) | copy-start | bytes 2308
  8.1 14.5 %copy-start.9 = (bf16[864,144]{1,0:T(8,128)(2,1)S(1)}, bf16[864,144]{1,0:T(8,128)(2,1)}, u32[]{:S(2)}) copy-start(bf16[864,144]{1,0:T(8,128)(2,1)} %constant.27.clone.rep_ref) | copy-start | bytes 746500
  8.1 14.5 %copy-start.10 = (bf16[192,864]{1,0:T(8,128)(2,1)S(1)}, bf16[192,864]{1,0:T(8,128)(2,1)}, u32[]{:S(2)}) copy-start(bf16[192,864]{1,0:T(8,128)(2,1)} %constant.29.clone.mask_t_ref) | copy-start | bytes 995332
  8.1 14.5 %copy-start.11 = (bf16[288,144]{1,0:T(8,128)(2,1)S(1)}, bf16[288,144]{1,0:T(8,128)(2,1)}, u32[]{:S(2)}) copy-start(bf16[288,144]{1,0:T(8,128)(2,1)} %constant.28.clone.twice_hbm.twice_ref) | copy-start | bytes 248836
  8.1 14.5 %copy-start.13 = (bf16[144,144]{1,0:T(8,128)(2,1)S(1)}, bf16[144,144]{1,0:T(8,128)(2,1)}, u32[]{:S(2)}) copy-start(bf16[144,144]{1,0:T(8,128)(2,1)} %constant.34.clone.join_t_ref) | copy-start | bytes 124420
  8.1 14.5 %copy-start.14 = (bf16[144,144]{1,0:T(8,128)(2,1)S(1)}, bf16[144,144]{1,0:T(8,128)(2,1)}, u32[]{:S(2)}) copy-start(bf16[144,144]{1,0:T(8,128)(2,1)} %constant.33.clone.join_ref) | copy-start | bytes 124420
  8.1 14.5 %copy-start.18 = (bf16[144,384]{1,0:T(8,128)(2,1)S(1)}, bf16[144,384]{1,0:T(8,128)(2,1)}, u32[]{:S(2)}) copy-start(bf16[144,384]{1,0:T(8,128)(2,1)} %get-tuple-element.28.stay_ref) | copy-start | bytes 331780
  8.1 13.1 %collective-permute-start = (bf16[144,384]{1,0:T(8,128)(2,1)}, bf16[144,384]{1,0:T(8,128)(2,1)S(1)}, u32[]{:S(2)}, u32[]{:S(2)}) collective-permute-start(bf16[144,384]{1,0:T(8,128)(2,1)} %get-tuple-element.29), channel_id=1, source_target_pairs={{0,15},{1,0},{2,1},{3,2},{4,3},{5,4},{6,5},{7,6},{8,7},{9,8},{10,9... | collective-permute-start | bytes 331784 | tf_op jit(solution)/shard_map/ppermute | solution.py:421
  10.5 10.8 %collective-permute-start.1 = (bf16[144,384]{1,0:T(8,128)(2,1)}, bf16[144,384]{1,0:T(8,128)(2,1)S(1)}, u32[]{:S(2)}, u32[]{:S(2)}) collective-permute-start(bf16[144,384]{1,0:T(8,128)(2,1)} %get-tuple-element.30), channel_id=1, source_target_pairs={{0,240},{16,0},{32,16},{48,32},{64,48},{80,64},{96,80},{112,96},{1... | collective-permute-start | bytes 331784 | tf_op jit(solution)/shard_map/ppermute | solution.py:422
  12.8 9.8 %collective-permute-start.2 = (bf16[144,384]{1,0:T(8,128)(2,1)}, bf16[144,384]{1,0:T(8,128)(2,1)S(1)}, u32[]{:S(2)}, u32[]{:S(2)}) collective-permute-start(bf16[144,384]{1,0:T(8,128)(2,1)} %get-tuple-element.31), channel_id=1, source_target_pairs={{0,255},{1,240},{2,241},{3,242},{4,243},{5,244},{6,245},{7,246},{8... | collective-permute-start | bytes 331784 | tf_op jit(solution)/shard_map/ppermute | solution.py:423
  22.6 13.3 %copy-start.6 = (bf16[192,192]{1,0:T(8,128)(2,1)S(1)}, bf16[192,192]{1,0:T(8,128)(2,1)}, u32[]{:S(2)}) copy-start(bf16[192,192]{1,0:T(8,128)(2,1)} %w_proj_ref.5) | copy-start | bytes 221188
  22.6 13.3 %copy-start.12 = (bf16[144,144]{1,0:T(8,128)(2,1)S(1)}, bf16[144,144]{1,0:T(8,128)(2,1)}, u32[]{:S(2)}) copy-start(bf16[144,144]{1,0:T(8,128)(2,1)} %constant.31.clone.split_ref) | copy-start | bytes 124420
  22.6 13.3 %copy-start.15 = (bf16[4,144,864]{2,1,0:T(8,128)(2,1)S(1)}, bf16[4,144,864]{2,1,0:T(8,128)(2,1)}, u32[]{:S(2)}) copy-start(bf16[4,144,864]{2,1,0:T(8,128)(2,1)} %get-tuple-element.23.probs_ref) | copy-start | bytes 2985988
  22.7 13.3 %copy-start.17 = (bf16[4,144,192]{2,1,0:T(8,128)(2,1)S(1)}, bf16[4,144,192]{2,1,0:T(8,128)(2,1)}, u32[]{:S(2)}) copy-start(bf16[4,144,192]{2,1,0:T(8,128)(2,1)} %get-tuple-element.37.v_ref) | copy-start | bytes 663556
  28.1 4.4 %collective-permute-start.3 = (bf16[72,384]{1,0:T(8,128)(2,1)S(1)}, bf16[72,384]{1,0:T(8,128)(2,1)S(1)}, u32[]{:S(2)}, u32[]{:S(2)}) collective-permute-start(bf16[72,384]{1,0:T(8,128)(2,1)S(1)} %get-tuple-element.34), channel_id=1, source_target_pairs={{0,1},{1,2},{2,3},{3,4},{4,5},{5,6},{6,7},{7,8},{8,9},{9,10},{10,1... | collective-permute-start | bytes 165896 | tf_op jit(solution)/shard_map/ppermute | solution.py:421
  28.2 7.5 %collective-permute-start.4 = (bf16[72,384]{1,0:T(8,128)(2,1)S(1)}, bf16[72,384]{1,0:T(8,128)(2,1)S(1)}, u32[]{:S(2)}, u32[]{:S(2)}) collective-permute-start(bf16[72,384]{1,0:T(8,128)(2,1)S(1)} %get-tuple-element.35), channel_id=1, source_target_pairs={{0,16},{16,32},{32,48},{48,64},{64,80},{80,96},{96,112},{112,128},... | collective-permute-start | bytes 165896 | tf_op jit(solution)/shard_map/ppermute | solution.py:422
  28.3 7.7 %collective-permute-start.5 = (bf16[72,384]{1,0:T(8,128)(2,1)S(1)}, bf16[72,384]{1,0:T(8,128)(2,1)S(1)}, u32[]{:S(2)}, u32[]{:S(2)}) collective-permute-start(bf16[72,384]{1,0:T(8,128)(2,1)S(1)} %get-tuple-element.36), channel_id=1, source_target_pairs={{0,17},{1,18},{2,19},{3,20},{4,21},{5,22},{6,23},{7,24},{8,25},{9,... | collective-permute-start | bytes 165896 | tf_op jit(solution)/shard_map/ppermute | solution.py:423
  36.0 11.8 %copy-start.2 = (bf16[8,6,12,192]{3,0,2,1:T(8,128)(2,1)S(1)}, bf16[8,6,12,192]{3,0,2,1:T(8,128)(2,1)}, u32[]{:S(2)}) copy-start(bf16[8,6,12,192]{3,0,2,1:T(8,128)(2,1)} %param.18) | copy-start | bytes 663556
  36.0 11.7 %copy-start.4 = (bf16[192,576]{1,0:T(8,128)(2,1)S(1)}, bf16[192,576]{1,0:T(8,128)(2,1)}, u32[]{:S(2)}) copy-start(bf16[192,576]{1,0:T(8,128)(2,1)} %w_qkv_ref.3) | copy-start | bytes 663556
  36.0 11.7 %copy-start.8 = (f32[192]{0:T(256)S(1)}, f32[192]{0:T(256)}, u32[]{:S(2)}) copy-start(f32[192]{0:T(256)} %param.20) | copy-start | bytes 2308
  39.4 18.2 %all-to-all-start = ((bf16[16,80,128]{2,1,0:T(8,128)(2,1)}), bf16[16,80,128]{2,1,0:T(8,128)(2,1)S(1)}, u32[]{:S(2)}, u32[]{:S(2)}) async-start(bf16[16,80,128]{2,1,0:T(8,128)(2,1)} %get-tuple-element.40), calls=%async_computation | async-start | bytes 655360 | tf_op jit(solution)/shard_map/all_to_all | solution.py:505
  47.8 1.2 %copy-start.16 = (bf16[4,144,864]{2,1,0:T(8,128)(2,1)S(1)}, bf16[4,144,864]{2,1,0:T(8,128)(2,1)}, u32[]{:S(2)}) copy-start(bf16[4,144,864]{2,1,0:T(8,128)(2,1)} %get-tuple-element.23.probs_ref) | copy-start | bytes 2985988

commit v7 on v6

--- a/solution.py
+++ b/solution.py
@@ -257,18 +257,19 @@
     _, _, q_rows, k_rows, v_rows = project(inputs, gain_ref[...], w_qkv_ref[...])
     q_spread = spread_heads(q_rows, twice_ref[...])
     write_bias(spread_ref, bias_ref)
+    split_t = split_t_ref[...]
+    for v, grad in enumerate(load_windows(grad_ref, picked)):
+        piece_ref[:, v * PIECE : (v + 1) * PIECE, D:] = dot(split_t, grad.astype(BF16)).reshape(4, PIECE, D)
     _, probs_low = attend(q_spread, k_rows, [bias_ref.at[v] for v in LEVELS])
     for v in LEVELS:
         v_ref[v] = v_rows[v]
         probs_ref[v] = probs_low[v]
-    grads = [x.astype(BF16) for x in load_windows(grad_ref, picked)]
     keep = Fetch([(v_ref, v_hbm), (probs_ref, probs_hbm)], keep_sem)
     attended = gathered(v_rows, probs_low, rep_ref[...], mask_t_ref[...])
     split_t = split_t_ref[...]
     for v in LEVELS:
         block_out = (inputs[v] + dot(attended[v], w_proj_ref[...])).astype(BF16)
         piece_ref[:, v * PIECE : (v + 1) * PIECE, :D] = dot(split_t, block_out).reshape(4, PIECE, D)
-        piece_ref[:, v * PIECE : (v + 1) * PIECE, D:] = dot(split_t, grads[v]).reshape(4, PIECE, D)
     out_ref[...] = piece_ref[...].astype(BF16)
     pairs = [(out_ref.at[k], ref) for k, ref in enumerate((stay_hbm, lon_hbm, lat_hbm, both_hbm))]
     sent = Fetch(pairs, out_sem)
@@ -308,9 +309,10 @@
     q_spread = spread_heads(q_rows, twice)
     attn_probs, probs_low = attend(q_spread, k_rows, [bias_ref.at[v] for v in LEVELS])
     _, mixed_spread, lows = score_grads(v_rows, attn_probs, grads, w_proj, twice)
-    results = input_grads(
-        normed, inv_std, q_spread, k_rows, probs_low, mixed_spread, lows, grads, gain, w_qkv_ref, rep_ref[...], mask_t_ref[...]
-    )
+    results = []
+    for part in (slice(0, 2), slice(2, 4)):
+        rows = [x[part] for x in (normed, inv_std, q_spread, k_rows, probs_low, mixed_spread, lows, grads)]
+        results += input_grads(*rows, gain, w_qkv_ref, rep_ref[...], mask_t_ref[...])
     for v in LEVELS:
         low_ref[v] = lows[v]
         row, lane = v % 2 * PIECE, v // 2 * D

time: 59.3 us -> 58.2 us (0.981)
  Pallas kernels: 26.3 us -> 25.3 us
where the time goes in v7:
time: 58.2 us; the launch traced here: 57.3 us
  Pallas kernels  25.3 us (43%)
  starting transfers between devices  19.4 us (33%)
  waiting for transfers between devices  10.4 us (18%)
  local copies, waits for them, and re-layouts  1.32 us (2%)
  between operations  0.93 us (2%)
    all_to_all x1, starting transfers between devices, body(): arrived = lax.all_to_all(terms, 'lon', 0, 0, tiled=True)  8.3 us
    pallas_call x1, Pallas kernels, body(): pl.pallas_call(first_kernel, in_specs=[HBM] * len(operands), out_specs=[H...  6.8 us
    ppermute x2, starting transfers between devices, exchange(): lax.ppermute(both, ('lat', 'lon'), shifted(('lat', 'lon'), by))  6.29 us
    pallas_call x1, Pallas kernels, body(): grid_out, = call(last_kernel, [(columns, BF16)], [], 3000000000)(*operands)  5.58 us
    pallas_call x1, Pallas kernels, body(): call(second_kernel, [single] * 4 + [(scores, BF16)], [(LEV_WIN, WIN_TOK,...  4.98 us
    pallas_call x1, Pallas kernels, body(): call(third_kernel, [((tiles, 2 * TERM, FLAT), BF16), (rows, BF16)], [rows...  3.39 us
    ppermute x2, waiting for transfers between devices, exchange(): lax.ppermute(lat, ('lat',), shifted(('lat',), by))  3.16 us
    all_to_all x1, waiting for transfers between devices, body(): arrived = lax.all_to_all(terms, 'lon', 0, 0, tiled=True)  2.98 us
  transfers between devices with their start and end apart: 7, of which 5 were waited for; matrix products, arithmetic and copies ran while one was open for 0% of the time, Pallas kernels for 16%

profile of v7, /device:TPU:2, one launch (start us, length us, event | category | flops | bytes accessed | tf_op | source)
XLA Modules:
  0.0 57.3 jit_solution(5911705210801739548)
XLA Ops:
  0.6 0.0 copy-start
  0.6 0.0 copy-start.1
  0.7 6.8 %shard_map.193 = (bf16[144,384]{1,0:T(8,128)(2,1)}, bf16[144,384]{1,0:T(8,128)(2,1)}, bf16[144,384]{1,0:T(8,128)(2,1)}, bf16[144,384]{1,0:T(8,128)(2,1)}, bf16[4...) custom-call(bf16[72,8,192]{2,1,0:T(8,128)(2,1)} %bitcast.12, bf16[72,8,192]{2,1,0:T(8,128)(2,1)} %bitcast.17, ...), custom_call_target="tpu_custom_call" | custom-call | flops 2000000000 | bytes 4000000 | tf_op jit(solution)/shard_map/pallas_call | solution.py:458
  7.5 0.0 copy-start.3
  7.5 0.0 copy-start.5
  7.5 0.0 copy-start.7
  7.5 0.0 copy-start.9
  7.5 0.0 copy-start.10
  7.5 0.0 copy-start.11
  7.5 0.0 copy-start.13
  7.5 0.0 copy-start.14
  7.6 0.0 copy-start.18
  7.6 2.3 %collective-permute-start = (bf16[144,384]{1,0:T(8,128)(2,1)}, bf16[144,384]{1,0:T(8,128)(2,1)S(1)}, u32[]{:S(2)}, u32[]{:S(2)}) collective-permute-start(bf16[144,384]{1,0:T(8,128)(2,1)} %get-tuple-element.29), channel_id=1, source_target_pairs={{0,15},{1,0},{2,1},{3,2},{4,3},{5,4},{6,5},{7,6},{8,7},{9,8},{10,9... | collective-permute-start | bytes 331784 | tf_op jit(solution)/shard_map/ppermute | solution.py:423
  9.9 2.3 %collective-permute-start.1 = (bf16[144,384]{1,0:T(8,128)(2,1)}, bf16[144,384]{1,0:T(8,128)(2,1)S(1)}, u32[]{:S(2)}, u32[]{:S(2)}) collective-permute-start(bf16[144,384]{1,0:T(8,128)(2,1)} %get-tuple-element.30), channel_id=1, source_target_pairs={{0,240},{16,0},{32,16},{48,32},{64,48},{80,64},{96,80},{112,96},{1... | collective-permute-start | bytes 331784 | tf_op jit(solution)/shard_map/ppermute | solution.py:424
  12.2 6.0 %collective-permute-start.2 = (bf16[144,384]{1,0:T(8,128)(2,1)}, bf16[144,384]{1,0:T(8,128)(2,1)S(1)}, u32[]{:S(2)}, u32[]{:S(2)}) collective-permute-start(bf16[144,384]{1,0:T(8,128)(2,1)} %get-tuple-element.31), channel_id=1, source_target_pairs={{0,255},{1,240},{2,241},{3,242},{4,243},{5,244},{6,245},{7,246},{8... | collective-permute-start | bytes 331784 | tf_op jit(solution)/shard_map/ppermute | solution.py:425
  18.2 0.0 copy-done
  18.2 0.0 copy-done.1
  18.2 2.5 %shard_map.194.bias_ref = f32[4,144,864]{2,1,0:T(8,128)S(1)} custom-call(f32[1,1]{1,0:T(1,128)} %bitcast.6.active_ref, f32[1,79488]{1,0:T(1,128)S(1)} %copy-done, bf16[276,384]{1,0:T(8,128)(2,1)S(1)} %copy-done.1), custom_call_target="tpu_custom_call" | custom-call | flops 500000000 | bytes 4000000 | tf_op jit(solution)/shard_map/pallas_call | solution.py:478
  20.7 0.0 collective-permute-done.lon_ref
  20.7 0.0 collective-permute-done.1.lat_ref
  20.7 1.3 %collective-permute-done.2.both_ref = bf16[144,384]{1,0:T(8,128)(2,1)S(1)} collective-permute-done((bf16[144,384]{1,0:T(8,128)(2,1)}, bf16[144,384]{1,0:T(8,128)(2,1)S(1)}, u32[]{:S(2)}, u32[]{:S(2)}) %collective-permute-start.2) | collective-permute-done | bytes 110624 | tf_op jit(solution)/shard_map/ppermute | solution.py:425
  22.0 0.0 copy-done.3
  22.0 0.0 copy-done.5
  22.0 0.0 copy-done.7
  22.0 0.0 copy-done.9
  22.0 0.0 copy-done.10
  22.0 0.0 copy-done.11
  22.0 0.0 copy-done.13
  22.0 0.0 copy-done.14
  22.0 0.0 copy-done.18
  22.1 0.0 copy-start.6
  22.1 0.0 copy-start.12
  22.1 0.0 copy-start.15
  22.1 0.0 copy-start.17
  22.1 5.0 %shard_map.195 = (bf16[72,384]{1,0:T(8,128)(2,1)S(1)}, bf16[72,384]{1,0:T(8,128)(2,1)S(1)}, bf16[72,384]{1,0:T(8,128)(2,1)S(1)}, bf16[72,384]{1,0:T(8,128)(2,1)S(1)}, bf16[4,144,864]{2,1,0:T(8,128)(2,1)S(1)}) custom-call(bf16[144,384]{1,0:T(8,128)(2,1)S(1)} %copy-done.18, bf16[144,384]{1,0:T(8,128)(2,1)S(1)} %collective-permute-done.lon_ref, ...), custom_call_target="tpu_custom_call" | custom-call | flops 4000000000 | bytes 4000000 | tf_op jit(solution)/shard_map/pallas_call | solution.py:487
  27.1 0.1 collective-permute-start.3
  27.2 0.1 collective-permute-start.4
  27.3 0.3 collective-permute-start.5
  27.6 1.2 %shard_map.196.other_ref = f32[16,40,128]{2,1,0:T(8,128)S(1)} custom-call(bf16[4,144,864]{2,1,0:T(8,128)(2,1)S(1)} %get-tuple-element.38.low_ref, bf16[276,384]{1,0:T(8,128)(2,1)S(1)} %copy-done.1), custom_call_target="tpu_custom_call" | custom-call | flops 500000000 | bytes 4000000 | tf_op jit(solution)/shard_map/pallas_call | solution.py:496
  28.8 2.7 %collective-permute-done.3.lon_ref = bf16[72,384]{1,0:T(8,128)(2,1)S(1)} collective-permute-done((bf16[72,384]{1,0:T(8,128)(2,1)S(1)}, bf16[72,384]{1,0:T(8,128)(2,1)S(1)}, u32[]{:S(2)}, u32[]{:S(2)}) %collective-permute-start.3) | collective-permute-done | bytes 55328 | tf_op jit(solution)/shard_map/ppermute | solution.py:423
  31.5 3.2 %collective-permute-done.4.lat_ref = bf16[72,384]{1,0:T(8,128)(2,1)S(1)} collective-permute-done((bf16[72,384]{1,0:T(8,128)(2,1)S(1)}, bf16[72,384]{1,0:T(8,128)(2,1)S(1)}, u32[]{:S(2)}, u32[]{:S(2)}) %collective-permute-start.4) | collective-permute-done | bytes 55328 | tf_op jit(solution)/shard_map/ppermute | solution.py:424
  34.6 0.3 collective-permute-done.5.both_ref
  34.9 0.0 copy-done.6
  34.9 0.0 copy-done.12
  34.9 0.0 copy-done.15
  34.9 0.0 copy-done.17
  34.9 0.0 copy-start.2
  35.0 0.0 copy-start.4
  35.0 0.0 copy-start.8
  35.0 3.4 %shard_map.197 = (bf16[16,80,128]{2,1,0:T(8,128)(2,1)}, bf16[4,144,192]{2,1,0:T(8,128)(2,1)S(1)}) custom-call(bf16[72,384]{1,0:T(8,128)(2,1)S(1)} %get-tuple-element.33.stay_ref, bf16[72,384]{1,0:T(8,128)(2,1)S(1)} %collective-permute-done.3.lon_ref, bf16[72,384]{1,0:T(8,128)(2,1)S(1)} %collective-permute-done.4.lat_ref, ...), custom_call_target="tpu_custom_call" | custom-call | flops 2000000000 | bytes 4000000 | tf_op jit(solution)/shard_map/pallas_call | solution.py:500
  38.4 8.3 %all-to-all-start = ((bf16[16,80,128]{2,1,0:T(8,128)(2,1)}), bf16[16,80,128]{2,1,0:T(8,128)(2,1)S(1)}, u32[]{:S(2)}, u32[]{:S(2)}) async-start(bf16[16,80,128]{2,1,0:T(8,128)(2,1)} %get-tuple-element.40), calls=%async_computation | async-start | bytes 655360 | tf_op jit(solution)/shard_map/all_to_all | solution.py:507
  46.7 0.0 copy-done.2
  46.7 0.0 copy-done.4
  46.7 0.0 copy-done.8
  46.7 0.0 copy-start.16
  46.7 1.2 %copy-done.16 = bf16[4,144,864]{2,1,0:T(8,128)(2,1)S(1)} copy-done((bf16[4,144,864]{2,1,0:T(8,128)(2,1)S(1)}, bf16[4,144,864]{2,1,0:T(8,128)(2,1)}, u32[]{:S(2)}) %copy-start.16) | copy-done | bytes 995352
  47.9 5.6 %shard_map.198 = bf16[72,8,192]{2,1,0:T(8,128)(2,1)} custom-call(bf16[72,8,192]{2,1,0:T(8,128)(2,1)S(1)} %bitcast.13, bf16[4,144,864]{2,1,0:T(8,128)(2,1)S(1)} %copy-done.16, bf16[4,144,192]{2,1,0:T(8,128)(2,1)S(1)} %get-tuple-element.39.grad_ref, f32[1,192]{1,0:T(1,128)S(1)} %bitcast.16, bf16[192,576]{1,0:T(8,128)(2,1)S(1)} %copy-done.4, ...), custom_call_target="tpu_custom_call" | custom-call | flops 3000000000 | bytes 4000000 | tf_op jit(solution)/shard_map/pallas_call | solution.py:509
  53.5 3.0 %all-to-all-done.arrived_ref = bf16[16,80,128]{2,1,0:T(8,128)(2,1)S(1)} async-done(((bf16[16,80,128]{2,1,0:T(8,128)(2,1)}), bf16[16,80,128]{2,1,0:T(8,128)(2,1)S(1)}, u32[]{:S(2)}, u32[]{:S(2)}) %all-to-all-start) | async-done | bytes 327712 | tf_op jit(solution)/shard_map/all_to_all | solution.py:507
  56.5 0.8 %shard_map.199 = (f32[1,4968]{1,0:T(1,128)}, f32[1,4968]{1,0:T(1,128)}) custom-call(bf16[16,80,128]{2,1,0:T(8,128)(2,1)S(1)} %all-to-all-done.arrived_ref), custom_call_target="tpu_custom_call" | custom-call | flops 1000000 | bytes 4000000 | tf_op jit(solution)/shard_map/pallas_call | solution.py:512
Async XLA Ops:
  0.6 17.6 %copy-start = (f32[1,79488]{1,0:T(1,128)S(1)}, f32[1,79488]{1,0:T(1,128)}, u32[]{:S(2)}) copy-start(f32[1,79488]{1,0:T(1,128)} %flat_hbm.2) | copy-start | bytes 953860
  0.6 17.6 %copy-start.1 = (bf16[276,384]{1,0:T(8,128)(2,1)S(1)}, bf16[276,384]{1,0:T(8,128)(2,1)}, u32[]{:S(2)}) copy-start(bf16[276,384]{1,0:T(8,128)(2,1)} %constant.30.clone.perm_hbm.perm_ref) | copy-start | bytes 635908
  7.5 14.5 %copy-start.3 = (bf16[192,576]{1,0:T(8,128)(2,1)S(1)}, bf16[192,576]{1,0:T(8,128)(2,1)}, u32[]{:S(2)}) copy-start(bf16[192,576]{1,0:T(8,128)(2,1)} %w_qkv_ref.2) | copy-start | bytes 663556
  7.5 14.5 %copy-start.5 = (bf16[192,192]{1,0:T(8,128)(2,1)S(1)}, bf16[192,192]{1,0:T(8,128)(2,1)}, u32[]{:S(2)}) copy-start(bf16[192,192]{1,0:T(8,128)(2,1)} %w_proj_ref.3) | copy-start | bytes 221188
  7.5 14.5 %copy-start.7 = (f32[192]{0:T(256)S(1)}, f32[192]{0:T(256)}, u32[]{:S(2)}) copy-start(f32[192]{0:T(256)} %param.24) | copy-start | bytes 2308
  7.5 14.5 %copy-start.9 = (bf16[864,144]{1,0:T(8,128)(2,1)S(1)}, bf16[864,144]{1,0:T(8,128)(2,1)}, u32[]{:S(2)}) copy-start(bf16[864,144]{1,0:T(8,128)(2,1)} %constant.27.clone.rep_ref) | copy-start | bytes 746500
  7.5 14.5 %copy-start.10 = (bf16[192,864]{1,0:T(8,128)(2,1)S(1)}, bf16[192,864]{1,0:T(8,128)(2,1)}, u32[]{:S(2)}) copy-start(bf16[192,864]{1,0:T(8,128)(2,1)} %constant.29.clone.mask_t_ref) | copy-start | bytes 995332
  7.5 14.5 %copy-start.11 = (bf16[288,144]{1,0:T(8,128)(2,1)S(1)}, bf16[288,144]{1,0:T(8,128)(2,1)}, u32[]{:S(2)}) copy-start(bf16[288,144]{1,0:T(8,128)(2,1)} %constant.28.clone.twice_hbm.twice_ref) | copy-start | bytes 248836
  7.5 14.5 %copy-start.13 = (bf16[144,144]{1,0:T(8,128)(2,1)S(1)}, bf16[144,144]{1,0:T(8,128)(2,1)}, u32[]{:S(2)}) copy-start(bf16[144,144]{1,0:T(8,128)(2,1)} %constant.34.clone.join_t_ref) | copy-start | bytes 124420
  7.5 14.5 %copy-start.14 = (bf16[144,144]{1,0:T(8,128)(2,1)S(1)}, bf16[144,144]{1,0:T(8,128)(2,1)}, u32[]{:S(2)}) copy-start(bf16[144,144]{1,0:T(8,128)(2,1)} %constant.33.clone.join_ref) | copy-start | bytes 124420
  7.6 14.5 %copy-start.18 = (bf16[144,384]{1,0:T(8,128)(2,1)S(1)}, bf16[144,384]{1,0:T(8,128)(2,1)}, u32[]{:S(2)}) copy-start(bf16[144,384]{1,0:T(8,128)(2,1)} %get-tuple-element.28.stay_ref) | copy-start | bytes 331780
  7.6 13.1 %collective-permute-start = (bf16[144,384]{1,0:T(8,128)(2,1)}, bf16[144,384]{1,0:T(8,128)(2,1)S(1)}, u32[]{:S(2)}, u32[]{:S(2)}) collective-permute-start(bf16[144,384]{1,0:T(8,128)(2,1)} %get-tuple-element.29), channel_id=1, source_target_pairs={{0,15},{1,0},{2,1},{3,2},{4,3},{5,4},{6,5},{7,6},{8,7},{9,8},{10,9... | collective-permute-start | bytes 331784 | tf_op jit(solution)/shard_map/ppermute | solution.py:423
  9.9 10.8 %collective-permute-start.1 = (bf16[144,384]{1,0:T(8,128)(2,1)}, bf16[144,384]{1,0:T(8,128)(2,1)S(1)}, u32[]{:S(2)}, u32[]{:S(2)}) collective-permute-start(bf16[144,384]{1,0:T(8,128)(2,1)} %get-tuple-element.30), channel_id=1, source_target_pairs={{0,240},{16,0},{32,16},{48,32},{64,48},{80,64},{96,80},{112,96},{1... | collective-permute-start | bytes 331784 | tf_op jit(solution)/shard_map/ppermute | solution.py:424
  12.2 9.8 %collective-permute-start.2 = (bf16[144,384]{1,0:T(8,128)(2,1)}, bf16[144,384]{1,0:T(8,128)(2,1)S(1)}, u32[]{:S(2)}, u32[]{:S(2)}) collective-permute-start(bf16[144,384]{1,0:T(8,128)(2,1)} %get-tuple-element.31), channel_id=1, source_target_pairs={{0,255},{1,240},{2,241},{3,242},{4,243},{5,244},{6,245},{7,246},{8... | collective-permute-start | bytes 331784 | tf_op jit(solution)/shard_map/ppermute | solution.py:425
  22.1 12.9 %copy-start.6 = (bf16[192,192]{1,0:T(8,128)(2,1)S(1)}, bf16[192,192]{1,0:T(8,128)(2,1)}, u32[]{:S(2)}) copy-start(bf16[192,192]{1,0:T(8,128)(2,1)} %w_proj_ref.5) | copy-start | bytes 221188
  22.1 12.9 %copy-start.12 = (bf16[144,144]{1,0:T(8,128)(2,1)S(1)}, bf16[144,144]{1,0:T(8,128)(2,1)}, u32[]{:S(2)}) copy-start(bf16[144,144]{1,0:T(8,128)(2,1)} %constant.31.clone.split_ref) | copy-start | bytes 124420
  22.1 12.9 %copy-start.15 = (bf16[4,144,864]{2,1,0:T(8,128)(2,1)S(1)}, bf16[4,144,864]{2,1,0:T(8,128)(2,1)}, u32[]{:S(2)}) copy-start(bf16[4,144,864]{2,1,0:T(8,128)(2,1)} %get-tuple-element.23.probs_ref) | copy-start | bytes 2985988
  22.1 12.9 %copy-start.17 = (bf16[4,144,192]{2,1,0:T(8,128)(2,1)S(1)}, bf16[4,144,192]{2,1,0:T(8,128)(2,1)}, u32[]{:S(2)}) copy-start(bf16[4,144,192]{2,1,0:T(8,128)(2,1)} %get-tuple-element.37.v_ref) | copy-start | bytes 663556
  27.1 4.4 %collective-permute-start.3 = (bf16[72,384]{1,0:T(8,128)(2,1)S(1)}, bf16[72,384]{1,0:T(8,128)(2,1)S(1)}, u32[]{:S(2)}, u32[]{:S(2)}) collective-permute-start(bf16[72,384]{1,0:T(8,128)(2,1)S(1)} %get-tuple-element.34), channel_id=1, source_target_pairs={{0,1},{1,2},{2,3},{3,4},{4,5},{5,6},{6,7},{7,8},{8,9},{9,10},{10,1... | collective-permute-start | bytes 165896 | tf_op jit(solution)/shard_map/ppermute | solution.py:423
  27.2 7.5 %collective-permute-start.4 = (bf16[72,384]{1,0:T(8,128)(2,1)S(1)}, bf16[72,384]{1,0:T(8,128)(2,1)S(1)}, u32[]{:S(2)}, u32[]{:S(2)}) collective-permute-start(bf16[72,384]{1,0:T(8,128)(2,1)S(1)} %get-tuple-element.35), channel_id=1, source_target_pairs={{0,16},{16,32},{32,48},{48,64},{64,80},{80,96},{96,112},{112,128},... | collective-permute-start | bytes 165896 | tf_op jit(solution)/shard_map/ppermute | solution.py:424
  27.3 7.7 %collective-permute-start.5 = (bf16[72,384]{1,0:T(8,128)(2,1)S(1)}, bf16[72,384]{1,0:T(8,128)(2,1)S(1)}, u32[]{:S(2)}, u32[]{:S(2)}) collective-permute-start(bf16[72,384]{1,0:T(8,128)(2,1)S(1)} %get-tuple-element.36), channel_id=1, source_target_pairs={{0,17},{1,18},{2,19},{3,20},{4,21},{5,22},{6,23},{7,24},{8,25},{9,... | collective-permute-start | bytes 165896 | tf_op jit(solution)/shard_map/ppermute | solution.py:425
  34.9 11.7 %copy-start.2 = (bf16[8,6,12,192]{3,0,2,1:T(8,128)(2,1)S(1)}, bf16[8,6,12,192]{3,0,2,1:T(8,128)(2,1)}, u32[]{:S(2)}) copy-start(bf16[8,6,12,192]{3,0,2,1:T(8,128)(2,1)} %param.18) | copy-start | bytes 663556
  35.0 11.7 %copy-start.4 = (bf16[192,576]{1,0:T(8,128)(2,1)S(1)}, bf16[192,576]{1,0:T(8,128)(2,1)}, u32[]{:S(2)}) copy-start(bf16[192,576]{1,0:T(8,128)(2,1)} %w_qkv_ref.3) | copy-start | bytes 663556
  35.0 11.7 %copy-start.8 = (f32[192]{0:T(256)S(1)}, f32[192]{0:T(256)}, u32[]{:S(2)}) copy-start(f32[192]{0:T(256)} %param.20) | copy-start | bytes 2308
  38.4 18.1 %all-to-all-start = ((bf16[16,80,128]{2,1,0:T(8,128)(2,1)}), bf16[16,80,128]{2,1,0:T(8,128)(2,1)S(1)}, u32[]{:S(2)}, u32[]{:S(2)}) async-start(bf16[16,80,128]{2,1,0:T(8,128)(2,1)} %get-tuple-element.40), calls=%async_computation | async-start | bytes 655360 | tf_op jit(solution)/shard_map/all_to_all | solution.py:507
  46.7 1.2 %copy-start.16 = (bf16[4,144,864]{2,1,0:T(8,128)(2,1)S(1)}, bf16[4,144,864]{2,1,0:T(8,128)(2,1)}, u32[]{:S(2)}) copy-start(bf16[4,144,864]{2,1,0:T(8,128)(2,1)} %get-tuple-element.23.probs_ref) | copy-start | bytes 2985988

commit v8 on v7

--- a/solution.py
+++ b/solution.py
@@ -106,14 +106,14 @@
             bias_ref[v, :, query_lon * SLAB : (query_lon + 1) * SLAB] = block
 
 
-def fold_scores(lows, perm_ref, folded_ref, table_ref, pack_ref):
+def fold_scores(lows, factor, perm_ref, folded_ref, table_ref, pack_ref):
     folded_ref[...] = jnp.zeros_like(folded_ref)
     wide = [low.astype(F32) for low in lows]
     for query_lon in range(WIN_LON):
         first = (WIN_LON - 1 - query_lon) * BAND
         block = jnp.concatenate([low[:, query_lon * SLAB : (query_lon + 1) * SLAB] for low in wide], 1)
         folded_ref[first : first + WIN_TOK, :] += block
-    folded = (folded_ref[...] * (1.0 / SCALE)).astype(BF16)
+    folded = (folded_ref[...] * factor).astype(BF16)
     table_ref[...] = dot(folded, perm_ref[...], TN)
     for tile in range(LEV_WIN * SLAB // SHARE):
         top = tile * SHARE
@@ -201,12 +201,12 @@
     return [dot(x, rep).T.astype(BF16) for x in spread]
 
 
-def score_grads(v_rows, attn_probs, grads, w_proj, twice):
+def score_grads(v_rows, attn_probs, grads, w_proj, twice, scale=SCALE):
     grad_mixed = [dot(x, w_proj, NT).astype(BF16) for x in grads]
     mixed_spread = spread_heads(grad_mixed, twice)
     grad_probs = [dot(v, m, NT) for v, m in zip(v_rows, mixed_spread)]
     lows = [
-        ((p * (x - jnp.sum(x * p, 0, keepdims=True))) * SCALE).astype(BF16) for p, x in zip(attn_probs, grad_probs)
+        (p * (x - jnp.sum(x * p, 0, keepdims=True)) * scale).astype(BF16) for p, x in zip(attn_probs, grad_probs)
     ]
     return grad_mixed, mixed_spread, lows
 
@@ -256,16 +256,16 @@
     expand_table(rows_ref, perm_ref, (part_a, part_b, part_c), spread_ref)
     _, _, q_rows, k_rows, v_rows = project(inputs, gain_ref[...], w_qkv_ref[...])
     q_spread = spread_heads(q_rows, twice_ref[...])
-    write_bias(spread_ref, bias_ref)
     split_t = split_t_ref[...]
     for v, grad in enumerate(load_windows(grad_ref, picked)):
         piece_ref[:, v * PIECE : (v + 1) * PIECE, D:] = dot(split_t, grad.astype(BF16)).reshape(4, PIECE, D)
+    write_bias(spread_ref, bias_ref)
     _, probs_low = attend(q_spread, k_rows, [bias_ref.at[v] for v in LEVELS])
     for v in LEVELS:
         v_ref[v] = v_rows[v]
         probs_ref[v] = probs_low[v]
+    attended = gathered(v_rows, probs_low, rep_ref[...], mask_t_ref[...])
     keep = Fetch([(v_ref, v_hbm), (probs_ref, probs_hbm)], keep_sem)
-    attended = gathered(v_rows, probs_low, rep_ref[...], mask_t_ref[...])
     split_t = split_t_ref[...]
     for v in LEVELS:
         block_out = (inputs[v] + dot(attended[v], w_proj_ref[...])).astype(BF16)
@@ -322,7 +322,7 @@
 
 
 def fold_kernel(low_ref, perm_ref, pack_ref, folded_ref, table_ref):
-    fold_scores([low_ref[v] for v in LEVELS], perm_ref, folded_ref, table_ref, pack_ref)
+    fold_scores([low_ref[v] for v in LEVELS], 1.0 / SCALE, perm_ref, folded_ref, table_ref, pack_ref)
 
 
 def third_kernel(
@@ -338,10 +338,10 @@
             window_ref[v, place * PIECE : (place + 1) * PIECE, :] = wide[row : row + PIECE, lane : lane + D]
     grads = [dot(split, window_ref[v].astype(BF16)).astype(BF16) for v in LEVELS]
     attn_probs = [probs_ref[v].astype(F32) for v in LEVELS]
-    _, _, lows = score_grads([v_ref[v] for v in LEVELS], attn_probs, grads, w_proj_ref[...], twice_ref[...])
+    _, _, lows = score_grads([v_ref[v] for v in LEVELS], attn_probs, grads, w_proj_ref[...], twice_ref[...], 1.0)
     for v in LEVELS:
         grad_ref[v] = grads[v]
-    fold_scores(lows, perm_ref, folded_ref, table_ref, pack_ref)
+    fold_scores(lows, 1.0, perm_ref, folded_ref, table_ref, pack_ref)
     terms_ref[...] = jnp.concatenate([pack_ref[...], other_ref[...]], 1).astype(BF16)
 
 

time: 58.2 us -> 58.1 us (level)
  no operation moved by 1% of the time
where the time goes in v8:
time: 58.1 us; the launch traced here: 57.1 us
  Pallas kernels  25.1 us (43%)
  starting transfers between devices  19.4 us (33%)
  waiting for transfers between devices  10.4 us (18%)
  local copies, waits for them, and re-layouts  1.32 us (2%)
  between operations  0.93 us (2%)
    all_to_all x1, starting transfers between devices, body(): arrived = lax.all_to_all(terms, 'lon', 0, 0, tiled=True)  8.3 us
    pallas_call x1, Pallas kernels, body(): pl.pallas_call(first_kernel, in_specs=[HBM] * len(operands), out_specs=[H...  6.8 us
    ppermute x2, starting transfers between devices, exchange(): lax.ppermute(both, ('lat', 'lon'), shifted(('lat', 'lon'), by))  6.29 us
    pallas_call x1, Pallas kernels, body(): grid_out, = call(last_kernel, [(columns, BF16)], [], 3000000000)(*operands)  5.58 us
    pallas_call x1, Pallas kernels, body(): call(second_kernel, [single] * 4 + [(scores, BF16)], [(LEV_WIN, WIN_TOK,...  4.98 us
    pallas_call x1, Pallas kernels, body(): call(third_kernel, [((tiles, 2 * TERM, FLAT), BF16), (rows, BF16)], [rows...  3.24 us
    ppermute x2, waiting for transfers between devices, exchange(): lax.ppermute(lat, ('lat',), shifted(('lat',), by))  3.16 us
    all_to_all x1, waiting for transfers between devices, body(): arrived = lax.all_to_all(terms, 'lon', 0, 0, tiled=True)  2.98 us
  transfers between devices with their start and end apart: 7, of which 5 were waited for; matrix products, arithmetic and copies ran while one was open for 0% of the time, Pallas kernels for 16%

profile of v8, /device:TPU:2, one launch (start us, length us, event | category | flops | bytes accessed | tf_op | source)
XLA Modules:
  0.0 57.1 jit_solution(1754162026075939828)
XLA Ops:
  0.6 0.0 copy-start
  0.6 0.0 copy-start.1
  0.7 6.8 %shard_map.193 = (bf16[144,384]{1,0:T(8,128)(2,1)}, bf16[144,384]{1,0:T(8,128)(2,1)}, bf16[144,384]{1,0:T(8,128)(2,1)}, bf16[144,384]{1,0:T(8,128)(2,1)}, bf16[4...) custom-call(bf16[72,8,192]{2,1,0:T(8,128)(2,1)} %bitcast.12, bf16[72,8,192]{2,1,0:T(8,128)(2,1)} %bitcast.17, ...), custom_call_target="tpu_custom_call" | custom-call | flops 2000000000 | bytes 4000000 | tf_op jit(solution)/shard_map/pallas_call | solution.py:458
  7.5 0.0 copy-start.3
  7.5 0.0 copy-start.5
  7.5 0.0 copy-start.7
  7.5 0.0 copy-start.9
  7.5 0.0 copy-start.10
  7.5 0.0 copy-start.11
  7.5 0.0 copy-start.13
  7.5 0.0 copy-start.14
  7.6 0.0 copy-start.18
  7.6 2.3 %collective-permute-start = (bf16[144,384]{1,0:T(8,128)(2,1)}, bf16[144,384]{1,0:T(8,128)(2,1)S(1)}, u32[]{:S(2)}, u32[]{:S(2)}) collective-permute-start(bf16[144,384]{1,0:T(8,128)(2,1)} %get-tuple-element.29), channel_id=1, source_target_pairs={{0,15},{1,0},{2,1},{3,2},{4,3},{5,4},{6,5},{7,6},{8,7},{9,8},{10,9... | collective-permute-start | bytes 331784 | tf_op jit(solution)/shard_map/ppermute | solution.py:423
  9.9 2.3 %collective-permute-start.1 = (bf16[144,384]{1,0:T(8,128)(2,1)}, bf16[144,384]{1,0:T(8,128)(2,1)S(1)}, u32[]{:S(2)}, u32[]{:S(2)}) collective-permute-start(bf16[144,384]{1,0:T(8,128)(2,1)} %get-tuple-element.30), channel_id=1, source_target_pairs={{0,240},{16,0},{32,16},{48,32},{64,48},{80,64},{96,80},{112,96},{1... | collective-permute-start | bytes 331784 | tf_op jit(solution)/shard_map/ppermute | solution.py:424
  12.2 6.0 %collective-permute-start.2 = (bf16[144,384]{1,0:T(8,128)(2,1)}, bf16[144,384]{1,0:T(8,128)(2,1)S(1)}, u32[]{:S(2)}, u32[]{:S(2)}) collective-permute-start(bf16[144,384]{1,0:T(8,128)(2,1)} %get-tuple-element.31), channel_id=1, source_target_pairs={{0,255},{1,240},{2,241},{3,242},{4,243},{5,244},{6,245},{7,246},{8... | collective-permute-start | bytes 331784 | tf_op jit(solution)/shard_map/ppermute | solution.py:425
  18.2 0.0 copy-done
  18.2 0.0 copy-done.1
  18.2 2.5 %shard_map.194.bias_ref = f32[4,144,864]{2,1,0:T(8,128)S(1)} custom-call(f32[1,1]{1,0:T(1,128)} %bitcast.6.active_ref, f32[1,79488]{1,0:T(1,128)S(1)} %copy-done, bf16[276,384]{1,0:T(8,128)(2,1)S(1)} %copy-done.1), custom_call_target="tpu_custom_call" | custom-call | flops 500000000 | bytes 4000000 | tf_op jit(solution)/shard_map/pallas_call | solution.py:478
  20.7 0.0 collective-permute-done.lon_ref
  20.7 0.0 collective-permute-done.1.lat_ref
  20.7 1.3 %collective-permute-done.2.both_ref = bf16[144,384]{1,0:T(8,128)(2,1)S(1)} collective-permute-done((bf16[144,384]{1,0:T(8,128)(2,1)}, bf16[144,384]{1,0:T(8,128)(2,1)S(1)}, u32[]{:S(2)}, u32[]{:S(2)}) %collective-permute-start.2) | collective-permute-done | bytes 110624 | tf_op jit(solution)/shard_map/ppermute | solution.py:425
  22.0 0.0 copy-done.3
  22.0 0.0 copy-done.5
  22.0 0.0 copy-done.7
  22.0 0.0 copy-done.9
  22.0 0.0 copy-done.10
  22.0 0.0 copy-done.11
  22.0 0.0 copy-done.13
  22.0 0.0 copy-done.14
  22.0 0.0 copy-done.18
  22.1 0.0 copy-start.6
  22.1 0.0 copy-start.12
  22.1 0.0 copy-start.15
  22.1 0.0 copy-start.17
  22.1 5.0 %shard_map.195 = (bf16[72,384]{1,0:T(8,128)(2,1)S(1)}, bf16[72,384]{1,0:T(8,128)(2,1)S(1)}, bf16[72,384]{1,0:T(8,128)(2,1)S(1)}, bf16[72,384]{1,0:T(8,128)(2,1)S(1)}, bf16[4,144,864]{2,1,0:T(8,128)(2,1)S(1)}) custom-call(bf16[144,384]{1,0:T(8,128)(2,1)S(1)} %copy-done.18, bf16[144,384]{1,0:T(8,128)(2,1)S(1)} %collective-permute-done.lon_ref, ...), custom_call_target="tpu_custom_call" | custom-call | flops 4000000000 | bytes 4000000 | tf_op jit(solution)/shard_map/pallas_call | solution.py:487
  27.1 0.1 collective-permute-start.3
  27.2 0.1 collective-permute-start.4
  27.3 0.3 collective-permute-start.5
  27.6 1.2 %shard_map.196.other_ref = f32[16,40,128]{2,1,0:T(8,128)S(1)} custom-call(bf16[4,144,864]{2,1,0:T(8,128)(2,1)S(1)} %get-tuple-element.38.low_ref, bf16[276,384]{1,0:T(8,128)(2,1)S(1)} %copy-done.1), custom_call_target="tpu_custom_call" | custom-call | flops 500000000 | bytes 4000000 | tf_op jit(solution)/shard_map/pallas_call | solution.py:496
  28.8 2.7 %collective-permute-done.3.lon_ref = bf16[72,384]{1,0:T(8,128)(2,1)S(1)} collective-permute-done((bf16[72,384]{1,0:T(8,128)(2,1)S(1)}, bf16[72,384]{1,0:T(8,128)(2,1)S(1)}, u32[]{:S(2)}, u32[]{:S(2)}) %collective-permute-start.3) | collective-permute-done | bytes 55328 | tf_op jit(solution)/shard_map/ppermute | solution.py:423
  31.5 3.2 %collective-permute-done.4.lat_ref = bf16[72,384]{1,0:T(8,128)(2,1)S(1)} collective-permute-done((bf16[72,384]{1,0:T(8,128)(2,1)S(1)}, bf16[72,384]{1,0:T(8,128)(2,1)S(1)}, u32[]{:S(2)}, u32[]{:S(2)}) %collective-permute-start.4) | collective-permute-done | bytes 55328 | tf_op jit(solution)/shard_map/ppermute | solution.py:424
  34.6 0.3 collective-permute-done.5.both_ref
  34.9 0.0 copy-done.6
  34.9 0.0 copy-done.12
  34.9 0.0 copy-done.15
  34.9 0.0 copy-done.17
  34.9 0.0 copy-start.2
  35.0 0.0 copy-start.4
  35.0 0.0 copy-start.8
  35.0 3.2 %shard_map.197 = (bf16[16,80,128]{2,1,0:T(8,128)(2,1)}, bf16[4,144,192]{2,1,0:T(8,128)(2,1)S(1)}) custom-call(bf16[72,384]{1,0:T(8,128)(2,1)S(1)} %get-tuple-element.33.stay_ref, bf16[72,384]{1,0:T(8,128)(2,1)S(1)} %collective-permute-done.3.lon_ref, bf16[72,384]{1,0:T(8,128)(2,1)S(1)} %collective-permute-done.4.lat_ref, ...), custom_call_target="tpu_custom_call" | custom-call | flops 2000000000 | bytes 4000000 | tf_op jit(solution)/shard_map/pallas_call | solution.py:500
  38.2 8.3 %all-to-all-start = ((bf16[16,80,128]{2,1,0:T(8,128)(2,1)}), bf16[16,80,128]{2,1,0:T(8,128)(2,1)S(1)}, u32[]{:S(2)}, u32[]{:S(2)}) async-start(bf16[16,80,128]{2,1,0:T(8,128)(2,1)} %get-tuple-element.40), calls=%async_computation | async-start | bytes 655360 | tf_op jit(solution)/shard_map/all_to_all | solution.py:507
  46.5 0.0 copy-done.2
  46.5 0.0 copy-done.4
  46.5 0.0 copy-done.8
  46.5 0.0 copy-start.16
  46.6 1.2 %copy-done.16 = bf16[4,144,864]{2,1,0:T(8,128)(2,1)S(1)} copy-done((bf16[4,144,864]{2,1,0:T(8,128)(2,1)S(1)}, bf16[4,144,864]{2,1,0:T(8,128)(2,1)}, u32[]{:S(2)}) %copy-start.16) | copy-done | bytes 995352
  47.8 5.6 %shard_map.198 = bf16[72,8,192]{2,1,0:T(8,128)(2,1)} custom-call(bf16[72,8,192]{2,1,0:T(8,128)(2,1)S(1)} %bitcast.13, bf16[4,144,864]{2,1,0:T(8,128)(2,1)S(1)} %copy-done.16, bf16[4,144,192]{2,1,0:T(8,128)(2,1)S(1)} %get-tuple-element.39.grad_ref, f32[1,192]{1,0:T(1,128)S(1)} %bitcast.16, bf16[192,576]{1,0:T(8,128)(2,1)S(1)} %copy-done.4, ...), custom_call_target="tpu_custom_call" | custom-call | flops 3000000000 | bytes 4000000 | tf_op jit(solution)/shard_map/pallas_call | solution.py:509
  53.3 3.0 %all-to-all-done.arrived_ref = bf16[16,80,128]{2,1,0:T(8,128)(2,1)S(1)} async-done(((bf16[16,80,128]{2,1,0:T(8,128)(2,1)}), bf16[16,80,128]{2,1,0:T(8,128)(2,1)S(1)}, u32[]{:S(2)}, u32[]{:S(2)}) %all-to-all-start) | async-done | bytes 327712 | tf_op jit(solution)/shard_map/all_to_all | solution.py:507
  56.3 0.8 %shard_map.199 = (f32[1,4968]{1,0:T(1,128)}, f32[1,4968]{1,0:T(1,128)}) custom-call(bf16[16,80,128]{2,1,0:T(8,128)(2,1)S(1)} %all-to-all-done.arrived_ref), custom_call_target="tpu_custom_call" | custom-call | flops 1000000 | bytes 4000000 | tf_op jit(solution)/shard_map/pallas_call | solution.py:512
Async XLA Ops:
  0.6 17.6 %copy-start = (f32[1,79488]{1,0:T(1,128)S(1)}, f32[1,79488]{1,0:T(1,128)}, u32[]{:S(2)}) copy-start(f32[1,79488]{1,0:T(1,128)} %flat_hbm.2) | copy-start | bytes 953860
  0.6 17.6 %copy-start.1 = (bf16[276,384]{1,0:T(8,128)(2,1)S(1)}, bf16[276,384]{1,0:T(8,128)(2,1)}, u32[]{:S(2)}) copy-start(bf16[276,384]{1,0:T(8,128)(2,1)} %constant.30.clone.perm_hbm.perm_ref) | copy-start | bytes 635908
  7.5 14.5 %copy-start.3 = (bf16[192,576]{1,0:T(8,128)(2,1)S(1)}, bf16[192,576]{1,0:T(8,128)(2,1)}, u32[]{:S(2)}) copy-start(bf16[192,576]{1,0:T(8,128)(2,1)} %w_qkv_ref.2) | copy-start | bytes 663556
  7.5 14.5 %copy-start.5 = (bf16[192,192]{1,0:T(8,128)(2,1)S(1)}, bf16[192,192]{1,0:T(8,128)(2,1)}, u32[]{:S(2)}) copy-start(bf16[192,192]{1,0:T(8,128)(2,1)} %w_proj_ref.3) | copy-start | bytes 221188
  7.5 14.5 %copy-start.7 = (f32[192]{0:T(256)S(1)}, f32[192]{0:T(256)}, u32[]{:S(2)}) copy-start(f32[192]{0:T(256)} %param.24) | copy-start | bytes 2308
  7.5 14.5 %copy-start.9 = (bf16[864,144]{1,0:T(8,128)(2,1)S(1)}, bf16[864,144]{1,0:T(8,128)(2,1)}, u32[]{:S(2)}) copy-start(bf16[864,144]{1,0:T(8,128)(2,1)} %constant.27.clone.rep_ref) | copy-start | bytes 746500
  7.5 14.5 %copy-start.10 = (bf16[192,864]{1,0:T(8,128)(2,1)S(1)}, bf16[192,864]{1,0:T(8,128)(2,1)}, u32[]{:S(2)}) copy-start(bf16[192,864]{1,0:T(8,128)(2,1)} %constant.29.clone.mask_t_ref) | copy-start | bytes 995332
  7.5 14.5 %copy-start.11 = (bf16[288,144]{1,0:T(8,128)(2,1)S(1)}, bf16[288,144]{1,0:T(8,128)(2,1)}, u32[]{:S(2)}) copy-start(bf16[288,144]{1,0:T(8,128)(2,1)} %constant.28.clone.twice_hbm.twice_ref) | copy-start | bytes 248836
  7.5 14.5 %copy-start.13 = (bf16[144,144]{1,0:T(8,128)(2,1)S(1)}, bf16[144,144]{1,0:T(8,128)(2,1)}, u32[]{:S(2)}) copy-start(bf16[144,144]{1,0:T(8,128)(2,1)} %constant.34.clone.join_t_ref) | copy-start | bytes 124420
  7.5 14.5 %copy-start.14 = (bf16[144,144]{1,0:T(8,128)(2,1)S(1)}, bf16[144,144]{1,0:T(8,128)(2,1)}, u32[]{:S(2)}) copy-start(bf16[144,144]{1,0:T(8,128)(2,1)} %constant.33.clone.join_ref) | copy-start | bytes 124420
  7.6 14.5 %copy-start.18 = (bf16[144,384]{1,0:T(8,128)(2,1)S(1)}, bf16[144,384]{1,0:T(8,128)(2,1)}, u32[]{:S(2)}) copy-start(bf16[144,384]{1,0:T(8,128)(2,1)} %get-tuple-element.28.stay_ref) | copy-start | bytes 331780
  7.6 13.1 %collective-permute-start = (bf16[144,384]{1,0:T(8,128)(2,1)}, bf16[144,384]{1,0:T(8,128)(2,1)S(1)}, u32[]{:S(2)}, u32[]{:S(2)}) collective-permute-start(bf16[144,384]{1,0:T(8,128)(2,1)} %get-tuple-element.29), channel_id=1, source_target_pairs={{0,15},{1,0},{2,1},{3,2},{4,3},{5,4},{6,5},{7,6},{8,7},{9,8},{10,9... | collective-permute-start | bytes 331784 | tf_op jit(solution)/shard_map/ppermute | solution.py:423
  9.9 10.8 %collective-permute-start.1 = (bf16[144,384]{1,0:T(8,128)(2,1)}, bf16[144,384]{1,0:T(8,128)(2,1)S(1)}, u32[]{:S(2)}, u32[]{:S(2)}) collective-permute-start(bf16[144,384]{1,0:T(8,128)(2,1)} %get-tuple-element.30), channel_id=1, source_target_pairs={{0,240},{16,0},{32,16},{48,32},{64,48},{80,64},{96,80},{112,96},{1... | collective-permute-start | bytes 331784 | tf_op jit(solution)/shard_map/ppermute | solution.py:424
  12.2 9.8 %collective-permute-start.2 = (bf16[144,384]{1,0:T(8,128)(2,1)}, bf16[144,384]{1,0:T(8,128)(2,1)S(1)}, u32[]{:S(2)}, u32[]{:S(2)}) collective-permute-start(bf16[144,384]{1,0:T(8,128)(2,1)} %get-tuple-element.31), channel_id=1, source_target_pairs={{0,255},{1,240},{2,241},{3,242},{4,243},{5,244},{6,245},{7,246},{8... | collective-permute-start | bytes 331784 | tf_op jit(solution)/shard_map/ppermute | solution.py:425
  22.1 12.9 %copy-start.6 = (bf16[192,192]{1,0:T(8,128)(2,1)S(1)}, bf16[192,192]{1,0:T(8,128)(2,1)}, u32[]{:S(2)}) copy-start(bf16[192,192]{1,0:T(8,128)(2,1)} %w_proj_ref.5) | copy-start | bytes 221188
  22.1 12.9 %copy-start.12 = (bf16[144,144]{1,0:T(8,128)(2,1)S(1)}, bf16[144,144]{1,0:T(8,128)(2,1)}, u32[]{:S(2)}) copy-start(bf16[144,144]{1,0:T(8,128)(2,1)} %constant.31.clone.split_ref) | copy-start | bytes 124420
  22.1 12.9 %copy-start.15 = (bf16[4,144,864]{2,1,0:T(8,128)(2,1)S(1)}, bf16[4,144,864]{2,1,0:T(8,128)(2,1)}, u32[]{:S(2)}) copy-start(bf16[4,144,864]{2,1,0:T(8,128)(2,1)} %get-tuple-element.23.probs_ref) | copy-start | bytes 2985988
  22.1 12.9 %copy-start.17 = (bf16[4,144,192]{2,1,0:T(8,128)(2,1)S(1)}, bf16[4,144,192]{2,1,0:T(8,128)(2,1)}, u32[]{:S(2)}) copy-start(bf16[4,144,192]{2,1,0:T(8,128)(2,1)} %get-tuple-element.37.v_ref) | copy-start | bytes 663556
  27.1 4.4 %collective-permute-start.3 = (bf16[72,384]{1,0:T(8,128)(2,1)S(1)}, bf16[72,384]{1,0:T(8,128)(2,1)S(1)}, u32[]{:S(2)}, u32[]{:S(2)}) collective-permute-start(bf16[72,384]{1,0:T(8,128)(2,1)S(1)} %get-tuple-element.34), channel_id=1, source_target_pairs={{0,1},{1,2},{2,3},{3,4},{4,5},{5,6},{6,7},{7,8},{8,9},{9,10},{10,1... | collective-permute-start | bytes 165896 | tf_op jit(solution)/shard_map/ppermute | solution.py:423
  27.2 7.5 %collective-permute-start.4 = (bf16[72,384]{1,0:T(8,128)(2,1)S(1)}, bf16[72,384]{1,0:T(8,128)(2,1)S(1)}, u32[]{:S(2)}, u32[]{:S(2)}) collective-permute-start(bf16[72,384]{1,0:T(8,128)(2,1)S(1)} %get-tuple-element.35), channel_id=1, source_target_pairs={{0,16},{16,32},{32,48},{48,64},{64,80},{80,96},{96,112},{112,128},... | collective-permute-start | bytes 165896 | tf_op jit(solution)/shard_map/ppermute | solution.py:424
  27.3 7.7 %collective-permute-start.5 = (bf16[72,384]{1,0:T(8,128)(2,1)S(1)}, bf16[72,384]{1,0:T(8,128)(2,1)S(1)}, u32[]{:S(2)}, u32[]{:S(2)}) collective-permute-start(bf16[72,384]{1,0:T(8,128)(2,1)S(1)} %get-tuple-element.36), channel_id=1, source_target_pairs={{0,17},{1,18},{2,19},{3,20},{4,21},{5,22},{6,23},{7,24},{8,25},{9,... | collective-permute-start | bytes 165896 | tf_op jit(solution)/shard_map/ppermute | solution.py:425
  34.9 11.6 %copy-start.2 = (bf16[8,6,12,192]{3,0,2,1:T(8,128)(2,1)S(1)}, bf16[8,6,12,192]{3,0,2,1:T(8,128)(2,1)}, u32[]{:S(2)}) copy-start(bf16[8,6,12,192]{3,0,2,1:T(8,128)(2,1)} %param.18) | copy-start | bytes 663556
  35.0 11.6 %copy-start.4 = (bf16[192,576]{1,0:T(8,128)(2,1)S(1)}, bf16[192,576]{1,0:T(8,128)(2,1)}, u32[]{:S(2)}) copy-start(bf16[192,576]{1,0:T(8,128)(2,1)} %w_qkv_ref.3) | copy-start | bytes 663556
  35.0 11.6 %copy-start.8 = (f32[192]{0:T(256)S(1)}, f32[192]{0:T(256)}, u32[]{:S(2)}) copy-start(f32[192]{0:T(256)} %param.20) | copy-start | bytes 2308
  38.2 18.1 %all-to-all-start = ((bf16[16,80,128]{2,1,0:T(8,128)(2,1)}), bf16[16,80,128]{2,1,0:T(8,128)(2,1)S(1)}, u32[]{:S(2)}, u32[]{:S(2)}) async-start(bf16[16,80,128]{2,1,0:T(8,128)(2,1)} %get-tuple-element.40), calls=%async_computation | async-start | bytes 655360 | tf_op jit(solution)/shard_map/all_to_all | solution.py:507
  46.5 1.2 %copy-start.16 = (bf16[4,144,864]{2,1,0:T(8,128)(2,1)S(1)}, bf16[4,144,864]{2,1,0:T(8,128)(2,1)}, u32[]{:S(2)}) copy-start(bf16[4,144,864]{2,1,0:T(8,128)(2,1)} %get-tuple-element.23.probs_ref) | copy-start | bytes 2985988
